TPU v7x, 128 devices: a whole 4x4x4 slice. The times are simulated.
128 devices in a mesh: lat: 16 (over y, z_lo, core), mp: 8 (over x, z_hi).
Axes of the slice: x: 4, y: 4, z: 4 (z_hi: 2, z_lo: 2; z = z_hi * 2 + z_lo), core: 2. Of those that a mesh axis runs over, the one named last changes fastest.
Arguments:
- fields: bfloat16 [192, 288, 512], P('lat', None, 'mp'), may hold values from -16 to 16
- first_gain: float32 [512], P('mp'), may hold values from 0.1 to 1.9
- qkv_weight: bfloat16 [512, 3, 512], P(None, None, 'mp'), may hold values from -1 to 1
- proj_weight: bfloat16 [512, 512], P(None, 'mp'), may hold values from -0.25 to 0.25
- merge_gain: float32 [4, 512], P(None, 'mp'), may hold values from 0.1 to 1.9
- merge_weight: bfloat16 [4, 512, 1024], P(None, 'mp'), may hold values from -0.125 to 0.125
- mlp_gain: float32 [1024], replicated, may hold values from 0.1 to 1.9
- up_weight: bfloat16 [1024, 4096], P(None, 'mp'), may hold values from -0.1875 to 0.1875
- down_weight: bfloat16 [1024, 4096], P(None, 'mp'), may hold values from -0.09375 to 0.09375
- expand_weight: bfloat16 [1024, 4, 512], P(None, None, 'mp'), may hold values from -0.1875 to 0.1875
- lat_shift: int32 [1], replicated, may hold values from 1 to 5
- lon_shift: int32 [1], replicated, may hold values from 1 to 11
- cotangent: bfloat16 [192, 288, 512], P('lat', None, 'mp'), may hold values from -6 to 6
Outputs:
- decoded: bfloat16 [192, 288, 512], P('lat', None, 'mp')
- grad_input: float32 [192, 288, 512], P('lat', None, 'mp')
- grad_qkv: float32 [512, 3, 512], P('lat', None, 'mp')
- grad_proj: float32 [512, 512], P('lat', 'mp')
- grad_up: float32 [1024, 4096], P('lat', 'mp')
- grad_down: float32 [1024, 4096], P('lat', 'mp')
All inputs are finite; a program needn't handle non-finite values.
Results may differ from a plain program's by a relative error of at most 0.035.
Values may be sent and summed in bfloat16 or wider, within the bound.
A program may use at most 128 MiB of HBM per device.

v0:
```python
import jax
import jax.numpy as jnp
from jax import lax
from jax.experimental import pallas as pl
from jax.experimental.pallas import tpu as pltpu
from jax.sharding import PartitionSpec as P

WIN_H = 6
WIN_W = 12
HDIM = 64
EPSILON = 1e-05
MASKED = -1e30
BF16 = jnp.bfloat16
F32 = jnp.float32


def positions():
    lat, mp = lax.axis_index("lat"), lax.axis_index("mp")
    return {
        "lat": lat,
        "mp": mp,
        "core": lax.rem(lat, 2),
        "x": lax.div(mp, 2),
        "z": lax.rem(mp, 2),
    }


def reached(here, down, right):
    n_lat, n_mp = lax.axis_size("lat"), lax.axis_size("mp")
    if down == "sibling":
        return {"lat": here["lat"] + 1 - 2 * here["core"], "mp": here["mp"]}
    return {
        "lat": lax.rem(here["lat"] + n_lat + down, n_lat),
        "mp": lax.rem(here["mp"] + n_mp + right, n_mp),
    }


def device_of(target):
    return {
        "device_id": (target["lat"], target["mp"]),
        "device_id_type": pl.DeviceIdType.MESH,
    }


def greet(here, steps):
    barrier = pltpu.get_barrier_semaphore()
    for down, right in steps:
        source = reached(here, down if down == "sibling" else -down, -right)
        pl.semaphore_signal(barrier, inc=1, **device_of(source))
    pl.semaphore_wait(barrier, len(steps))


def remote(source, landing, send, receive, target):
    return pltpu.make_async_remote_copy(
        src_ref=source, dst_ref=landing, send_sem=send, recv_sem=receive, **device_of(target)
    )


def exchange(collective, inputs, outputs, moves):
    steps = []
    for move in moves:
        if move[4:6] != (0, 0) and move[4:6] not in steps:
            steps.append(move[4:6])

    def body(*refs):
        sources = refs[: len(inputs)]
        landings = refs[len(inputs) : len(inputs) + len(outputs)]
        send, receive = refs[-2:]
        here = positions()

        def part_of(ref, part, place, target):
            if part is None:
                return ref
            if isinstance(part, str):
                return ref.at[place[part]]
            if callable(part):
                return part(ref, here, target)
            return ref.at[part]

        greet(here, steps)
        copies = []
        arrived = set()
        for index, move in enumerate(moves):
            source, source_part, landing, landing_part, down, right = move[:6]
            target = reached(here, down, right)
            if len(move) > 6:
                copies[move[6]].wait_recv()
                arrived.add(move[6])
                source_ref = part_of(landings[source], source_part, target, target)
            else:
                source_ref = part_of(sources[source], source_part, target, target)
            landing_ref = part_of(landings[landing], landing_part, here, target)
            if (down, right) == (0, 0):
                copy = pltpu.make_async_copy(source_ref, landing_ref, receive.at[index])
            else:
                copy = remote(
                    source_ref, landing_ref, send.at[index], receive.at[index], target
                )
            copy.start()
            copies.append(copy)
        for index, copy in enumerate(copies):
            if moves[index][4:6] == (0, 0):
                copy.wait()
            else:
                copy.wait_send()
                if index not in arrived:
                    copy.wait_recv()

    return pl.pallas_call(
        body,
        out_shape=[jax.ShapeDtypeStruct(shape, dtype) for shape, dtype in outputs],
        in_specs=[pl.BlockSpec(memory_space=pl.ANY)] * len(inputs),
        out_specs=[pl.BlockSpec(memory_space=pl.ANY)] * len(outputs),
        scratch_shapes=[
            pltpu.SemaphoreType.DMA((len(moves),)),
            pltpu.SemaphoreType.DMA((len(moves),)),
        ],
        compiler_params=pltpu.CompilerParams(collective_id=collective, has_side_effects=True),
    )(*inputs)


X_STEPS = ((4, 2), (2, 1), (-2, 3))


def terms_back(collective, terms):
    count, _, rows, width = terms.shape

    def body(terms_ref, parts_ref, other, own, total, send, receive, fetch):
        here = positions()
        core, x = here["core"], here["x"]
        sibling = reached(here, "sibling", 0)
        greet(here, [("sibling", 0)] + [(0, right) for right, _ in X_STEPS])
        order = [lax.rem(x + step, count) for _, step in X_STEPS] + [x]
        swaps, loads = [], []
        for index, spot in enumerate(order):
            swap = remote(
                terms_ref.at[spot, 1 - core],
                other.at[index],
                send.at[index],
                receive.at[index],
                sibling,
            )
            load = pltpu.make_async_copy(terms_ref.at[spot, core], own.at[index], fetch.at[index])
            swap.start()
            load.start()
            swaps.append(swap)
            loads.append(load)
        sends = []
        for index, spot in enumerate(order):
            loads[index].wait()
            swaps[index].wait_recv()
            total[index] = (own[index].astype(F32) + other[index].astype(F32)).astype(BF16)
            if index < len(X_STEPS):
                copy = remote(
                    total.at[index],
                    parts_ref.at[x],
                    send.at[count + index],
                    receive.at[count + index],
                    reached(here, 0, X_STEPS[index][0]),
                )
            else:
                copy = pltpu.make_async_copy(total.at[index], parts_ref.at[x], fetch.at[count])
            copy.start()
            sends.append(copy)
        for swap in swaps:
            swap.wait_send()
        for copy in sends:
            copy.wait()

    return pl.pallas_call(
        body,
        out_shape=jax.ShapeDtypeStruct((count, rows, width), BF16),
        in_specs=[pl.BlockSpec(memory_space=pl.ANY)],
        out_specs=pl.BlockSpec(memory_space=pl.ANY),
        scratch_shapes=[
            pltpu.VMEM((count, rows, width), BF16),
            pltpu.VMEM((count, rows, width), BF16),
            pltpu.VMEM((count, rows, width), BF16),
            pltpu.SemaphoreType.DMA((2 * count,)),
            pltpu.SemaphoreType.DMA((2 * count,)),
            pltpu.SemaphoreType.DMA((count + 1,)),
        ],
        compiler_params=pltpu.CompilerParams(
            collective_id=collective, has_side_effects=True, vmem_limit_bytes=48 * 1024 * 1024
        ),
    )(terms)


def gradients_out(collective, weight_grads, slabs):
    n_lat, n_mp = lax.axis_size("lat"), lax.axis_size("mp")
    kinds, width, _ = weight_grads.shape
    pair, group, share = kinds // 2, width // n_mp, width // n_lat

    def body(
        weight_ref, slab_ref, out_ref, got_ref, edge_ref,
        other, total, parts, turned, landed, send, receive,
    ):
        here = positions()
        lat, mp, core = here["lat"], here["mp"], here["core"]
        sibling = reached(here, "sibling", 0)
        barrier = pltpu.get_barrier_semaphore()
        greeted = [sibling]
        greeted += [reached(here, 0, -step) for step in range(1, n_mp)]
        greeted += [reached(here, -1, -step) for step in range(n_mp)]
        greeted += [reached(here, -step, 0) for step in range(1, n_lat)]
        for target in greeted:
            pl.semaphore_signal(barrier, inc=1, **device_of(target))
        pl.semaphore_wait(barrier, len(greeted))

        copies = []

        def sent(source, landing, target):
            index = len(copies)
            copy = remote(source, landing, send.at[index], receive.at[index], target)
            copy.start()
            copies.append(copy)
            return copy

        swap = sent(weight_ref.at[pl.ds(pair * (1 - core), pair)], other, sibling)
        for step in range(1, n_mp):
            target = reached(here, 0, step)
            sent(slab_ref.at[target["mp"]], got_ref.at[mp], target)
        for step in range(n_mp):
            target = reached(here, 1, step)
            sent(slab_ref.at[target["mp"]], edge_ref.at[mp], target)

        own_slab = pltpu.make_async_copy(slab_ref.at[mp], got_ref.at[mp], send.at[60])
        own_slab.start()

        swap.wait_recv()
        total[...] = (
            weight_ref[pl.ds(pair * core, pair)].astype(F32) + other[...].astype(F32)
        ).astype(BF16)
        scattered = []
        for step in range(1, n_mp):
            target = reached(here, 0, step)
            rows = pl.ds(pl.multiple_of(group * target["mp"], group), group)
            scattered.append(sent(total.at[:, rows], parts.at[mp], target))
        gathered = total[:, pl.ds(pl.multiple_of(group * mp, group), group), :].astype(F32)
        for step in range(1, n_mp):
            scattered[step - 1].wait_recv()
            gathered = gathered + parts[lax.rem(mp + n_mp - step, n_mp)].astype(F32)
        flat = gathered.reshape(pair * group, width).T.astype(BF16)
        for index in range(n_lat):
            turned[index] = flat[index * share : (index + 1) * share]
        spread = []
        for step in range(1, n_lat):
            target = reached(here, step, 0)
            spread.append(sent(turned.at[target["lat"]], landed.at[lat], target))
        landed[lat] = turned[lat]
        for copy in spread:
            copy.wait_recv()
        for half in range(2):
            result = landed[half].astype(F32)
            for index in range(half + 2, n_lat, 2):
                result = result + landed[index].astype(F32)
            out_ref[:, half * pair * group : (half + 1) * pair * group] = result

        done = [swap] + scattered + spread
        for copy in copies:
            copy.wait_send()
            if not any(copy is other_copy for other_copy in done):
                copy.wait_recv()
        own_slab.wait()

    any_space = pl.BlockSpec(memory_space=pl.ANY)
    vmem = pl.BlockSpec(memory_space=pltpu.VMEM)
    return pl.pallas_call(
        body,
        out_shape=[
            jax.ShapeDtypeStruct((share, kinds * group), F32),
            jax.ShapeDtypeStruct(slabs.shape, BF16),
            jax.ShapeDtypeStruct(slabs.shape, BF16),
        ],
        in_specs=[vmem, any_space],
        out_specs=[vmem, any_space, any_space],
        scratch_shapes=[
            pltpu.VMEM((pair, width, width), BF16),
            pltpu.VMEM((pair, width, width), BF16),
            pltpu.VMEM((n_mp, pair, group, width), BF16),
            pltpu.VMEM((n_lat, share, pair * group), BF16),
            pltpu.VMEM((n_lat, share, pair * group), BF16),
            pltpu.SemaphoreType.DMA((64,)),
            pltpu.SemaphoreType.DMA((64,)),
        ],
        compiler_params=pltpu.CompilerParams(
            collective_id=collective, has_side_effects=True, vmem_limit_bytes=48 * 1024 * 1024
        ),
    )(weight_grads, slabs)


def local_kernel(body, operands, outputs, scratch=(), scalars=0, outside=0):
    spaces = [pltpu.SMEM] * scalars + [pltpu.VMEM] * (len(operands) - scalars - outside)
    spaces += [pl.ANY] * outside
    return pl.pallas_call(
        body,
        out_shape=[jax.ShapeDtypeStruct(shape, dtype) for shape, dtype in outputs],
        in_specs=[pl.BlockSpec(memory_space=space) for space in spaces],
        out_specs=[pl.BlockSpec(memory_space=pltpu.VMEM)] * len(outputs),
        scratch_shapes=list(scratch),
        compiler_params=pltpu.CompilerParams(vmem_limit_bytes=48 * 1024 * 1024),
    )(*operands)


def dot_nn(left, right):
    return lax.dot_general(left, right, (((1,), (0,)), ((), ())), preferred_element_type=F32)


def dot_nt(left, right):
    return lax.dot_general(left, right, (((1,), (1,)), ((), ())), preferred_element_type=F32)


def dot_tn(left, right):
    return lax.dot_general(left, right, (((0,), (0,)), ((), ())), preferred_element_type=F32)


def halves_beside(values):
    half = values.shape[-2] // 2
    return jnp.concatenate([values[..., :half, :], values[..., half:, :]], axis=-1)


def groups_joined(slabs):
    count, half, _ = slabs.shape
    view = slabs.reshape(count, half, 2, HDIM).transpose(2, 1, 0, 3)
    return view.reshape(2 * half, count * HDIM)


def to_windows(grid):
    row_count, lon_count = (grid.shape[0], grid.shape[1])
    trailing = grid.shape[2:]
    view = grid.reshape((row_count // WIN_H, WIN_H, lon_count // WIN_W, WIN_W) + trailing)
    view = jnp.swapaxes(view, 1, 2)
    return view.reshape(((row_count // WIN_H) * (lon_count // WIN_W), WIN_H * WIN_W) + trailing)


def from_windows(windows):
    bands, columns, _, width = windows.shape
    view = windows.reshape((bands, columns, WIN_H, WIN_W, width))
    view = jnp.swapaxes(view, 1, 2)
    return view.reshape((bands * WIN_H, columns * WIN_W, width))


def merge_patches(grid, padded):
    row_count, lon_count, features = grid.shape
    view = grid.reshape(row_count // 2, 2, lon_count // 2, 2, features)
    view = view.transpose(1, 3, 0, 2, 4).reshape(4, row_count * lon_count // 4, features)
    return jnp.pad(view, ((0, 0), (0, padded - view.shape[1]), (0, 0)))


def norm_stats(values, count):
    center = sum(jnp.sum(value, axis=1, keepdims=True) for value in values) / count
    second = sum(jnp.sum(value * value, axis=1, keepdims=True) for value in values) / count
    return (center, lax.rsqrt(second - center * center + EPSILON))


def norm_backward(grads, gains, units, scale_inv, count):
    scaled = [grad * gain for grad, gain in zip(grads, gains)]
    first = sum(jnp.sum(value, axis=1, keepdims=True) for value in scaled) / count
    second = (
        sum(jnp.sum(value * unit, axis=1, keepdims=True) for value, unit in zip(scaled, units))
        / count
    )
    return [scale_inv * (value - first - unit * second) for value, unit in zip(scaled, units)]


def pair_slabs(upper, lower, out_ref, first_rows):
    low = lax.broadcasted_iota(jnp.int32, (upper.shape[0], 2 * HDIM), 1) < HDIM
    rows = pl.ds(first_rows, upper.shape[0])
    for pair in range(upper.shape[1] // (2 * HDIM)):
        lanes = slice(2 * HDIM * pair, 2 * HDIM * (pair + 1))
        one, two = upper[:, lanes], lower[:, lanes]
        swapped_one = jnp.concatenate([one[:, HDIM:], one[:, :HDIM]], axis=1)
        swapped_two = jnp.concatenate([two[:, HDIM:], two[:, :HDIM]], axis=1)
        out_ref[2 * pair, rows, :] = jnp.where(low, one, swapped_two).astype(BF16)
        out_ref[2 * pair + 1, rows, :] = jnp.where(low, swapped_one, two).astype(BF16)


WIN = WIN_H * WIN_W
FACTOR = HDIM ** (-0.5)


def heads_apart(values):
    low = lax.broadcasted_iota(jnp.int32, values.shape, 1) < HDIM
    zero = jnp.zeros_like(values)
    both = [jnp.where(low, values, zero), jnp.where(low, zero, values)]
    return jnp.concatenate(both, axis=0).astype(BF16)


def heads_together(values):
    low = lax.broadcasted_iota(jnp.int32, (WIN, 2 * HDIM), 1) < HDIM
    return jnp.where(low, values[:WIN], values[WIN:])


def window_probs(cut, window, query, keys):
    scores = dot_nt(query, keys) * FACTOR
    spot = lax.broadcasted_iota(jnp.int32, scores.shape, 0)
    spot = jnp.where(spot >= WIN, spot - WIN, spot)
    other = lax.broadcasted_iota(jnp.int32, scores.shape, 1)
    edge = cut * WIN_W - jnp.where(window >= 3, WIN, 0)
    same = (spot >= edge) == (other >= edge)
    scores = jnp.where(same, scores, MASKED)
    weights = jnp.exp(scores - jnp.max(scores, axis=1, keepdims=True))
    return weights / jnp.sum(weights, axis=1, keepdims=True)


def framed_packed(fields_ref, gain_ref, weights_ref, packed):
    values = fields_ref[...].astype(F32)
    center, scale_inv = norm_stats([values], values.shape[1])
    unit = (values - center) * scale_inv
    framed = (unit * gain_ref[...]).astype(BF16)
    for kind in range(3):
        packed[kind] = dot_nt(framed, weights_ref[kind]).astype(BF16).astype(F32)
    return (framed, unit, scale_inv)


def window_parts(refs, window, pair):
    rows = pl.ds(pl.multiple_of(window * WIN, 8), WIN)
    lanes = slice(2 * HDIM * pair, 2 * HDIM * (pair + 1))
    return [ref[rows, lanes] for ref in refs]


def attention_forward(cut_ref, fields_ref, gain_ref, weights_ref, out_ref, context_ref, packed, held):
    framed_packed(fields_ref, gain_ref, weights_ref, packed)
    cut = cut_ref[0]
    windows = fields_ref.shape[0] // WIN

    def step(window, carry):
        rows = pl.ds(pl.multiple_of(window * WIN, 8), WIN)
        for pair in range(fields_ref.shape[1] // (2 * HDIM)):
            query, keys, values = window_parts([packed.at[kind] for kind in range(3)], window, pair)
            probs = window_probs(cut, window, heads_apart(query), keys.astype(BF16))
            joined = dot_nn(probs.astype(BF16), values.astype(BF16))
            held[rows, 2 * HDIM * pair : 2 * HDIM * (pair + 1)] = heads_together(joined)
        return carry

    lax.fori_loop(0, windows, step, 0)
    context = held[...].astype(BF16)
    context_ref[...] = context
    out_ref[...] = dot_nn(context, weights_ref[3]).astype(BF16)


def attention_backward(
    cut_ref, fields_ref, gain_ref, weights_ref, context_ref, grad_ref, slab_ref, weight_ref,
    packed, grads, held,
):
    framed, unit, scale_inv = framed_packed(fields_ref, gain_ref, weights_ref, packed)
    cut = cut_ref[0]
    windows = fields_ref.shape[0] // WIN
    grad_framed = grad_ref[...]
    held[...] = dot_nt(grad_framed, weights_ref[3]).astype(BF16).astype(F32)

    def step(window, carry):
        rows = pl.ds(pl.multiple_of(window * WIN, 8), WIN)
        for pair in range(fields_ref.shape[1] // (2 * HDIM)):
            lanes = slice(2 * HDIM * pair, 2 * HDIM * (pair + 1))
            query, keys, values, grad = window_parts(
                [packed.at[kind] for kind in range(3)] + [held], window, pair
            )
            query, grad = heads_apart(query), heads_apart(grad)
            keys, values = keys.astype(BF16), values.astype(BF16)
            probs = window_probs(cut, window, query, keys)
            grad_probs = dot_nt(grad, values)
            inner = jnp.sum(grad_probs * probs, axis=1, keepdims=True)
            grad_scores = (probs * (grad_probs - inner) * FACTOR).astype(BF16)
            grads[0, rows, lanes] = heads_together(dot_nn(grad_scores, keys))
            grads[1, rows, lanes] = dot_tn(grad_scores, query)
            grads[2, rows, lanes] = dot_tn(probs.astype(BF16), grad)
        return carry

    lax.fori_loop(0, windows, step, 0)
    grad_normed = jnp.zeros(fields_ref.shape, F32)
    for kind in range(3):
        grad_kind = grads[kind].astype(BF16)
        weight_ref[kind] = dot_tn(grad_kind, framed).astype(BF16)
        grad_normed = grad_normed + dot_nn(grad_kind, weights_ref[kind])
    weight_ref[3] = dot_tn(context_ref[...], grad_framed).astype(BF16)
    (back,) = norm_backward([grad_normed], [gain_ref[...]], [unit], scale_inv, unit.shape[1])
    result = grad_framed.astype(F32) + back
    half = result.shape[0] // 2
    pair_slabs(result[:half], result[half:], slab_ref, 0)


def section_loads(core_ref, own_ref, other_ref, weights, loaded):
    core = core_ref[0]
    loads = [
        pltpu.make_async_copy(own_ref, weights.at[core], loaded.at[0]),
        pltpu.make_async_copy(other_ref, weights.at[1 - core], loaded.at[1]),
    ]
    for load in loads:
        load.start()
    return loads


def merge_forward(
    core_ref, fields_ref, attention_ref, cot_ref, gain_ref, mlp_gain_ref, own_ref, other_ref,
    pair_ref, hidden_ref, merged_ref, grad_ref, weights, loaded,
):
    loads = section_loads(core_ref, own_ref, other_ref, weights, loaded)
    width_two = merged_ref.shape[1]
    hidden = []
    for patch in range(4):
        value = fields_ref[patch].astype(F32) + attention_ref[patch].astype(F32)
        hidden_ref[patch] = value.astype(BF16)
        hidden.append(value.astype(BF16).astype(F32))
    center, scale_inv = norm_stats(hidden, 4 * hidden[0].shape[1])
    merged = jnp.zeros(merged_ref.shape, F32)
    grad = jnp.zeros(merged_ref.shape, F32)
    for load in loads:
        load.wait()
    for patch in range(4):
        normed = (hidden[patch] - center) * scale_inv * gain_ref[patch : patch + 1, :]
        merged = merged + dot_nn(normed.astype(BF16), weights[0, patch])
        grad = grad + dot_nn(cot_ref[patch], weights[1, patch])
    merged_ref[...] = merged.astype(BF16)
    merged = merged.astype(BF16).astype(F32)
    center, scale_inv = norm_stats([merged], width_two)
    mlp_in = (merged - center) * scale_inv * mlp_gain_ref[...]
    pair_ref[:, :width_two] = mlp_in.astype(BF16)
    pair_ref[:, width_two:] = grad.astype(BF16)
    grad_ref[...] = grad


def merge_backward(
    core_ref, parts_ref, merged_ref, grad_ref, hidden_ref, cot_ref, gain_ref, mlp_gain_ref,
    own_ref, other_ref, slab_ref, out_ref, weights, loaded,
):
    loads = section_loads(core_ref, own_ref, other_ref, weights, loaded)
    width_two = merged_ref.shape[1]
    count = merged_ref.shape[0]
    total = parts_ref[0].astype(F32)
    for index in range(1, parts_ref.shape[0]):
        total = total + parts_ref[index].astype(F32)
    merged = merged_ref[...].astype(F32)
    bottom = (merged + total[:, :width_two]).astype(BF16)
    for load in loads:
        load.wait()
    decoded = [
        hidden_ref[patch].astype(F32) + dot_nt(bottom, weights[1, patch])
        for patch in range(4)
    ]
    for side in range(2):
        pair_slabs(decoded[side], decoded[2 + side], slab_ref, side * count)
    center, scale_inv = norm_stats([merged], width_two)
    unit = (merged - center) * scale_inv
    (back,) = norm_backward(
        [total[:, width_two:]], [mlp_gain_ref[...]], [unit], scale_inv, width_two
    )
    grad_merged = (grad_ref[...] + back).astype(BF16)
    hidden = [hidden_ref[patch].astype(F32) for patch in range(4)]
    center, scale_inv = norm_stats(hidden, 4 * hidden[0].shape[1])
    units = [(value - center) * scale_inv for value in hidden]
    backs = norm_backward(
        [dot_nt(grad_merged, weights[0, patch]) for patch in range(4)],
        [gain_ref[patch : patch + 1, :] for patch in range(4)],
        units,
        scale_inv,
        4 * hidden[0].shape[1],
    )
    for patch in range(4):
        out_ref[patch] = (cot_ref[patch].astype(F32) + backs[patch]).astype(BF16)


def shards(
    fields,
    first_gain,
    qkv_weight,
    proj_weight,
    merge_gain,
    merge_weight,
    mlp_gain,
    up_weight,
    down_weight,
    expand_weight,
    lat_shift,
    lon_shift,
    cotangent,
):
    n_lat, n_mp = lax.axis_size("lat"), lax.axis_size("mp")
    lat, core = lax.axis_index("lat"), lax.rem(lax.axis_index("lat"), 2)
    lat_offset = lat_shift[0]
    lon_offset = lon_shift[0]
    rows, lon_count, group = fields.shape
    width = group * n_mp
    block = lon_count // n_mp
    wide = block + WIN_W
    bands, columns = rows // WIN_H, block // WIN_W
    tokens = rows * block
    width_two = merge_weight.shape[2]
    span = up_weight.shape[1]
    merged_count = tokens // 4
    padded = -(-merged_count // 16) * 16
    others = range(n_mp)

    section = jnp.where(core == 0, merge_weight, expand_weight.transpose(1, 2, 0))
    section_own = lax.all_gather(section, "mp", axis=1, tiled=True)
    blocks = fields.reshape(rows, n_mp, block, group).transpose(1, 0, 2, 3)
    margin = jnp.roll(blocks[:, :, :WIN_W], -1, axis=0)
    field_blocks = jnp.concatenate([blocks, margin], axis=2)
    body_slab = halves_beside(field_blocks.reshape(n_mp, rows * wide, group))
    edge_slab = halves_beside(field_blocks[:, :WIN_H].reshape(n_mp, WIN_H * wide, group))
    cot_blocks = cotangent.reshape(rows, n_mp, block, group).transpose(1, 0, 2, 3)
    cot_slab = halves_beside(cot_blocks.reshape(n_mp, tokens, group))
    weights = jnp.concatenate(
        [qkv_weight.transpose(1, 2, 0), proj_weight.transpose(1, 0)[None]], axis=0
    )
    gains = jnp.pad(jnp.concatenate([first_gain[None], merge_gain], axis=0), ((0, 3), (0, 64)))

    def rows_at(here, step):
        return pl.ds(pl.multiple_of(lax.rem(here["mp"] + n_mp - step, n_mp) * group, group), group)

    def core_half(ref, here, target):
        return ref.at[pl.ds(2 * here["core"], 2)]

    def core_half_rows(step):
        return lambda ref, here, target: ref.at[pl.ds(2 * here["core"], 2), rows_at(here, step)]

    def own_rows(ref, here, target):
        return ref.at[:, rows_at(here, 0)]

    body_got, edge_got, weights_all, gains_all = exchange(
        1,
        [body_slab, edge_slab, weights, gains],
        [
            (body_slab.shape, BF16),
            (edge_slab.shape, BF16),
            ((4, width, width), BF16),
            ((n_mp,) + gains.shape, F32),
        ],
        [(2, core_half, 2, core_half_rows(0), 0, step) for step in range(1, n_mp)]
        + [(3, None, 3, "mp", 0, step) for step in others]
        + [(0, "mp", 0, "mp", 0, step) for step in others]
        + [(1, "mp", 1, "mp", -1, step) for step in others]
        + [(2, None, 2, own_rows, 0, 0)]
        + [
            (2, core_half_rows(step), 2, core_half_rows(step), "sibling", 0, step - 1)
            for step in range(1, n_mp)
        ],
    )
    body = groups_joined(body_got).reshape(rows, wide, width)
    edge = groups_joined(edge_got).reshape(WIN_H, wide, width)
    has_shard = lax.rem(lax.axis_index("mp"), 2) == core
    fetch = [
        (at * n_mp + m, at * n_mp + (m ^ 1))
        for at in range(n_lat)
        for m in range(n_mp)
        if at % 2 == m % 2
    ]
    up_late, down_late, gains_all = lax.optimization_barrier((up_weight, down_weight, gains_all))
    up_shard, down_shard = (
        jnp.where(has_shard, weight, lax.ppermute(weight, ("lat", "mp"), fetch))
        for weight in (up_late, down_late)
    )

    first_all = gains_all[:, 0, :group].reshape(1, width)
    merge_gain_all = gains_all[:, 1:5, :group].transpose(1, 0, 2).reshape(4, width)
    mlp_gain_row = mlp_gain.reshape(1, width_two)
    own_fields = merge_patches(body[:, :block], padded)

    def into_frame(whole):
        part = lax.dynamic_slice(
            whole, (lat_offset, lon_offset, jnp.int32(0)), (rows, block, width)
        )
        return to_windows(part).reshape(tokens, width)

    framed_fields = into_frame(jnp.concatenate([body, edge], axis=0))
    cut = (jnp.int32(rows) * (n_lat - lat) - lat_offset).reshape(1)
    attention_framed, context = local_kernel(
        attention_forward,
        [cut, framed_fields, first_all, weights_all],
        [((tokens, width), BF16), ((tokens, width), BF16)],
        [pltpu.VMEM((3, tokens, width), F32), pltpu.VMEM((tokens, width), F32)],
        scalars=1,
    )
    window_shape = (bands, columns, WIN, width)
    around = (bands + 1, columns + 1, WIN, width)
    own_windows = attention_framed.reshape(window_shape)
    halo, section_other, cot_got = exchange(
        2,
        [own_windows, section_own, cot_slab],
        [(around, BF16), (section_own.shape, BF16), (cot_slab.shape, BF16)],
        [
            (0, (bands - 1, columns - 1), 0, (0, 0), 1, 1),
            (0, (slice(0, bands), columns - 1), 0, (slice(1, bands + 1), 0), 0, 1),
            (0, (bands - 1,), 0, (0, slice(1, columns + 1)), 1, 0),
            (1, None, 1, None, "sibling", 0),
        ]
        + [(2, "mp", 2, "mp", 0, step) for step in others],
    )
    cot_patches = merge_patches(groups_joined(cot_got).reshape(rows, block, width), padded)
    halo = halo.at[1:, 1:].set(own_windows)
    attention = lax.dynamic_slice(
        from_windows(halo),
        (WIN_H - lat_offset, WIN_W - lon_offset, jnp.int32(0)),
        (rows, block, width),
    )
    n_x = n_mp // 2
    section_scratch = [
        pltpu.VMEM((2,) + section_own.shape, BF16),
        pltpu.SemaphoreType.DMA((2,)),
    ]
    pair, hidden, merged, grad_bottom = local_kernel(
        merge_forward,
        [
            core.reshape(1),
            own_fields,
            merge_patches(attention, padded),
            cot_patches,
            merge_gain_all,
            mlp_gain_row,
            section_own,
            section_other,
        ],
        [
            ((padded, 2 * width_two), BF16),
            ((4, padded, width), BF16),
            ((padded, width_two), BF16),
            ((padded, width_two), F32),
        ],
        section_scratch,
        scalars=1,
        outside=2,
    )

    def chip_spot(step):
        def spot(ref, here, target):
            return ref.at[lax.rem(here["x"] + n_x + step, n_x), here["core"]]

        return spot

    (pairs,) = exchange(
        3,
        [pair],
        [((n_x, 2) + pair.shape, BF16)],
        [
            (0, None, 0, chip_spot(0), 0, 4),
            (0, None, 0, chip_spot(0), 0, 2),
            (0, None, 0, chip_spot(0), 0, -2),
            (0, None, 0, chip_spot(0), "sibling", 0),
            (0, None, 0, chip_spot(0), 0, 0),
            (0, chip_spot(-1), 0, chip_spot(-1), "sibling", 0, 1),
            (0, chip_spot(1), 0, chip_spot(1), "sibling", 0, 2),
            (0, chip_spot(-2), 0, chip_spot(-2), "sibling", 0, 0),
        ],
    )
    pairs = pairs.reshape(n_mp * padded, 2 * width_two)
    mlp_in, bottom_grad = pairs[:, :width_two], pairs[:, width_two:]
    hidden_up = jnp.dot(mlp_in, up_shard, preferred_element_type=F32)
    activated = jax.nn.gelu(hidden_up).astype(BF16)
    grad_act = jnp.dot(bottom_grad, down_shard, preferred_element_type=F32)
    gelu_back = jax.vjp(jax.nn.gelu, hidden_up)[1]
    grad_pre = gelu_back(grad_act)[0].astype(BF16)
    terms = jnp.concatenate(
        [
            jnp.einsum("af,ef->ae", activated, down_shard, preferred_element_type=F32),
            jnp.einsum("af,ef->ae", grad_pre, up_shard, preferred_element_type=F32),
        ],
        axis=1,
    ).astype(BF16)
    parts = terms_back(4, terms.reshape(n_x, 2, padded, 2 * width_two))
    shard_groups = [
        [at * n_mp + 2 * x + z for at in range(core_at, n_lat, 2) for z in range(2)]
        for x in range(n_x)
        for core_at in range(2)
    ]
    owners = [
        ((2 * spot + c) * n_mp + 2 * x + z, (2 * spot + z) * n_mp + 2 * x + c)
        for spot in range(n_lat // 2)
        for x in range(n_x)
        for c in range(2)
        for z in range(2)
    ]
    local_grads = [
        jnp.einsum("ae,af->ef", mlp_in, grad_pre, preferred_element_type=F32),
        jnp.einsum("ao,af->of", bottom_grad, activated, preferred_element_type=F32),
    ]
    grad_up, grad_down = (
        lax.ppermute(
            lax.psum_scatter(
                part.astype(BF16),
                ("lat", "mp"),
                scatter_dimension=0,
                axis_index_groups=shard_groups,
                tiled=True,
            ),
            ("lat", "mp"),
            owners,
        ).astype(F32)
        for part in local_grads
    )
    decoded_slab, grad_hidden = local_kernel(
        merge_backward,
        [
            core.reshape(1),
            parts,
            merged,
            grad_bottom,
            hidden,
            cot_patches,
            merge_gain_all,
            mlp_gain_row,
            section_own,
            section_other,
        ],
        [((n_mp, 2 * padded, 2 * group), BF16), ((4, padded, width), BF16)],
        section_scratch,
        scalars=1,
        outside=2,
    )
    grad_windows = grad_hidden[:, :merged_count].reshape(
        2, 2, bands, WIN_H // 2, columns, WIN_W // 2, width
    )
    grad_windows = grad_windows.transpose(2, 4, 3, 0, 5, 1, 6).reshape(window_shape)
    halo, decoded_got = exchange(
        5,
        [grad_windows, decoded_slab],
        [(around, BF16), (decoded_slab.shape, BF16)],
        [
            (0, (0, 0), 0, (bands, columns), -1, -1),
            (0, (slice(0, bands), 0), 0, (slice(0, bands), columns), 0, -1),
            (0, (0,), 0, (bands, slice(0, columns)), -1, 0),
        ]
        + [(1, "mp", 1, "mp", 0, step) for step in others],
    )
    halo = halo.at[:bands, :columns].set(grad_windows)
    grad_framed = into_frame(from_windows(halo))
    grad_slab, weight_grads = local_kernel(
        attention_backward,
        [cut, framed_fields, first_all, weights_all, context, grad_framed],
        [((n_mp, tokens // 2, 2 * group), BF16), ((4, width, width), BF16)],
        [
            pltpu.VMEM((3, tokens, width), F32),
            pltpu.VMEM((3, tokens, width), F32),
            pltpu.VMEM((tokens, width), F32),
        ],
        scalars=1,
    )
    weight_total, grad_got, edge_got = gradients_out(6, weight_grads, grad_slab)
    grad_qkv = weight_total[:, : 3 * group].reshape(width // n_lat, 3, group)
    grad_proj = weight_total[:, 3 * group :]
    decoded_view = decoded_got.reshape(n_mp, 2, padded, 2, group)[:, :, :merged_count]
    decoded_view = decoded_view.reshape(n_mp, 2, rows // 2, block // 2, 2, group)
    decoded = decoded_view.transpose(2, 4, 0, 3, 1, 5).reshape(rows, lon_count, group)

    def columns_joined(slabs):
        view = slabs.reshape(n_mp, columns, WIN_H, WIN_W, -1, group)
        return view.transpose(4, 2, 0, 1, 3, 5).reshape(-1, lon_count, group)

    grad_rows = jnp.concatenate(
        [columns_joined(edge_got[..., group:]), columns_joined(grad_got)], axis=0
    )
    grad_rows = jnp.concatenate([grad_rows[:, -WIN_W:], grad_rows], axis=1)
    grad_input = lax.dynamic_slice(
        grad_rows,
        (WIN_H - lat_offset, WIN_W - lon_offset, jnp.int32(0)),
        (rows, lon_count, group),
    ).astype(F32)
    return (decoded, grad_input, grad_qkv, grad_proj, grad_up, grad_down)


def solution(mesh):
    return jax.shard_map(
        shards,
        mesh=mesh,
        in_specs=(
            P("lat", None, "mp"),
            P("mp"),
            P(None, None, "mp"),
            P(None, "mp"),
            P(None, "mp"),
            P(None, "mp", None),
            P(),
            P(None, "mp"),
            P(None, "mp"),
            P(None, None, "mp"),
            P(),
            P(),
            P("lat", None, "mp"),
        ),
        out_specs=(
            P("lat", None, "mp"),
            P("lat", None, "mp"),
            P("lat", None, "mp"),
            P("lat", "mp"),
            P("lat", "mp"),
            P("lat", "mp"),
        ),
        check_vma=False,
    )
```

profile of v0, /device:TPU:1, one launch (start us, length us, event | category | flops | bytes accessed | tf_op | source)
XLA Modules:
  0.0 386.1 jit_solution(13301432662670577987)
XLA Ops:
  7.2 1.9 bitcast_select_fusion
  14.6 38.9 %shard_map.172 = (bf16[8,288,128]{2,1,0:T(8,128)(2,1)}, bf16[8,144,128]{2,1,0:T(8,128)(2,1)}, bf16[4,512,512]{2,1,0:T(8,128)(2,1)}, f32[8,8,128]{2,1,0:T(8,128)}) custom-call(bf16[8,288,128]{2,1,0:T(8,128)(2,1)} %pad_maximum_fusion.1.refs_0_, bf16[8,144,128]{2,1,0:T(8,128)(2,1)} %pad_maximum_fusion.3.refs_1_, bf16[4,64,512]{2,1,0:T(8,128)(2,1)} %pad_maximum_fusion.4.refs_2_, ...), custom_call_target="tpu_custom_call" | custom-call | tf_op jit(solution)/shard_map/pallas_call | solution.py:109
  69.6 6.9 %shard_map.173 = (bf16[432,512]{1,0:T(8,128)(2,1)S(1)}, bf16[432,512]{1,0:T(8,128)(2,1)S(1)}) custom-call(s32[1]{0:T(128)} %bitcast.12.cut_ref, bf16[432,512]{1,0:T(8,128)(2,1)S(1)} %reshape_reshape.14.fields_ref, f32[1,512]{1,0:T(1,128)S(1)} %reshape_squeeze.3.gain_ref, bf16[4,512,512]{2,1,0:T(8,128)(2,1)S(1)} %copy-done), custom_call_target="tpu_custom_call" | custom-call | tf_op jit(solution)/shard_map/pallas_call | solution.py:295
  78.3 23.3 %all-gather.2.cloned.1.call-done.refs_1_.own_ref = bf16[4,512,1024]{2,1,0:T(8,128)(2,1)} async-done(((bf16[4,64,1024]{2,1,0:T(8,128)(2,1)}), bf16[4,512,1024]{2,1,0:T(8,128)(2,1)}) %all-gather.2.cloned.1.call-update) | async-done | bytes 4194320 | tf_op jit(solution)/shard_map/all_gather | solution.py:595
  101.6 20.9 %shard_map.174 = (bf16[3,4,72,512]{3,2,1,0:T(8,128)(2,1)}, bf16[4,512,1024]{2,1,0:T(8,128)(2,1)}, bf16[8,216,128]{2,1,0:T(8,128)(2,1)}) custom-call(bf16[2,3,72,512]{3,2,1,0:T(8,128)(2,1)} %bitcast.79, bf16[4,512,1024]{2,1,0:T(8,128)(2,1)} %all-gather.2.cloned.1.call-done.refs_1_.own_ref, bf16[8,216,128]{2,1,0:T(8,128)(2,1)} %pad_maximum_fusion.2.refs_2_), custom_call_target="tpu_custom_call" | custom-call | tf_op jit(solution)/shard_map/pallas_call | solution.py:109
  123.4 1.6 copy.75
  126.3 2.1 reshape.216
  128.4 1.9 constant_dynamic-slice_fusion.1
  134.5 2.0 copy.79
  136.6 2.4 copy.80
  138.9 2.5 reshape_reshape_reshape.3
  142.4 2.0 reshape.239
  146.4 4.9 %shard_map.175 = (bf16[112,2048]{1,0:T(8,128)(2,1)S(1)}, bf16[4,112,512]{2,1,0:T(8,128)(2,1)S(1)}, bf16[112,1024]{1,0:T(8,128)(2,1)S(1)}, f32[112,1024]{1,0:T(8,128)S(1)}) custom-call(s32[1]{0:T(128)} %bitcast.core_ref, bf16[4,112,512]{2,1,0:T(8,128)(2,1)S(1)} %pad.23.fields_ref, bf16[4,112,512]{2,1,0:T(8,128)(2,1)S(1)} %copy-done.1, ...), custom_call_target="tpu_custom_call" | custom-call | tf_op jit(solution)/shard_map/pallas_call | solution.py:295
  154.3 26.1 %shard_map.176 = bf16[4,2,112,2048]{3,2,1,0:T(8,128)(2,1)} custom-call(bf16[112,2048]{1,0:T(8,128)(2,1)} %copy-done.9), custom_call_target="tpu_custom_call" | custom-call | tf_op jit(solution)/shard_map/pallas_call | solution.py:109
  180.4 3.0 fusion.13
  184.7 2.4 fusion.18
  188.8 17.8 %collective-permute-done.1 = bf16[1024,512]{1,0:T(8,128)(2,1)S(1)} collective-permute-done((bf16[1024,512]{1,0:T(8,128)(2,1)}, bf16[1024,512]{1,0:T(8,128)(2,1)S(1)}, u32[]{:S(2)}, u32[]{:S(2)}) %collective-permute-start.1) | collective-permute-done | bytes 1048608 | tf_op jit(solution)/shard_map/ppermute | solution.py:650
  206.6 4.5 %fusion.6 = bf16[896,512]{1,0:T(8,128)(2,1)S(1)} fusion(f32[896,512]{1,0:T(8,128)} %copy-done.30, bf16[896,2048]{1,0:T(8,128)(2,1)} %bitcast.92, bf16[1024,512]{1,0:T(8,128)(2,1)} %param.25, bf16[1024,512]{1,0:T(8,128)(2,1)S(1)} %collective-permute-done.1, pred[]{:T(512)S(6)} %eq.7), kind=kOutput, calls=%fused_computation.9 | convolution fusion | flops 949223424 | bytes 6684673 | tf_op jit(solution)/shard_map/dot_general | solution.py:749
  212.0 2.2 fusion.15
  214.4 2.8 convolution_convert_fusion
  219.0 25.5 %shard_map.177.parts_ref = bf16[4,112,2048]{2,1,0:T(8,128)(2,1)S(1)} custom-call(bf16[4,2,112,2048]{3,2,1,0:T(8,128)(2,1)S(1)} %pad_maximum_fusion.terms_ref), custom_call_target="tpu_custom_call" | custom-call | tf_op jit(solution)/shard_map/pallas_call | solution.py:170
  244.5 6.8 %shard_map.178 = (bf16[8,224,128]{2,1,0:T(8,128)(2,1)S(1)}, bf16[4,112,512]{2,1,0:T(8,128)(2,1)S(1)}) custom-call(s32[1]{0:T(128)} %bitcast.core_ref, bf16[4,112,2048]{2,1,0:T(8,128)(2,1)S(1)} %shard_map.177.parts_ref, bf16[112,1024]{1,0:T(8,128)(2,1)S(1)} %copy-done.13, f32[112,1024]{1,0:T(8,128)S(1)} %copy-done.8, bf16[4,112,512]{2,1,0:T(8,128)(2,1)S(1)} %copy-done.6, ...), custom_call_target="tpu_custom_call" | custom-call | tf_op jit(solution)/shard_map/pallas_call | solution.py:295
  253.8 21.3 %shard_map.179 = (bf16[3,4,72,512]{3,2,1,0:T(8,128)(2,1)}, bf16[8,224,128]{2,1,0:T(8,128)(2,1)}) custom-call(bf16[2,3,72,512]{3,2,1,0:T(8,128)(2,1)} %reshape.225.refs_0_, bf16[8,224,128]{2,1,0:T(8,128)(2,1)} %copy-done.4), custom_call_target="tpu_custom_call" | custom-call | tf_op jit(solution)/shard_map/pallas_call | solution.py:109
  275.1 1.8 constant_dynamic-update-slice_fusion.2
  282.1 2.0 reshape.231
  284.1 1.9 copy.91
  287.2 14.5 %shard_map.180 = (bf16[8,216,128]{2,1,0:T(8,128)(2,1)S(1)}, bf16[4,512,512]{2,1,0:T(8,128)(2,1)S(1)}) custom-call(s32[1]{0:T(128)} %bitcast.12.cut_ref, bf16[432,512]{1,0:T(8,128)(2,1)S(1)} %reshape_reshape.14.fields_ref, f32[1,512]{1,0:T(1,128)S(1)} %reshape_squeeze.3.gain_ref, bf16[4,512,512]{2,1,0:T(8,128)(2,1)S(1)} %copy-done, ...), custom_call_target="tpu_custom_call" | custom-call | tf_op jit(solution)/shard_map/pallas_call | solution.py:295
  301.7 38.6 %shard_map.181 = (f32[32,256]{1,0:T(8,128)S(1)}, bf16[8,216,128]{2,1,0:T(8,128)(2,1)S(1)}, bf16[8,216,128]{2,1,0:T(8,128)(2,1)S(1)}) custom-call(bf16[4,512,512]{2,1,0:T(8,128)(2,1)S(1)} %get-tuple-element.75.weight_ref, bf16[8,216,128]{2,1,0:T(8,128)(2,1)S(1)} %get-tuple-element.76.slab_ref), custom_call_target="tpu_custom_call" | custom-call | tf_op jit(solution)/shard_map/pallas_call | solution.py:268
  344.0 3.6 collective-permute-start.3
  347.5 10.7 %reduce-scatter.3.cloned.1.call-done = bf16[64,512]{1,0:T(8,128)(2,1)} async-done(((bf16[1024,512]{1,0:T(8,128)(2,1)}), bf16[64,512]{1,0:T(8,128)(2,1)}) %reduce-scatter.3.cloned.1.call-update) | async-done | bytes 65552 | tf_op jit(solution)/shard_map/reduce_scatter | solution.py:778
  358.2 13.0 %collective-permute-start.2 = (bf16[64,512]{1,0:T(8,128)(2,1)}, bf16[64,512]{1,0:T(8,128)(2,1)S(1)}, u32[]{:S(2)}, u32[]{:S(2)}) collective-permute-start(bf16[64,512]{1,0:T(8,128)(2,1)} %reduce-scatter.3.cloned.1.call-done), channel_id=1, source_target_pairs={{0,0},{1,8},{8,1},{9,9},{2,2},{3,10},{10,3},{11,11},{4,4},{5,12},{... | collective-permute-start | bytes 196616 | tf_op jit(solution)/shard_map/ppermute | solution.py:777
  371.6 1.7 copy.96
  (158 shorter events, 58.3 us)
Async XLA Ops:
  7.2 2.1 copy-start.19
  7.2 94.4 %all-gather.2.cloned.1.call-start = ((), (), s32[]{:S(2)}) async-start(), calls=%async_computation.2 | async-start | bytes 4718592 | tf_op jit(solution)/shard_map/all_gather | solution.py:595
  9.2 334.8 %reduce-scatter.5.cloned.1.call-start = ((), (), s32[]{:S(2)}) async-start(), calls=%async_computation.4 | async-start | bytes 1114112 | tf_op jit(solution)/shard_map/reduce_scatter | solution.py:778
  10.4 1.3 copy-start.22
  10.5 1.3 copy-start.23
  53.6 126.9 %collective-permute-start = (bf16[1024,512]{1,0:T(8,128)(2,1)}, bf16[1024,512]{1,0:T(8,128)(2,1)}, u32[]{:S(2)}, u32[]{:S(2)}) collective-permute-start(bf16[1024,512]{1,0:T(8,128)(2,1)} %param.24), channel_id=1, source_target_pairs={{0,1},{2,3},{4,5},{6,7},{9,8},{11,10},{13,12},{15,14},{16,17},{18,... | collective-permute-start | bytes 3145736 | tf_op jit(solution)/shard_map/ppermute | solution.py:650
  56.6 1.6 copy-start.21
  65.3 4.3 %copy-start = (bf16[4,512,512]{2,1,0:T(8,128)(2,1)S(1)}, bf16[4,512,512]{2,1,0:T(8,128)(2,1)}, u32[]{:S(2)}) copy-start(bf16[4,512,512]{2,1,0:T(8,128)(2,1)} %get-tuple-element.59.weights_ref) | copy-start | bytes 6291460
  68.4 8.8 %copy-start.17 = (bf16[8,216,64]{2,1,0:T(8,128)(2,1)S(1)}, bf16[8,216,64]{2,1,0:T(8,128)(2,1)}, u32[]{:S(2)}) copy-start(bf16[8,216,64]{2,1,0:T(8,128)(2,1)} %copy.104) | copy-start | bytes 663556
  68.4 8.8 %copy-start.18 = (bf16[8,216,64]{2,1,0:T(8,128)(2,1)S(1)}, bf16[8,216,64]{2,1,0:T(8,128)(2,1)}, u32[]{:S(2)}) copy-start(bf16[8,216,64]{2,1,0:T(8,128)(2,1)} %copy.105) | copy-start | bytes 663556
  77.3 24.3 %copy-start.10 = (bf16[432,512]{1,0:T(8,128)(2,1)}, bf16[432,512]{1,0:T(8,128)(2,1)S(1)}, u32[]{:S(2)}) copy-start(bf16[432,512]{1,0:T(8,128)(2,1)S(1)} %get-tuple-element.73.context_ref) | copy-start | bytes 1327108
  101.6 21.0 %copy-start.3 = (bf16[432,512]{1,0:T(8,128)(2,1)S(1)}, bf16[432,512]{1,0:T(8,128)(2,1)}, u32[]{:S(2)}) copy-start(bf16[432,512]{1,0:T(8,128)(2,1)} %copy-done.2) | copy-start | bytes 1327108
  141.5 3.9 %copy-start.14 = (f32[1024]{0:T(1024)S(1)}, f32[1024]{0:T(1024)}, u32[]{:S(2)}) copy-start(f32[1024]{0:T(1024)} %param.23) | copy-start | bytes 12292
  145.4 1.0 copy-start.1
  151.3 0.8 copy-start.5
  180.4 4.3 %copy-start.15 = (bf16[4,2,112,2048]{3,2,1,0:T(8,128)(2,1)S(1)}, bf16[4,2,112,2048]{3,2,1,0:T(8,128)(2,1)}, u32[]{:S(2)}) copy-start(bf16[4,2,112,2048]{3,2,1,0:T(8,128)(2,1)} %shard_map.176) | copy-start | bytes 11010052
  183.5 1.3 copy-start.30
  187.2 171.1 %reduce-scatter.3.cloned.1.call-start = ((), (), s32[]{:S(2)}) async-start(), calls=%async_computation.3 | async-start | bytes 1114112 | tf_op jit(solution)/shard_map/reduce_scatter | solution.py:778
  187.2 24.8 %copy-start.16 = (bf16[4,2,112,2048]{3,2,1,0:T(8,128)(2,1)S(1)}, bf16[4,2,112,2048]{3,2,1,0:T(8,128)(2,1)}, u32[]{:S(2)}) copy-start(bf16[4,2,112,2048]{3,2,1,0:T(8,128)(2,1)} %shard_map.176) | copy-start | bytes 11010052
  187.2 19.4 %collective-permute-start.1 = (bf16[1024,512]{1,0:T(8,128)(2,1)}, bf16[1024,512]{1,0:T(8,128)(2,1)S(1)}, u32[]{:S(2)}, u32[]{:S(2)}) collective-permute-start(bf16[1024,512]{1,0:T(8,128)(2,1)} %param.25), channel_id=1, source_target_pairs={{0,1},{2,3},{4,5},{6,7},{9,8},{11,10},{13,12},{15,14},{16,17},{18,... | collective-permute-start | bytes 3145736 | tf_op jit(solution)/shard_map/ppermute | solution.py:650
  206.6 4.5 %copy-start.28 = (bf16[1024,512]{1,0:T(8,128)(2,1)}, bf16[1024,512]{1,0:T(8,128)(2,1)S(1)}, u32[]{:S(2)}) copy-start(bf16[1024,512]{1,0:T(8,128)(2,1)S(1)} %collective-permute-done.1) | copy-start | bytes 3145732
  211.1 0.9 copy-start.32
  214.3 2.8 copy-start.27
  214.3 2.8 copy-start.29
  214.4 2.8 copy-start.31
  218.9 25.6 %copy-start.6 = (bf16[4,112,512]{2,1,0:T(8,128)(2,1)S(1)}, bf16[4,112,512]{2,1,0:T(8,128)(2,1)}, u32[]{:S(2)}) copy-start(bf16[4,112,512]{2,1,0:T(8,128)(2,1)} %copy-done.5) | copy-start | bytes 1376260
  218.9 25.6 %copy-start.8 = (f32[112,1024]{1,0:T(8,128)S(1)}, f32[112,1024]{1,0:T(8,128)}, u32[]{:S(2)}) copy-start(f32[112,1024]{1,0:T(8,128)} %copy-done.7) | copy-start | bytes 1376260
  218.9 25.6 %copy-start.13 = (bf16[112,1024]{1,0:T(8,128)(2,1)S(1)}, bf16[112,1024]{1,0:T(8,128)(2,1)}, u32[]{:S(2)}) copy-start(bf16[112,1024]{1,0:T(8,128)(2,1)} %copy-done.12) | copy-start | bytes 688132
  282.1 5.1 %copy-start.11 = (bf16[432,512]{1,0:T(8,128)(2,1)S(1)}, bf16[432,512]{1,0:T(8,128)(2,1)}, u32[]{:S(2)}) copy-start(bf16[432,512]{1,0:T(8,128)(2,1)} %copy-done.10) | copy-start | bytes 1327108
  344.0 34.1 %collective-permute-start.3 = (bf16[64,512]{1,0:T(8,128)(2,1)}, bf16[64,512]{1,0:T(8,128)(2,1)S(1)}, u32[]{:S(2)}, u32[]{:S(2)}) collective-permute-start(bf16[64,512]{1,0:T(8,128)(2,1)} %reduce-scatter.5.cloned.1.call-done), channel_id=1, source_target_pairs={{0,0},{1,8},{8,1},{9,9},{2,2},{3,10},{10,3},{11,11},{4,4},{5,12},{... | collective-permute-start | bytes 196616 | tf_op jit(solution)/shard_map/ppermute | solution.py:777
  358.2 20.5 %collective-permute-start.2 = (bf16[64,512]{1,0:T(8,128)(2,1)}, bf16[64,512]{1,0:T(8,128)(2,1)S(1)}, u32[]{:S(2)}, u32[]{:S(2)}) collective-permute-start(bf16[64,512]{1,0:T(8,128)(2,1)} %reduce-scatter.3.cloned.1.call-done), channel_id=1, source_target_pairs={{0,0},{1,8},{8,1},{9,9},{2,2},{3,10},{10,3},{11,11},{4,4},{5,12},{... | collective-permute-start | bytes 196616 | tf_op jit(solution)/shard_map/ppermute | solution.py:777
  371.6 3.1 copy-start.20
  (8 other events, 5.9 us)
Sparse Core Ops, SparseCore 0:
  10.9 90.6 all-gather.1
  187.3 74.4 reduce-scatter.4
  264.3 93.8 reduce-scatter.2
where the time goes:
time: 390 us; the launch traced here: 386 us
  Pallas kernels  204 us (52%)
  local copies, waits for them, and re-layouts  68.3 us (18%)
  waiting for transfers between devices  51.9 us (13%)
  starting transfers between devices  19.8 us (5%)
  matrix products  16.3 us (4%)
  between operations  16.1 us (4%)
  other arithmetic  9.15 us (2%)
    pallas_call x4, Pallas kernels, exchange(): pl.pallas_call(body, out_shape=[jax.ShapeDtypeStruct(shape, dtype) for sh...  107 us
    pallas_call x1, Pallas kernels, gradients_out(): pl.pallas_call(body, out_shape=[jax.ShapeDtypeStruct((share, kinds * grou...  38.6 us
    pallas_call x4, Pallas kernels, local_kernel(): pl.pallas_call(body, out_shape=[jax.ShapeDtypeStruct(shape, dtype) for sh...  33.1 us
    pallas_call x1, Pallas kernels, terms_back(): pl.pallas_call(body, out_shape=jax.ShapeDtypeStruct((count, rows, width),...  25.5 us
    all_gather x1, waiting for transfers between devices, shards(): section_own = lax.all_gather(section, 'mp', axis=1, tiled=True)  23.3 us
    ppermute x2, waiting for transfers between devices, shards(): lax.ppermute(weight, ('lat', 'mp'), fetch)  17.8 us
    unnamed x74, local copies, waits for them, and re-layouts  16.9 us
    ppermute x2, starting transfers between devices, shards(): lax.ppermute(lax.psum_scatter(part.astype(BF16), ('lat', 'mp'), scatter_d...  16.6 us
  transfers between devices with their start and end apart: 7, of which 3 were waited for; matrix products, arithmetic and copies ran while one was open for 20% of the time, Pallas kernels for 53%

commit v1 on v0

--- a/solution.py
+++ b/solution.py
@@ -1,5 +1,6 @@
 import jax
 import jax.numpy as jnp
+import numpy as np
 from jax import lax
 from jax.experimental import pallas as pl
 from jax.experimental.pallas import tpu as pltpu
@@ -29,6 +30,8 @@
     n_lat, n_mp = lax.axis_size("lat"), lax.axis_size("mp")
     if down == "sibling":
         return {"lat": here["lat"] + 1 - 2 * here["core"], "mp": here["mp"]}
+    if down == "flip":
+        return {"lat": here["lat"], "mp": 2 * here["x"] + 1 - here["z"]}
     return {
         "lat": lax.rem(here["lat"] + n_lat + down, n_lat),
         "mp": lax.rem(here["mp"] + n_mp + right, n_mp),
@@ -45,7 +48,7 @@
 def greet(here, steps):
     barrier = pltpu.get_barrier_semaphore()
     for down, right in steps:
-        source = reached(here, down if down == "sibling" else -down, -right)
+        source = reached(here, down if isinstance(down, str) else -down, -right)
         pl.semaphore_signal(barrier, inc=1, **device_of(source))
     pl.semaphore_wait(barrier, len(steps))
 
@@ -96,11 +99,17 @@
                 copy = remote(
                     source_ref, landing_ref, send.at[index], receive.at[index], target
                 )
-            copy.start()
+            if down == "flip":
+                pl.when(here["z"] == here["core"])(copy.start)
+            else:
+                copy.start()
             copies.append(copy)
         for index, copy in enumerate(copies):
             if moves[index][4:6] == (0, 0):
                 copy.wait()
+            elif moves[index][4] == "flip":
+                pl.when(here["z"] == here["core"])(copy.wait_send)
+                pl.when(here["z"] != here["core"])(copy.wait_recv)
             else:
                 copy.wait_send()
                 if index not in arrived:
@@ -122,14 +131,31 @@
 X_STEPS = ((4, 2), (2, 1), (-2, 3))
 
 
-def terms_back(collective, terms):
+def terms_back(collective, terms, up_grads, down_grads):
     count, _, rows, width = terms.shape
-
-    def body(terms_ref, parts_ref, other, own, total, send, receive, fetch):
+    n_lat = lax.axis_size("lat")
+
+    def body(
+        terms_ref, up_ref, down_ref, parts_ref, up_got, down_got,
+        other, own, total, send, receive, fetch, large_send, large_receive,
+    ):
         here = positions()
-        core, x = here["core"], here["x"]
+        lat, core, x, z = here["lat"], here["core"], here["x"], here["z"]
+        mine = 2 * lax.div(lat, 2) + z
+        owner = z == core
         sibling = reached(here, "sibling", 0)
-        greet(here, [("sibling", 0)] + [(0, right) for right, _ in X_STEPS])
+        barrier = pltpu.get_barrier_semaphore()
+        greeted = [sibling] + [reached(here, 0, -right) for right, _ in X_STEPS]
+        for target in greeted:
+            pl.semaphore_signal(barrier, inc=1, **device_of(target))
+        for source in range(n_lat):
+
+            @pl.when(jnp.logical_or(jnp.logical_not(owner), mine != source))
+            def _():
+                target = {"lat": 2 * (source // 2) + z, "mp": 2 * x + source % 2}
+                pl.semaphore_signal(barrier, inc=1, **device_of(target))
+
+        pl.semaphore_wait(barrier, len(greeted) + n_lat - jnp.where(owner, 1, 0))
         order = [lax.rem(x + step, count) for _, step in X_STEPS] + [x]
         swaps, loads = [], []
         for index, spot in enumerate(order):
@@ -145,6 +171,32 @@
             load.start()
             swaps.append(swap)
             loads.append(load)
+
+        def to_owner(which, step):
+            source, landing = ((up_ref, up_got), (down_ref, down_got))[which]
+            target = {"lat": lax.rem(lat + step, n_lat), "mp": 2 * x + core}
+            return remote(
+                source.at[target["lat"]],
+                landing.at[mine],
+                large_send.at[which, step],
+                large_receive.at[which, mine],
+                target,
+            )
+
+        for which, (source, landing) in enumerate(((up_ref, up_got), (down_ref, down_got))):
+            for step in range(1, n_lat):
+                to_owner(which, step).start()
+
+            @pl.when(owner)
+            def _():
+                pltpu.make_async_copy(
+                    source.at[lat], landing.at[mine], large_receive.at[which, mine]
+                ).start()
+
+            @pl.when(jnp.logical_not(owner))
+            def _():
+                to_owner(which, 0).start()
+
         sends = []
         for index, spot in enumerate(order):
             loads[index].wait()
@@ -166,12 +218,31 @@
             swap.wait_send()
         for copy in sends:
             copy.wait()
+        for which, (source, landing) in enumerate(((up_ref, up_got), (down_ref, down_got))):
+            for step in range(n_lat):
+                remote(
+                    source.at[step],
+                    landing.at[step],
+                    large_send.at[which, step],
+                    large_receive.at[which, step],
+                    sibling,
+                ).wait_recv()
+            for step in range(1, n_lat):
+                to_owner(which, step).wait_send()
+
+            @pl.when(jnp.logical_not(owner))
+            def _():
+                to_owner(which, 0).wait_send()
 
     return pl.pallas_call(
         body,
-        out_shape=jax.ShapeDtypeStruct((count, rows, width), BF16),
-        in_specs=[pl.BlockSpec(memory_space=pl.ANY)],
-        out_specs=pl.BlockSpec(memory_space=pl.ANY),
+        out_shape=[
+            jax.ShapeDtypeStruct((count, rows, width), BF16),
+            jax.ShapeDtypeStruct(up_grads.shape, BF16),
+            jax.ShapeDtypeStruct(down_grads.shape, BF16),
+        ],
+        in_specs=[pl.BlockSpec(memory_space=pl.ANY)] * 3,
+        out_specs=[pl.BlockSpec(memory_space=pl.ANY)] * 3,
         scratch_shapes=[
             pltpu.VMEM((count, rows, width), BF16),
             pltpu.VMEM((count, rows, width), BF16),
@@ -179,11 +250,13 @@
             pltpu.SemaphoreType.DMA((2 * count,)),
             pltpu.SemaphoreType.DMA((2 * count,)),
             pltpu.SemaphoreType.DMA((count + 1,)),
+            pltpu.SemaphoreType.DMA((2, n_lat)),
+            pltpu.SemaphoreType.DMA((2, n_lat)),
         ],
         compiler_params=pltpu.CompilerParams(
             collective_id=collective, has_side_effects=True, vmem_limit_bytes=48 * 1024 * 1024
         ),
-    )(terms)
+    )(terms, up_grads, down_grads)
 
 
 def gradients_out(collective, weight_grads, slabs):
@@ -319,32 +392,116 @@
     return jnp.concatenate([values[..., :half, :], values[..., half:, :]], axis=-1)
 
 
-def groups_joined(slabs):
-    count, half, _ = slabs.shape
-    view = slabs.reshape(count, half, 2, HDIM).transpose(2, 1, 0, 3)
-    return view.reshape(2 * half, count * HDIM)
-
-
-def to_windows(grid):
-    row_count, lon_count = (grid.shape[0], grid.shape[1])
-    trailing = grid.shape[2:]
-    view = grid.reshape((row_count // WIN_H, WIN_H, lon_count // WIN_W, WIN_W) + trailing)
-    view = jnp.swapaxes(view, 1, 2)
-    return view.reshape(((row_count // WIN_H) * (lon_count // WIN_W), WIN_H * WIN_W) + trailing)
-
-
-def from_windows(windows):
-    bands, columns, _, width = windows.shape
-    view = windows.reshape((bands, columns, WIN_H, WIN_W, width))
-    view = jnp.swapaxes(view, 1, 2)
-    return view.reshape((bands * WIN_H, columns * WIN_W, width))
-
-
-def merge_patches(grid, padded):
-    row_count, lon_count, features = grid.shape
-    view = grid.reshape(row_count // 2, 2, lon_count // 2, 2, features)
-    view = view.transpose(1, 3, 0, 2, 4).reshape(4, row_count * lon_count // 4, features)
-    return jnp.pad(view, ((0, 0), (0, padded - view.shape[1]), (0, 0)))
+def picked(places, values):
+    spots = lax.broadcasted_iota(jnp.int32, (places.shape[0], values.shape[0]), 1)
+    return dot_nn(jnp.where(spots == places, 1.0, 0.0).astype(BF16), values)
+
+
+def spread_over(places, values, count):
+    spots = lax.broadcasted_iota(jnp.int32, (places.shape[0], count), 1)
+    return dot_tn(values, jnp.where(spots == places, 1.0, 0.0).astype(BF16))
+
+
+def swapped(values):
+    return jnp.concatenate([values[:, HDIM:], values[:, :HDIM]], axis=1)
+
+
+def join_slabs(slab_ref, out_ref, first_rows, second_rows):
+    half = slab_ref.shape[1]
+    low = lax.broadcasted_iota(jnp.int32, (half, 2 * HDIM), 1) < HDIM
+    for pair in range(slab_ref.shape[0] // 2):
+        lanes = slice(2 * HDIM * pair, 2 * HDIM * (pair + 1))
+        one = slab_ref[2 * pair].astype(F32)
+        two = slab_ref[2 * pair + 1].astype(F32)
+        first = jnp.where(low, one, swapped(two)).astype(out_ref.dtype)
+        second = jnp.where(low, swapped(one), two).astype(out_ref.dtype)
+        out_ref[first_rows : first_rows + half, lanes] = first
+        out_ref[second_rows : second_rows + half, lanes] = second
+
+
+PADDED_COLUMNS = 48
+FRAME, OWN, BACK, BACK_HALO, COT, UNPATCH, GRAD, GRAD_HALO, BY_ROW, BY_ROW_PATCH, SHIFT, STAY = range(12)
+
+
+def place_table(lat_offset, lon_offset, rows, block, padded, n_mp):
+    columns = block // WIN_W
+    size = max(rows * block, 4 * padded, n_mp * PADDED_COLUMNS)
+
+    def window_place(row, column):
+        window = (row // WIN_H) * columns + column // WIN_W
+        return window * WIN + (row % WIN_H) * WIN_W + column % WIN_W
+
+    token = np.arange(rows * block)
+    window, spot = token // WIN, token % WIN
+    row = (window // columns) * WIN_H + spot // WIN_W
+    column = (window % columns) * WIN_W + spot % WIN_W
+    patch, at = np.arange(4 * padded) // padded, np.arange(4 * padded) % padded
+    real = at < rows * block // 4
+    prow = np.where(real, 2 * (at // (block // 2)) + patch // 2, 0)
+    pcolumn = np.where(real, 2 * (at % (block // 2)) + patch % 2, 0)
+    side, spot = np.arange(WIN_H * PADDED_COLUMNS) // PADDED_COLUMNS, np.arange(WIN_H * PADDED_COLUMNS) % PADDED_COLUMNS
+    shown = spot < block
+    spot = np.where(shown, spot, 0)
+    group = np.arange(n_mp * PADDED_COLUMNS) // PADDED_COLUMNS
+    place = np.arange(n_mp * PADDED_COLUMNS) % PADDED_COLUMNS
+    inside = place < block
+    lon = group * block + place
+
+    def halo(down, right, row, column):
+        corner = row % WIN_H * WIN_W + column % WIN_W
+        slot = jnp.where(
+            down,
+            jnp.where(right, 0, 3 + column // WIN_W),
+            1 + row // WIN_H,
+        )
+        return jnp.where(jnp.logical_or(down, right), slot * WIN + corner, -1)
+
+    wide = block + WIN_W
+    back_row, back_column = prow - lat_offset, pcolumn - lon_offset
+    above, left = back_row < 0, back_column < 0
+    grad_row, grad_column = row + lat_offset, column + lon_offset
+    below, right = grad_row >= rows, grad_column >= block
+    table = {
+        FRAME: (row + lat_offset) * wide + column + lon_offset,
+        OWN: np.where(real, prow * wide + pcolumn, -1),
+        BACK: jnp.where(
+            jnp.logical_and(real, jnp.logical_not(jnp.logical_or(above, left))),
+            window_place(back_row, back_column),
+            -1,
+        ),
+        BACK_HALO: jnp.where(
+            real,
+            halo(
+                above,
+                left,
+                jnp.where(above, back_row + WIN_H, back_row),
+                jnp.where(left, back_column + WIN_W, back_column),
+            ),
+            -1,
+        ),
+        COT: np.where(real, prow * block + pcolumn, -1),
+        UNPATCH: (2 * (row % 2) + column % 2) * padded + (row // 2) * (block // 2) + column // 2,
+        GRAD: jnp.where(
+            jnp.logical_or(below, right), -1, window_place(grad_row, grad_column)
+        ),
+        GRAD_HALO: halo(
+            below,
+            right,
+            jnp.where(below, grad_row - rows, grad_row),
+            jnp.where(right, grad_column - block, grad_column),
+        ),
+        BY_ROW: np.where(shown, (spot // WIN_W) * WIN + side * WIN_W + spot % WIN_W, -1),
+        BY_ROW_PATCH: np.where(
+            shown, (spot % 2) * padded + side * (block // 2) + spot // 2, -1
+        ),
+        SHIFT: jnp.where(inside, (lon + lon_offset) % (n_mp * block), -1),
+        STAY: np.where(inside, lon, -1),
+    }
+    columns_list = [
+        jnp.pad(jnp.asarray(table[key], jnp.int32), (0, size - table[key].shape[0]))
+        for key in range(len(table))
+    ]
+    return jnp.stack(columns_list, axis=1)
 
 
 def norm_stats(values, count):
@@ -369,10 +526,8 @@
     for pair in range(upper.shape[1] // (2 * HDIM)):
         lanes = slice(2 * HDIM * pair, 2 * HDIM * (pair + 1))
         one, two = upper[:, lanes], lower[:, lanes]
-        swapped_one = jnp.concatenate([one[:, HDIM:], one[:, :HDIM]], axis=1)
-        swapped_two = jnp.concatenate([two[:, HDIM:], two[:, :HDIM]], axis=1)
-        out_ref[2 * pair, rows, :] = jnp.where(low, one, swapped_two).astype(BF16)
-        out_ref[2 * pair + 1, rows, :] = jnp.where(low, swapped_one, two).astype(BF16)
+        out_ref[2 * pair, rows, :] = jnp.where(low, one, swapped(two)).astype(BF16)
+        out_ref[2 * pair + 1, rows, :] = jnp.where(low, swapped(one), two).astype(BF16)
 
 
 WIN = WIN_H * WIN_W
@@ -419,7 +574,20 @@
     return [ref[rows, lanes] for ref in refs]
 
 
-def attention_forward(cut_ref, fields_ref, gain_ref, weights_ref, out_ref, context_ref, packed, held):
+def attention_forward(
+    cut_ref, body_ref, edge_ref, places_ref, gain_ref, weights_ref,
+    out_ref, context_ref, fields_ref, own_ref, packed, held, grid,
+):
+    half, rest = body_ref.shape[1], edge_ref.shape[1]
+    join_slabs(body_ref, grid, 0, half)
+    join_slabs(edge_ref, grid, 2 * half, 2 * half + rest)
+    tokens = fields_ref.shape[0]
+    whole = grid[...]
+    fields_ref[...] = picked(places_ref[:tokens, FRAME : FRAME + 1], whole).astype(BF16)
+    padded = own_ref.shape[1]
+    for patch in range(4):
+        rows = slice(padded * patch, padded * (patch + 1))
+        own_ref[patch] = picked(places_ref[rows, OWN : OWN + 1], whole).astype(BF16)
     framed_packed(fields_ref, gain_ref, weights_ref, packed)
     cut = cut_ref[0]
     windows = fields_ref.shape[0] // WIN
@@ -440,13 +608,17 @@
 
 
 def attention_backward(
-    cut_ref, fields_ref, gain_ref, weights_ref, context_ref, grad_ref, slab_ref, weight_ref,
-    packed, grads, held,
+    cut_ref, fields_ref, gain_ref, weights_ref, context_ref, grad_ref, halo_ref, places_ref,
+    slab_ref, weight_ref, packed, grads, held,
 ):
     framed, unit, scale_inv = framed_packed(fields_ref, gain_ref, weights_ref, packed)
     cut = cut_ref[0]
     windows = fields_ref.shape[0] // WIN
-    grad_framed = grad_ref[...]
+    tokens = fields_ref.shape[0]
+    grad_framed = (
+        picked(places_ref[:tokens, GRAD : GRAD + 1], grad_ref[...])
+        + picked(places_ref[:tokens, GRAD_HALO : GRAD_HALO + 1], halo_ref[...])
+    ).astype(BF16)
     held[...] = dot_nt(grad_framed, weights_ref[3]).astype(BF16).astype(F32)
 
     def step(window, carry):
@@ -477,7 +649,9 @@
     (back,) = norm_backward([grad_normed], [gain_ref[...]], [unit], scale_inv, unit.shape[1])
     result = grad_framed.astype(F32) + back
     half = result.shape[0] // 2
-    pair_slabs(result[:half], result[half:], slab_ref, 0)
+    by_row = places_ref[: slab_ref.shape[1], BY_ROW : BY_ROW + 1]
+    upper, lower = (picked(by_row, part.astype(BF16)) for part in (result[:half], result[half:]))
+    pair_slabs(upper, lower, slab_ref, 0)
 
 
 def section_loads(core_ref, own_ref, other_ref, weights, loaded):
@@ -492,14 +666,24 @@
 
 
 def merge_forward(
-    core_ref, fields_ref, attention_ref, cot_ref, gain_ref, mlp_gain_ref, own_ref, other_ref,
-    pair_ref, hidden_ref, merged_ref, grad_ref, weights, loaded,
+    core_ref, fields_ref, attention_ref, halo_ref, cot_got_ref, places_ref, gain_ref,
+    mlp_gain_ref, own_ref, other_ref,
+    pair_ref, hidden_ref, merged_ref, grad_ref, cot_ref, weights, loaded, joined,
 ):
     loads = section_loads(core_ref, own_ref, other_ref, weights, loaded)
     width_two = merged_ref.shape[1]
+    join_slabs(cot_got_ref, joined, 0, cot_got_ref.shape[1])
+    cot = joined[...].astype(BF16)
+    padded = merged_ref.shape[0]
     hidden = []
     for patch in range(4):
-        value = fields_ref[patch].astype(F32) + attention_ref[patch].astype(F32)
+        rows = slice(padded * patch, padded * (patch + 1))
+        cot_ref[patch] = picked(places_ref[rows, COT : COT + 1], cot).astype(BF16)
+        attention = picked(places_ref[rows, BACK : BACK + 1], attention_ref[...])
+        attention = attention + picked(
+            places_ref[rows, BACK_HALO : BACK_HALO + 1], halo_ref[...]
+        )
+        value = fields_ref[patch].astype(F32) + attention
         hidden_ref[patch] = value.astype(BF16)
         hidden.append(value.astype(BF16).astype(F32))
     center, scale_inv = norm_stats(hidden, 4 * hidden[0].shape[1])
@@ -521,12 +705,11 @@
 
 
 def merge_backward(
-    core_ref, parts_ref, merged_ref, grad_ref, hidden_ref, cot_ref, gain_ref, mlp_gain_ref,
-    own_ref, other_ref, slab_ref, out_ref, weights, loaded,
+    core_ref, parts_ref, merged_ref, grad_ref, hidden_ref, cot_ref, places_ref, gain_ref,
+    mlp_gain_ref, own_ref, other_ref, slab_ref, out_ref, weights, loaded,
 ):
     loads = section_loads(core_ref, own_ref, other_ref, weights, loaded)
     width_two = merged_ref.shape[1]
-    count = merged_ref.shape[0]
     total = parts_ref[0].astype(F32)
     for index in range(1, parts_ref.shape[0]):
         total = total + parts_ref[index].astype(F32)
@@ -538,8 +721,12 @@
         hidden_ref[patch].astype(F32) + dot_nt(bottom, weights[1, patch])
         for patch in range(4)
     ]
-    for side in range(2):
-        pair_slabs(decoded[side], decoded[2 + side], slab_ref, side * count)
+    by_row = places_ref[: slab_ref.shape[1], BY_ROW_PATCH : BY_ROW_PATCH + 1]
+    upper, lower = (
+        picked(by_row, jnp.concatenate([decoded[at], decoded[at + 1]], axis=0).astype(BF16))
+        for at in (0, 2)
+    )
+    pair_slabs(upper, lower, slab_ref, 0)
     center, scale_inv = norm_stats([merged], width_two)
     unit = (merged - center) * scale_inv
     (back,) = norm_backward(
@@ -556,8 +743,34 @@
         scale_inv,
         4 * hidden[0].shape[1],
     )
-    for patch in range(4):
-        out_ref[patch] = (cot_ref[patch].astype(F32) + backs[patch]).astype(BF16)
+    grads = [(cot_ref[patch].astype(F32) + backs[patch]) for patch in range(4)]
+    grads = jnp.concatenate(grads, axis=0).astype(BF16)
+    tokens = out_ref.shape[0]
+    out_ref[...] = picked(places_ref[:tokens, UNPATCH : UNPATCH + 1], grads).astype(BF16)
+
+
+def decoded_rows(got_ref, places_ref, out_ref):
+    places = places_ref[: got_ref.shape[0] * PADDED_COLUMNS, STAY : STAY + 1]
+    for side in range(WIN_H):
+        rows = slice(side * PADDED_COLUMNS, (side + 1) * PADDED_COLUMNS)
+        values = got_ref[:, rows, :].reshape(-1, 2 * HDIM)
+        both = spread_over(places, values, out_ref.shape[2])
+        for index in range(2):
+            out_ref[2 * side + index] = both[HDIM * index : HDIM * (index + 1)].astype(BF16)
+
+
+def input_rows(shift_ref, got_ref, edge_ref, places_ref, out_ref, framed):
+    places = places_ref[: got_ref.shape[0] * PADDED_COLUMNS, SHIFT : SHIFT + 1]
+    for side in range(WIN_H):
+        rows = slice(side * PADDED_COLUMNS, (side + 1) * PADDED_COLUMNS)
+        both = spread_over(places, got_ref[:, rows, :].reshape(-1, 2 * HDIM), out_ref.shape[2])
+        framed[WIN_H + side] = both[:HDIM]
+        framed[2 * WIN_H + side] = both[HDIM:]
+        both = spread_over(places, edge_ref[:, rows, :].reshape(-1, 2 * HDIM), out_ref.shape[2])
+        framed[side] = both[HDIM:]
+    first = WIN_H - shift_ref[0]
+    for row in range(out_ref.shape[0]):
+        out_ref[row] = framed[first + row]
 
 
 def shards(
@@ -617,6 +830,7 @@
     def own_rows(ref, here, target):
         return ref.at[:, rows_at(here, 0)]
 
+    places = place_table(lat_offset, lon_offset, rows, block, padded, n_mp)
     body_got, edge_got, weights_all, gains_all = exchange(
         1,
         [body_slab, edge_slab, weights, gains],
@@ -636,75 +850,52 @@
             for step in range(1, n_mp)
         ],
     )
-    body = groups_joined(body_got).reshape(rows, wide, width)
-    edge = groups_joined(edge_got).reshape(WIN_H, wide, width)
     has_shard = lax.rem(lax.axis_index("mp"), 2) == core
-    fetch = [
-        (at * n_mp + m, at * n_mp + (m ^ 1))
-        for at in range(n_lat)
-        for m in range(n_mp)
-        if at % 2 == m % 2
-    ]
-    up_late, down_late, gains_all = lax.optimization_barrier((up_weight, down_weight, gains_all))
-    up_shard, down_shard = (
-        jnp.where(has_shard, weight, lax.ppermute(weight, ("lat", "mp"), fetch))
-        for weight in (up_late, down_late)
-    )
-
     first_all = gains_all[:, 0, :group].reshape(1, width)
     merge_gain_all = gains_all[:, 1:5, :group].transpose(1, 0, 2).reshape(4, width)
     mlp_gain_row = mlp_gain.reshape(1, width_two)
-    own_fields = merge_patches(body[:, :block], padded)
-
-    def into_frame(whole):
-        part = lax.dynamic_slice(
-            whole, (lat_offset, lon_offset, jnp.int32(0)), (rows, block, width)
-        )
-        return to_windows(part).reshape(tokens, width)
-
-    framed_fields = into_frame(jnp.concatenate([body, edge], axis=0))
     cut = (jnp.int32(rows) * (n_lat - lat) - lat_offset).reshape(1)
-    attention_framed, context = local_kernel(
+    attention_framed, context, framed_fields, own_fields = local_kernel(
         attention_forward,
-        [cut, framed_fields, first_all, weights_all],
-        [((tokens, width), BF16), ((tokens, width), BF16)],
-        [pltpu.VMEM((3, tokens, width), F32), pltpu.VMEM((tokens, width), F32)],
+        [cut, body_got, edge_got, places, first_all, weights_all],
+        [((tokens, width), BF16)] * 3 + [((4, padded, width), BF16)],
+        [
+            pltpu.VMEM((3, tokens, width), F32),
+            pltpu.VMEM((tokens, width), F32),
+            pltpu.VMEM(((rows + WIN_H) * wide, width), BF16),
+        ],
         scalars=1,
     )
     window_shape = (bands, columns, WIN, width)
-    around = (bands + 1, columns + 1, WIN, width)
-    own_windows = attention_framed.reshape(window_shape)
-    halo, section_other, cot_got = exchange(
+    around = (2 * bands + 2, WIN, width)
+    halo, cot_got = exchange(
         2,
-        [own_windows, section_own, cot_slab],
-        [(around, BF16), (section_own.shape, BF16), (cot_slab.shape, BF16)],
-        [
-            (0, (bands - 1, columns - 1), 0, (0, 0), 1, 1),
-            (0, (slice(0, bands), columns - 1), 0, (slice(1, bands + 1), 0), 0, 1),
-            (0, (bands - 1,), 0, (0, slice(1, columns + 1)), 1, 0),
-            (1, None, 1, None, "sibling", 0),
+        [attention_framed.reshape(window_shape), cot_slab],
+        [(around, BF16), (cot_slab.shape, BF16)],
+        [
+            (0, (bands - 1, columns - 1), 0, (0,), 1, 1),
+            (0, (slice(0, bands), columns - 1), 0, (slice(1, 1 + bands),), 0, 1),
+            (0, (bands - 1,), 0, (slice(1 + bands, 1 + bands + columns),), 1, 0),
         ]
-        + [(2, "mp", 2, "mp", 0, step) for step in others],
-    )
-    cot_patches = merge_patches(groups_joined(cot_got).reshape(rows, block, width), padded)
-    halo = halo.at[1:, 1:].set(own_windows)
-    attention = lax.dynamic_slice(
-        from_windows(halo),
-        (WIN_H - lat_offset, WIN_W - lon_offset, jnp.int32(0)),
-        (rows, block, width),
+        + [(1, "mp", 1, "mp", 0, step) for step in others],
+    )
+    (section_other,) = exchange(
+        7, [section_own], [(section_own.shape, BF16)], [(0, None, 0, None, "sibling", 0)]
     )
     n_x = n_mp // 2
     section_scratch = [
         pltpu.VMEM((2,) + section_own.shape, BF16),
         pltpu.SemaphoreType.DMA((2,)),
     ]
-    pair, hidden, merged, grad_bottom = local_kernel(
+    pair, hidden, merged, grad_bottom, cot_patches = local_kernel(
         merge_forward,
         [
             core.reshape(1),
             own_fields,
-            merge_patches(attention, padded),
-            cot_patches,
+            attention_framed,
+            halo.reshape(-1, width),
+            cot_got,
+            places,
             merge_gain_all,
             mlp_gain_row,
             section_own,
@@ -715,8 +906,9 @@
             ((4, padded, width), BF16),
             ((padded, width_two), BF16),
             ((padded, width_two), F32),
-        ],
-        section_scratch,
+            ((4, padded, width), BF16),
+        ],
+        section_scratch + [pltpu.VMEM((tokens, width), F32)],
         scalars=1,
         outside=2,
     )
@@ -727,21 +919,29 @@
 
         return spot
 
-    (pairs,) = exchange(
+    pairs, up_other, down_other = exchange(
         3,
-        [pair],
-        [((n_x, 2) + pair.shape, BF16)],
+        [pair, up_weight, down_weight],
+        [
+            ((n_x, 2) + pair.shape, BF16),
+            (up_weight.shape, BF16),
+            (down_weight.shape, BF16),
+        ],
         [
             (0, None, 0, chip_spot(0), 0, 4),
             (0, None, 0, chip_spot(0), 0, 2),
             (0, None, 0, chip_spot(0), 0, -2),
             (0, None, 0, chip_spot(0), "sibling", 0),
             (0, None, 0, chip_spot(0), 0, 0),
+            (1, None, 1, None, "flip", 0),
+            (2, None, 2, None, "flip", 0),
             (0, chip_spot(-1), 0, chip_spot(-1), "sibling", 0, 1),
             (0, chip_spot(1), 0, chip_spot(1), "sibling", 0, 2),
             (0, chip_spot(-2), 0, chip_spot(-2), "sibling", 0, 0),
         ],
     )
+    up_shard = jnp.where(has_shard, up_weight, up_other)
+    down_shard = jnp.where(has_shard, down_weight, down_other)
     pairs = pairs.reshape(n_mp * padded, 2 * width_two)
     mlp_in, bottom_grad = pairs[:, :width_two], pairs[:, width_two:]
     hidden_up = jnp.dot(mlp_in, up_shard, preferred_element_type=F32)
@@ -756,38 +956,21 @@
         ],
         axis=1,
     ).astype(BF16)
-    parts = terms_back(4, terms.reshape(n_x, 2, padded, 2 * width_two))
-    shard_groups = [
-        [at * n_mp + 2 * x + z for at in range(core_at, n_lat, 2) for z in range(2)]
-        for x in range(n_x)
-        for core_at in range(2)
-    ]
-    owners = [
-        ((2 * spot + c) * n_mp + 2 * x + z, (2 * spot + z) * n_mp + 2 * x + c)
-        for spot in range(n_lat // 2)
-        for x in range(n_x)
-        for c in range(2)
-        for z in range(2)
-    ]
-    local_grads = [
-        jnp.einsum("ae,af->ef", mlp_in, grad_pre, preferred_element_type=F32),
-        jnp.einsum("ao,af->of", bottom_grad, activated, preferred_element_type=F32),
-    ]
-    grad_up, grad_down = (
-        lax.ppermute(
-            lax.psum_scatter(
-                part.astype(BF16),
-                ("lat", "mp"),
-                scatter_dimension=0,
-                axis_index_groups=shard_groups,
-                tiled=True,
-            ),
-            ("lat", "mp"),
-            owners,
-        ).astype(F32)
-        for part in local_grads
-    )
-    decoded_slab, grad_hidden = local_kernel(
+    large = (n_lat, width_two // n_lat, span)
+    parts, up_got, down_got = terms_back(
+        4,
+        terms.reshape(n_x, 2, padded, 2 * width_two),
+        jnp.einsum("ae,af->ef", mlp_in, grad_pre, preferred_element_type=F32)
+        .astype(BF16)
+        .reshape(large),
+        jnp.einsum("ao,af->of", bottom_grad, activated, preferred_element_type=F32)
+        .astype(BF16)
+        .reshape(large),
+    )
+    grad_up = jnp.sum(up_got.astype(F32), axis=0)
+    grad_down = jnp.sum(down_got.astype(F32), axis=0)
+    row_slab = (n_mp, WIN_H * PADDED_COLUMNS, 2 * group)
+    decoded_slab, grad_windows = local_kernel(
         merge_backward,
         [
             core.reshape(1),
@@ -796,37 +979,41 @@
             grad_bottom,
             hidden,
             cot_patches,
+            places,
             merge_gain_all,
             mlp_gain_row,
             section_own,
             section_other,
         ],
-        [((n_mp, 2 * padded, 2 * group), BF16), ((4, padded, width), BF16)],
+        [(row_slab, BF16), ((tokens, width), BF16)],
         section_scratch,
         scalars=1,
         outside=2,
     )
-    grad_windows = grad_hidden[:, :merged_count].reshape(
-        2, 2, bands, WIN_H // 2, columns, WIN_W // 2, width
-    )
-    grad_windows = grad_windows.transpose(2, 4, 3, 0, 5, 1, 6).reshape(window_shape)
     halo, decoded_got = exchange(
         5,
-        [grad_windows, decoded_slab],
+        [grad_windows.reshape(window_shape), decoded_slab],
         [(around, BF16), (decoded_slab.shape, BF16)],
         [
-            (0, (0, 0), 0, (bands, columns), -1, -1),
-            (0, (slice(0, bands), 0), 0, (slice(0, bands), columns), 0, -1),
-            (0, (0,), 0, (bands, slice(0, columns)), -1, 0),
+            (0, (0, 0), 0, (0,), -1, -1),
+            (0, (slice(0, bands), 0), 0, (slice(1, 1 + bands),), 0, -1),
+            (0, (0,), 0, (slice(1 + bands, 1 + bands + columns),), -1, 0),
         ]
         + [(1, "mp", 1, "mp", 0, step) for step in others],
     )
-    halo = halo.at[:bands, :columns].set(grad_windows)
-    grad_framed = into_frame(from_windows(halo))
     grad_slab, weight_grads = local_kernel(
         attention_backward,
-        [cut, framed_fields, first_all, weights_all, context, grad_framed],
-        [((n_mp, tokens // 2, 2 * group), BF16), ((4, width, width), BF16)],
+        [
+            cut,
+            framed_fields,
+            first_all,
+            weights_all,
+            context,
+            grad_windows,
+            halo.reshape(-1, width),
+            places,
+        ],
+        [(row_slab, BF16), ((4, width, width), BF16)],
         [
             pltpu.VMEM((3, tokens, width), F32),
             pltpu.VMEM((3, tokens, width), F32),
@@ -837,23 +1024,17 @@
     weight_total, grad_got, edge_got = gradients_out(6, weight_grads, grad_slab)
     grad_qkv = weight_total[:, : 3 * group].reshape(width // n_lat, 3, group)
     grad_proj = weight_total[:, 3 * group :]
-    decoded_view = decoded_got.reshape(n_mp, 2, padded, 2, group)[:, :, :merged_count]
-    decoded_view = decoded_view.reshape(n_mp, 2, rows // 2, block // 2, 2, group)
-    decoded = decoded_view.transpose(2, 4, 0, 3, 1, 5).reshape(rows, lon_count, group)
-
-    def columns_joined(slabs):
-        view = slabs.reshape(n_mp, columns, WIN_H, WIN_W, -1, group)
-        return view.transpose(4, 2, 0, 1, 3, 5).reshape(-1, lon_count, group)
-
-    grad_rows = jnp.concatenate(
-        [columns_joined(edge_got[..., group:]), columns_joined(grad_got)], axis=0
-    )
-    grad_rows = jnp.concatenate([grad_rows[:, -WIN_W:], grad_rows], axis=1)
-    grad_input = lax.dynamic_slice(
-        grad_rows,
-        (WIN_H - lat_offset, WIN_W - lon_offset, jnp.int32(0)),
-        (rows, lon_count, group),
-    ).astype(F32)
+    (decoded,) = local_kernel(
+        decoded_rows, [decoded_got, places], [((rows, group, lon_count), BF16)]
+    )
+    (grad_input,) = local_kernel(
+        input_rows,
+        [lat_shift, grad_got, edge_got, places],
+        [((rows, group, lon_count), F32)],
+        [pltpu.VMEM((rows + WIN_H, group, lon_count), F32)],
+        scalars=1,
+    )
+    decoded, grad_input = decoded.transpose(0, 2, 1), grad_input.transpose(0, 2, 1)
     return (decoded, grad_input, grad_qkv, grad_proj, grad_up, grad_down)
 
 

time: 390 us -> 311 us (0.80)
  local copies, waits for them, and re-layouts: 68.3 us -> 21.3 us
  waiting for transfers between devices: 51.9 us -> 16.6 us
  Pallas kernels: 204 us -> 236 us
  starting transfers between devices: 19.8 us -> 0.04 us
  matrix products: 16.3 us -> 10.3 us
    ppermute x4 -> x0, starting transfers between devices: 19.7 us -> none  [the longest x2 16.6 us: shards(): lax.ppermute(lax.psum_scatter(part.astype(BF16), ('lat', 'mp'), scatter_d...]
    reshape x20 -> x0, local copies, waits for them, and re-layouts: 18.4 us -> none  [the longest x6 6.88 us: merge_patches(): view.transpose(1, 3, 0, 2, 4)]
    ppermute x4 -> x0, waiting for transfers between devices: 17.8 us -> none  [the longest x2 17.8 us: shards(): lax.ppermute(weight, ('lat', 'mp'), fetch)]
    pallas_call x4 -> x5, Pallas kernels: 107 us -> 118 us  [exchange(): pl.pallas_call(body, out_shape=[jax.ShapeDtypeStruct(shape, dtype) for sh...]
    reduce_scatter x2 -> x0, waiting for transfers between devices: 10.7 us -> none  [shards(): lax.psum_scatter(part.astype(BF16), ('lat', 'mp'), scatter_dimension=0, a...]
    pallas_call x1, Pallas kernels: 25.5 us -> 35.2 us  [terms_back(): pl.pallas_call(body, out_shape=[jax.ShapeDtypeStruct((count, rows, width)...]
    transpose x10 -> x0, local copies, waits for them, and re-layouts: 9.35 us -> none  [the longest x3 3.49 us: groups_joined(): view = slabs.reshape(count, half, 2, HDIM).transpose(2, 1, 0, 3)]
    pallas_call x4 -> x6, Pallas kernels: 33.1 us -> 41 us  [local_kernel(): pl.pallas_call(body, out_shape=[jax.ShapeDtypeStruct(shape, dtype) for sh...]
  transfers between devices with their start and end apart: 7 -> 1, of which waited for: 3 -> 1; matrix products, arithmetic and copies ran while one was open for 20% -> 3% of each run, Pallas kernels for 53% -> 24%
where the time goes in v1:
time: 311 us; the launch traced here: 310 us
  Pallas kernels  236 us (76%)
  local copies, waits for them, and re-layouts  21.3 us (7%)
  waiting for transfers between devices  16.6 us (5%)
  between operations  16.1 us (5%)
  matrix products  10.3 us (3%)
  other arithmetic  9.98 us (3%)
    pallas_call x5, Pallas kernels, exchange(): pl.pallas_call(body, out_shape=[jax.ShapeDtypeStruct(shape, dtype) for sh...  118 us
    pallas_call x1, Pallas kernels, gradients_out(): pl.pallas_call(body, out_shape=[jax.ShapeDtypeStruct((share, kinds * grou...  41.5 us
    pallas_call x6, Pallas kernels, local_kernel(): pl.pallas_call(body, out_shape=[jax.ShapeDtypeStruct(shape, dtype) for sh...  41 us
    pallas_call x1, Pallas kernels, terms_back(): pl.pallas_call(body, out_shape=[jax.ShapeDtypeStruct((count, rows, width)...  35.2 us
    unnamed x103, local copies, waits for them, and re-layouts  16.9 us
    all_gather x1, waiting for transfers between devices, shards(): section_own = lax.all_gather(section, 'mp', axis=1, tiled=True)  16.6 us
  transfers between devices with their start and end apart: 1, of which 1 were waited for; matrix products, arithmetic and copies ran while one was open for 3% of the time, Pallas kernels for 24%

profile of v1, /device:TPU:1, one launch (start us, length us, event | category | flops | bytes accessed | tf_op | source)
XLA Modules:
  0.0 310.1 jit_solution(18070818779203953129)
XLA Ops:
  7.2 1.9 bitcast_select_fusion
  13.3 1.5 copy.55
  18.2 1.1 pad_maximum_fusion.1.refs_0_
  19.3 38.3 %shard_map.289 = (bf16[8,288,128]{2,1,0:T(8,128)(2,1)}, bf16[8,144,128]{2,1,0:T(8,128)(2,1)}, bf16[4,512,512]{2,1,0:T(8,128)(2,1)}, f32[8,8,128]{2,1,0:T(8,128)}) custom-call(bf16[8,288,128]{2,1,0:T(8,128)(2,1)} %pad_maximum_fusion.1.refs_0_, bf16[8,144,128]{2,1,0:T(8,128)(2,1)} %pad_maximum_fusion.3.refs_1_, bf16[4,64,512]{2,1,0:T(8,128)(2,1)} %pad_maximum_fusion.4.refs_2_, ...), custom_call_target="tpu_custom_call" | custom-call | tf_op jit(solution)/shard_map/pallas_call | solution.py:118
  59.3 1.6 copy-done
  60.9 1.1 copy-done.6
  62.0 1.0 copy-done.22
  62.9 8.4 %shard_map.290 = (bf16[432,512]{1,0:T(8,128)(2,1)S(1)}, bf16[432,512]{1,0:T(8,128)(2,1)S(1)}, bf16[432,512]{1,0:T(8,128)(2,1)S(1)}, bf16[4,112,512]{2,1,0:T(8,128)(2,1)S(1)}) custom-call(s32[1]{0:T(128)} %bitcast.2.cut_ref, bf16[8,288,128]{2,1,0:T(8,128)(2,1)S(1)} %copy-done.6, bf16[8,144,128]{2,1,0:T(8,128)(2,1)S(1)} %copy-done.22, ...), custom_call_target="tpu_custom_call" | custom-call | tf_op jit(solution)/shard_map/pallas_call | solution.py:368
  72.9 1.1 pad_maximum_fusion.2.refs_1_
  73.9 27.4 %shard_map.291 = (bf16[6,72,512]{2,1,0:T(8,128)(2,1)}, bf16[8,216,128]{2,1,0:T(8,128)(2,1)}) custom-call(bf16[2,3,72,512]{3,2,1,0:T(8,128)(2,1)} %bitcast.45, bf16[8,216,128]{2,1,0:T(8,128)(2,1)} %pad_maximum_fusion.2.refs_1_), custom_call_target="tpu_custom_call" | custom-call | tf_op jit(solution)/shard_map/pallas_call | solution.py:118
  101.3 16.6 %all-gather.2.cloned.1.call-done.refs_0_.own_ref = bf16[4,512,1024]{2,1,0:T(8,128)(2,1)} async-done(((bf16[4,64,1024]{2,1,0:T(8,128)(2,1)}), bf16[4,512,1024]{2,1,0:T(8,128)(2,1)}) %all-gather.2.cloned.1.call-update) | async-done | bytes 4194320 | tf_op jit(solution)/shard_map/all_gather | solution.py:808
  118.0 8.2 %shard_map.292.other_ref = bf16[4,512,1024]{2,1,0:T(8,128)(2,1)} custom-call(bf16[4,512,1024]{2,1,0:T(8,128)(2,1)} %all-gather.2.cloned.1.call-done.refs_0_.own_ref), custom_call_target="tpu_custom_call" | custom-call | tf_op jit(solution)/shard_map/pallas_call | solution.py:118
  126.2 5.0 %shard_map.293 = (bf16[112,2048]{1,0:T(8,128)(2,1)S(1)}, bf16[4,112,512]{2,1,0:T(8,128)(2,1)S(1)}, bf16[112,1024]{1,0:T(8,128)(2,1)S(1)}, f32[112,1024]{1,0:T(8,128)S(1)}, bf16[4,112,512]{2,1,0:T(8,128)(2,1)S(1)}) custom-call(s32[1]{0:T(128)} %bitcast.core_ref, bf16[4,112,512]{2,1,0:T(8,128)(2,1)S(1)} %get-tuple-element.40.fields_ref, ...), custom_call_target="tpu_custom_call" | custom-call | tf_op jit(solution)/shard_map/pallas_call | solution.py:368
  133.6 27.5 %shard_map.294 = (bf16[4,2,112,2048]{3,2,1,0:T(8,128)(2,1)}, bf16[1024,512]{1,0:T(8,128)(2,1)}, bf16[1024,512]{1,0:T(8,128)(2,1)}) custom-call(bf16[112,2048]{1,0:T(8,128)(2,1)} %copy-done.10, bf16[1024,512]{1,0:T(8,128)(2,1)} %refs_1_.1, bf16[1024,512]{1,0:T(8,128)(2,1)} %refs_2_.1), custom_call_target="tpu_custom_call" | custom-call | tf_op jit(solution)/shard_map/pallas_call | solution.py:118
  161.1 3.0 fusion.13
  164.6 2.1 fusion.6
  166.7 1.4 convolution_convert_fusion.1
  168.0 1.4 fusion.18
  169.5 1.3 fusion.15
  171.0 1.1 convolution_convert_fusion
  172.1 2.2 pad_maximum_fusion.terms_ref
  174.3 35.2 %shard_map.295 = (bf16[4,112,2048]{2,1,0:T(8,128)(2,1)S(1)}, bf16[16,64,512]{2,1,0:T(8,128)(2,1)S(1)}, bf16[16,64,512]{2,1,0:T(8,128)(2,1)S(1)}) custom-call(bf16[4,2,112,2048]{3,2,1,0:T(8,128)(2,1)} %pad_maximum_fusion.terms_ref, bf16[16,64,512]{2,1,0:T(8,128)(2,1)S(1)} %bitcast.48, bf16[16,64,512]{2,1,0:T(8,128)(2,1)S(1)} %bitcast.47), custom_call_target="tpu_custom_call" | custom-call | tf_op jit(solution)/shard_map/pallas_call | solution.py:237
  209.5 7.3 %shard_map.296 = (bf16[8,288,128]{2,1,0:T(8,128)(2,1)S(1)}, bf16[432,512]{1,0:T(8,128)(2,1)S(1)}) custom-call(s32[1]{0:T(128)} %bitcast.core_ref, bf16[4,112,2048]{2,1,0:T(8,128)(2,1)S(1)} %get-tuple-element.48.parts_ref, bf16[112,1024]{1,0:T(8,128)(2,1)S(1)} %get-tuple-element.49.merged_ref, f32[112,1024]{1,0:T(8,128)S(1)} %copy-done.12, ...), custom_call_target="tpu_custom_call" | custom-call | tf_op jit(solution)/shard_map/pallas_call | solution.py:368
  218.4 16.8 %shard_map.297 = (bf16[6,72,512]{2,1,0:T(8,128)(2,1)}, bf16[8,288,128]{2,1,0:T(8,128)(2,1)}) custom-call(bf16[2,3,72,512]{3,2,1,0:T(8,128)(2,1)} %bitcast.46, bf16[8,288,128]{2,1,0:T(8,128)(2,1)} %copy-done.5), custom_call_target="tpu_custom_call" | custom-call | tf_op jit(solution)/shard_map/pallas_call | solution.py:118
  235.2 1.1 copy-done.9
  236.3 1.5 shard_map.298
  237.7 1.0 copy-done.18
  238.7 1.0 copy-done.21
  239.8 16.7 %shard_map.299 = (bf16[8,288,128]{2,1,0:T(8,128)(2,1)S(1)}, bf16[4,512,512]{2,1,0:T(8,128)(2,1)S(1)}) custom-call(s32[1]{0:T(128)} %bitcast.2.cut_ref, bf16[432,512]{1,0:T(8,128)(2,1)S(1)} %copy-done.18, f32[1,512]{1,0:T(1,128)S(1)} %reshape_squeeze.3.gain_ref, bf16[4,512,512]{2,1,0:T(8,128)(2,1)} %get-tuple-element.39.weights_ref, ...), custom_call_target="tpu_custom_call" | custom-call | tf_op jit(solution)/shard_map/pallas_call | solution.py:368
  256.5 41.5 %shard_map.300 = (f32[32,256]{1,0:T(8,128)S(1)}, bf16[8,288,128]{2,1,0:T(8,128)(2,1)S(1)}, bf16[8,288,128]{2,1,0:T(8,128)(2,1)S(1)}) custom-call(bf16[4,512,512]{2,1,0:T(8,128)(2,1)S(1)} %get-tuple-element.59.weight_ref, bf16[8,288,128]{2,1,0:T(8,128)(2,1)S(1)} %get-tuple-element.60.slab_ref), custom_call_target="tpu_custom_call" | custom-call | tf_op jit(solution)/shard_map/pallas_call | solution.py:341
  300.1 1.0 convert_reduce_fusion
  301.1 2.2 shard_map.301
  (129 shorter events, 15.9 us)
Async XLA Ops:
  7.2 2.0 copy-start.28
  7.2 110.8 %all-gather.2.cloned.1.call-start = ((), (), s32[]{:S(2)}) async-start(), calls=%async_computation | async-start | bytes 4718592 | tf_op jit(solution)/shard_map/all_gather | solution.py:808
  10.3 1.6 copy-start.40
  10.3 1.6 copy-start.44
  10.4 1.6 copy-start.41
  10.4 1.6 copy-start.42
  10.4 1.7 copy-start.37
  10.4 1.7 copy-start.38
  10.4 1.7 copy-start.43
  10.4 1.7 copy-start.31
  10.4 1.7 copy-start.32
  10.4 1.7 copy-start.33
  10.5 1.7 copy-start.34
  10.5 1.7 copy-start.35
  10.5 1.7 copy-start.36
  15.2 2.0 copy-start.24
  59.3 1.6 copy-start
  101.3 24.9 %copy-start.2 = (bf16[432,512]{1,0:T(8,128)(2,1)S(1)}, bf16[432,512]{1,0:T(8,128)(2,1)}, u32[]{:S(2)}) copy-start(bf16[432,512]{1,0:T(8,128)(2,1)} %copy-done.1) | copy-start | bytes 1327108
  101.3 24.9 %copy-start.19 = (bf16[6,72,512]{2,1,0:T(8,128)(2,1)S(1)}, bf16[6,72,512]{2,1,0:T(8,128)(2,1)}, u32[]{:S(2)}) copy-start(bf16[6,72,512]{2,1,0:T(8,128)(2,1)} %get-tuple-element.42) | copy-start | bytes 1327108
  101.3 24.9 %copy-start.20 = (bf16[8,216,128]{2,1,0:T(8,128)(2,1)S(1)}, bf16[8,216,128]{2,1,0:T(8,128)(2,1)}, u32[]{:S(2)}) copy-start(bf16[8,216,128]{2,1,0:T(8,128)(2,1)} %get-tuple-element.43.cot_got_ref) | copy-start | bytes 1327108
  101.3 24.9 %copy-start.23 = (f32[1024]{0:T(1024)S(1)}, f32[1024]{0:T(1024)}, u32[]{:S(2)}) copy-start(f32[1024]{0:T(1024)} %param.32) | copy-start | bytes 12292
  133.6 27.5 %copy-start.26 = (bf16[1024,512]{1,0:T(8,128)(2,1)S(1)}, bf16[1024,512]{1,0:T(8,128)(2,1)}, u32[]{:S(2)}) copy-start(bf16[1024,512]{1,0:T(8,128)(2,1)} %refs_1_.1) | copy-start | bytes 3145732
  161.1 3.1 copy-start.25
  161.1 3.2 %copy-start.46 = (bf16[4,2,112,2048]{3,2,1,0:T(8,128)(2,1)S(1)}, bf16[4,2,112,2048]{3,2,1,0:T(8,128)(2,1)}, u32[]{:S(2)}) copy-start(bf16[4,2,112,2048]{3,2,1,0:T(8,128)(2,1)} %get-tuple-element.45) | copy-start | bytes 11010052
  161.1 3.5 %copy-start.48 = (bf16[1024,512]{1,0:T(8,128)(2,1)S(1)}, bf16[1024,512]{1,0:T(8,128)(2,1)}, u32[]{:S(2)}) copy-start(bf16[1024,512]{1,0:T(8,128)(2,1)} %get-tuple-element.47) | copy-start | bytes 3145732
  169.4 1.3 copy-start.27
  169.4 1.5 copy-start.47
  174.3 35.2 %copy-start.12 = (f32[112,1024]{1,0:T(8,128)S(1)}, f32[112,1024]{1,0:T(8,128)}, u32[]{:S(2)}) copy-start(f32[112,1024]{1,0:T(8,128)} %copy-done.11) | copy-start | bytes 1376260
  174.3 35.2 %copy-start.14 = (bf16[4,112,512]{2,1,0:T(8,128)(2,1)S(1)}, bf16[4,112,512]{2,1,0:T(8,128)(2,1)}, u32[]{:S(2)}) copy-start(bf16[4,112,512]{2,1,0:T(8,128)(2,1)} %copy-done.13) | copy-start | bytes 1376260
  218.4 19.3 %copy-start.16 = (bf16[432,512]{1,0:T(8,128)(2,1)S(1)}, bf16[432,512]{1,0:T(8,128)(2,1)}, u32[]{:S(2)}) copy-start(bf16[432,512]{1,0:T(8,128)(2,1)} %copy-done.15) | copy-start | bytes 1327108
  218.4 19.3 %copy-start.4 = (bf16[432,512]{1,0:T(8,128)(2,1)S(1)}, bf16[432,512]{1,0:T(8,128)(2,1)}, u32[]{:S(2)}) copy-start(bf16[432,512]{1,0:T(8,128)(2,1)} %copy-done.3) | copy-start | bytes 1327108
  299.5 1.6 copy-start.8
  (18 other events, 16.4 us)
Sparse Core Ops, SparseCore 0:
  10.9 106.9 all-gather.1

commit v2 on v1

--- a/solution.py
+++ b/solution.py
@@ -23,6 +23,7 @@
         "core": lax.rem(lat, 2),
         "x": lax.div(mp, 2),
         "z": lax.rem(mp, 2),
+        "quarter": 2 * lax.rem(lax.div(lat, 4), 2) + lax.rem(lat, 2),
     }
 
 
@@ -45,12 +46,64 @@
     }
 
 
-def greet(here, steps):
+def greet(here, steps, owned=False):
     barrier = pltpu.get_barrier_semaphore()
+    count = len(steps)
+    if owned:
+        n_lat, x, z = lax.axis_size("lat"), here["x"], here["z"]
+        owner = z == here["core"]
+        mine = 2 * lax.div(here["lat"], 2) + z
+        count = count + n_lat - jnp.where(owner, 1, 0)
+        for source in range(n_lat):
+
+            @pl.when(jnp.logical_or(jnp.logical_not(owner), mine != source))
+            def _():
+                target = {"lat": 2 * (source // 2) + z, "mp": 2 * x + source % 2}
+                pl.semaphore_signal(barrier, inc=1, **device_of(target))
+
     for down, right in steps:
         source = reached(here, down if isinstance(down, str) else -down, -right)
         pl.semaphore_signal(barrier, inc=1, **device_of(source))
-    pl.semaphore_wait(barrier, len(steps))
+    pl.semaphore_wait(barrier, count)
+
+
+def to_owners(here, source, landing, send, receive):
+    n_lat = lax.axis_size("lat")
+    lat, core, x, z = here["lat"], here["core"], here["x"], here["z"]
+    mine = 2 * lax.div(lat, 2) + z
+    owner = z == core
+
+    def copy_at(step):
+        target = {"lat": lax.rem(lat + step, n_lat), "mp": 2 * x + core}
+        rows = target["lat"]
+        return remote(source.at[rows], landing.at[mine], send.at[step], receive.at[mine], target)
+
+    def start():
+        for step in range(1, n_lat):
+            copy_at(step).start()
+
+        @pl.when(owner)
+        def _():
+            pltpu.make_async_copy(source.at[lat], landing.at[mine], receive.at[mine]).start()
+
+        @pl.when(jnp.logical_not(owner))
+        def _():
+            copy_at(0).start()
+
+    def wait():
+        sibling = reached(here, "sibling", 0)
+        for slot in range(n_lat):
+            remote(
+                source.at[slot], landing.at[slot], send.at[slot], receive.at[slot], sibling
+            ).wait_recv()
+        for step in range(1, n_lat):
+            copy_at(step).wait_send()
+
+        @pl.when(jnp.logical_not(owner))
+        def _():
+            copy_at(0).wait_send()
+
+    return start, wait
 
 
 def remote(source, landing, send, receive, target):
@@ -59,7 +112,8 @@
     )
 
 
-def exchange(collective, inputs, outputs, moves):
+def exchange(collective, inputs, outputs, moves, owned=()):
+    n_lat = lax.axis_size("lat")
     steps = []
     for move in moves:
         if move[4:6] != (0, 0) and move[4:6] not in steps:
@@ -68,7 +122,7 @@
     def body(*refs):
         sources = refs[: len(inputs)]
         landings = refs[len(inputs) : len(inputs) + len(outputs)]
-        send, receive = refs[-2:]
+        send, receive, owned_send, owned_receive = refs[-4:]
         here = positions()
 
         def part_of(ref, part, place, target):
@@ -80,9 +134,15 @@
                 return part(ref, here, target)
             return ref.at[part]
 
-        greet(here, steps)
+        greet(here, steps, bool(owned))
         copies = []
         arrived = set()
+        scatters = [
+            to_owners(
+                here, sources[one], landings[two], owned_send.at[index], owned_receive.at[index]
+            )
+            for index, (one, two) in enumerate(owned)
+        ]
         for index, move in enumerate(moves):
             source, source_part, landing, landing_part, down, right = move[:6]
             target = reached(here, down, right)
@@ -104,6 +164,10 @@
             else:
                 copy.start()
             copies.append(copy)
+        for start, _ in scatters:
+            start()
+        for _, wait in scatters:
+            wait()
         for index, copy in enumerate(copies):
             if moves[index][4:6] == (0, 0):
                 copy.wait()
@@ -123,6 +187,8 @@
         scratch_shapes=[
             pltpu.SemaphoreType.DMA((len(moves),)),
             pltpu.SemaphoreType.DMA((len(moves),)),
+            pltpu.SemaphoreType.DMA((max(len(owned), 1), n_lat)),
+            pltpu.SemaphoreType.DMA((max(len(owned), 1), n_lat)),
         ],
         compiler_params=pltpu.CompilerParams(collective_id=collective, has_side_effects=True),
     )(*inputs)
@@ -131,31 +197,19 @@
 X_STEPS = ((4, 2), (2, 1), (-2, 3))
 
 
-def terms_back(collective, terms, up_grads, down_grads):
+def terms_back(collective, terms, grads):
     count, _, rows, width = terms.shape
     n_lat = lax.axis_size("lat")
 
     def body(
-        terms_ref, up_ref, down_ref, parts_ref, up_got, down_got,
+        terms_ref, grads_ref, parts_ref, grads_got,
         other, own, total, send, receive, fetch, large_send, large_receive,
     ):
         here = positions()
-        lat, core, x, z = here["lat"], here["core"], here["x"], here["z"]
-        mine = 2 * lax.div(lat, 2) + z
-        owner = z == core
+        core, x = here["core"], here["x"]
         sibling = reached(here, "sibling", 0)
-        barrier = pltpu.get_barrier_semaphore()
-        greeted = [sibling] + [reached(here, 0, -right) for right, _ in X_STEPS]
-        for target in greeted:
-            pl.semaphore_signal(barrier, inc=1, **device_of(target))
-        for source in range(n_lat):
-
-            @pl.when(jnp.logical_or(jnp.logical_not(owner), mine != source))
-            def _():
-                target = {"lat": 2 * (source // 2) + z, "mp": 2 * x + source % 2}
-                pl.semaphore_signal(barrier, inc=1, **device_of(target))
-
-        pl.semaphore_wait(barrier, len(greeted) + n_lat - jnp.where(owner, 1, 0))
+        greet(here, [("sibling", 0)] + [(0, right) for right, _ in X_STEPS], True)
+        start, wait = to_owners(here, grads_ref, grads_got, large_send, large_receive)
         order = [lax.rem(x + step, count) for _, step in X_STEPS] + [x]
         swaps, loads = [], []
         for index, spot in enumerate(order):
@@ -171,32 +225,7 @@
             load.start()
             swaps.append(swap)
             loads.append(load)
-
-        def to_owner(which, step):
-            source, landing = ((up_ref, up_got), (down_ref, down_got))[which]
-            target = {"lat": lax.rem(lat + step, n_lat), "mp": 2 * x + core}
-            return remote(
-                source.at[target["lat"]],
-                landing.at[mine],
-                large_send.at[which, step],
-                large_receive.at[which, mine],
-                target,
-            )
-
-        for which, (source, landing) in enumerate(((up_ref, up_got), (down_ref, down_got))):
-            for step in range(1, n_lat):
-                to_owner(which, step).start()
-
-            @pl.when(owner)
-            def _():
-                pltpu.make_async_copy(
-                    source.at[lat], landing.at[mine], large_receive.at[which, mine]
-                ).start()
-
-            @pl.when(jnp.logical_not(owner))
-            def _():
-                to_owner(which, 0).start()
-
+        start()
         sends = []
         for index, spot in enumerate(order):
             loads[index].wait()
@@ -218,31 +247,16 @@
             swap.wait_send()
         for copy in sends:
             copy.wait()
-        for which, (source, landing) in enumerate(((up_ref, up_got), (down_ref, down_got))):
-            for step in range(n_lat):
-                remote(
-                    source.at[step],
-                    landing.at[step],
-                    large_send.at[which, step],
-                    large_receive.at[which, step],
-                    sibling,
-                ).wait_recv()
-            for step in range(1, n_lat):
-                to_owner(which, step).wait_send()
-
-            @pl.when(jnp.logical_not(owner))
-            def _():
-                to_owner(which, 0).wait_send()
+        wait()
 
     return pl.pallas_call(
         body,
         out_shape=[
             jax.ShapeDtypeStruct((count, rows, width), BF16),
-            jax.ShapeDtypeStruct(up_grads.shape, BF16),
-            jax.ShapeDtypeStruct(down_grads.shape, BF16),
-        ],
-        in_specs=[pl.BlockSpec(memory_space=pl.ANY)] * 3,
-        out_specs=[pl.BlockSpec(memory_space=pl.ANY)] * 3,
+            jax.ShapeDtypeStruct(grads.shape, BF16),
+        ],
+        in_specs=[pl.BlockSpec(memory_space=pl.ANY)] * 2,
+        out_specs=[pl.BlockSpec(memory_space=pl.ANY)] * 2,
         scratch_shapes=[
             pltpu.VMEM((count, rows, width), BF16),
             pltpu.VMEM((count, rows, width), BF16),
@@ -250,22 +264,22 @@
             pltpu.SemaphoreType.DMA((2 * count,)),
             pltpu.SemaphoreType.DMA((2 * count,)),
             pltpu.SemaphoreType.DMA((count + 1,)),
-            pltpu.SemaphoreType.DMA((2, n_lat)),
-            pltpu.SemaphoreType.DMA((2, n_lat)),
+            pltpu.SemaphoreType.DMA((n_lat,)),
+            pltpu.SemaphoreType.DMA((n_lat,)),
         ],
         compiler_params=pltpu.CompilerParams(
             collective_id=collective, has_side_effects=True, vmem_limit_bytes=48 * 1024 * 1024
         ),
-    )(terms, up_grads, down_grads)
-
-
-def gradients_out(collective, weight_grads, slabs):
+    )(terms, grads)
+
+
+def gradients_out(collective, weight_grads, slabs, edges):
     n_lat, n_mp = lax.axis_size("lat"), lax.axis_size("mp")
     kinds, width, _ = weight_grads.shape
     pair, group, share = kinds // 2, width // n_mp, width // n_lat
 
     def body(
-        weight_ref, slab_ref, out_ref, got_ref, edge_ref,
+        weight_ref, slab_ref, edge_ref, out_ref, got_ref, edge_got,
         other, total, parts, turned, landed, send, receive,
     ):
         here = positions()
@@ -290,13 +304,6 @@
             return copy
 
         swap = sent(weight_ref.at[pl.ds(pair * (1 - core), pair)], other, sibling)
-        for step in range(1, n_mp):
-            target = reached(here, 0, step)
-            sent(slab_ref.at[target["mp"]], got_ref.at[mp], target)
-        for step in range(n_mp):
-            target = reached(here, 1, step)
-            sent(slab_ref.at[target["mp"]], edge_ref.at[mp], target)
-
         own_slab = pltpu.make_async_copy(slab_ref.at[mp], got_ref.at[mp], send.at[60])
         own_slab.start()
 
@@ -309,6 +316,12 @@
             target = reached(here, 0, step)
             rows = pl.ds(pl.multiple_of(group * target["mp"], group), group)
             scattered.append(sent(total.at[:, rows], parts.at[mp], target))
+        for step in range(1, n_mp):
+            target = reached(here, 0, step)
+            sent(slab_ref.at[target["mp"]], got_ref.at[mp], target)
+        for step in range(n_mp):
+            target = reached(here, 1, step)
+            sent(edge_ref.at[target["mp"]], edge_got.at[mp], target)
         gathered = total[:, pl.ds(pl.multiple_of(group * mp, group), group), :].astype(F32)
         for step in range(1, n_mp):
             scattered[step - 1].wait_recv()
@@ -343,9 +356,9 @@
         out_shape=[
             jax.ShapeDtypeStruct((share, kinds * group), F32),
             jax.ShapeDtypeStruct(slabs.shape, BF16),
-            jax.ShapeDtypeStruct(slabs.shape, BF16),
-        ],
-        in_specs=[vmem, any_space],
+            jax.ShapeDtypeStruct(edges.shape, BF16),
+        ],
+        in_specs=[vmem, any_space, any_space],
         out_specs=[vmem, any_space, any_space],
         scratch_shapes=[
             pltpu.VMEM((pair, width, width), BF16),
@@ -359,7 +372,7 @@
         compiler_params=pltpu.CompilerParams(
             collective_id=collective, has_side_effects=True, vmem_limit_bytes=48 * 1024 * 1024
         ),
-    )(weight_grads, slabs)
+    )(weight_grads, slabs, edges)
 
 
 def local_kernel(body, operands, outputs, scratch=(), scalars=0, outside=0):
@@ -609,7 +622,7 @@
 
 def attention_backward(
     cut_ref, fields_ref, gain_ref, weights_ref, context_ref, grad_ref, halo_ref, places_ref,
-    slab_ref, weight_ref, packed, grads, held,
+    slab_ref, edge_ref, weight_ref, packed, grads, held,
 ):
     framed, unit, scale_inv = framed_packed(fields_ref, gain_ref, weights_ref, packed)
     cut = cut_ref[0]
@@ -652,25 +665,28 @@
     by_row = places_ref[: slab_ref.shape[1], BY_ROW : BY_ROW + 1]
     upper, lower = (picked(by_row, part.astype(BF16)) for part in (result[:half], result[half:]))
     pair_slabs(upper, lower, slab_ref, 0)
-
-
-def section_loads(core_ref, own_ref, other_ref, weights, loaded):
-    core = core_ref[0]
-    loads = [
-        pltpu.make_async_copy(own_ref, weights.at[core], loaded.at[0]),
-        pltpu.make_async_copy(other_ref, weights.at[1 - core], loaded.at[1]),
-    ]
+    half = edge_ref.shape[1]
+    pair_slabs(lower[:half], lower[half:], edge_ref, 0)
+
+
+def section_loads(quarter_ref, own_ref, got_ref, weights, loaded):
+    quarter = quarter_ref[0]
+    loads = []
+    for step in range(4):
+        place = pl.ds(2 * lax.rem(quarter + step, 4), 2)
+        source = own_ref if step == 0 else got_ref.at[place]
+        loads.append(pltpu.make_async_copy(source, weights.at[place], loaded.at[step]))
     for load in loads:
         load.start()
     return loads
 
 
 def merge_forward(
-    core_ref, fields_ref, attention_ref, halo_ref, cot_got_ref, places_ref, gain_ref,
-    mlp_gain_ref, own_ref, other_ref,
+    quarter_ref, fields_ref, attention_ref, halo_ref, cot_got_ref, places_ref, gain_ref,
+    mlp_gain_ref, own_ref, got_ref,
     pair_ref, hidden_ref, merged_ref, grad_ref, cot_ref, weights, loaded, joined,
 ):
-    loads = section_loads(core_ref, own_ref, other_ref, weights, loaded)
+    loads = section_loads(quarter_ref, own_ref, got_ref, weights, loaded)
     width_two = merged_ref.shape[1]
     join_slabs(cot_got_ref, joined, 0, cot_got_ref.shape[1])
     cot = joined[...].astype(BF16)
@@ -693,8 +709,8 @@
         load.wait()
     for patch in range(4):
         normed = (hidden[patch] - center) * scale_inv * gain_ref[patch : patch + 1, :]
-        merged = merged + dot_nn(normed.astype(BF16), weights[0, patch])
-        grad = grad + dot_nn(cot_ref[patch], weights[1, patch])
+        merged = merged + dot_nn(normed.astype(BF16), weights[patch])
+        grad = grad + dot_nn(cot_ref[patch], weights[4 + patch])
     merged_ref[...] = merged.astype(BF16)
     merged = merged.astype(BF16).astype(F32)
     center, scale_inv = norm_stats([merged], width_two)
@@ -705,10 +721,10 @@
 
 
 def merge_backward(
-    core_ref, parts_ref, merged_ref, grad_ref, hidden_ref, cot_ref, places_ref, gain_ref,
-    mlp_gain_ref, own_ref, other_ref, slab_ref, out_ref, weights, loaded,
+    quarter_ref, parts_ref, merged_ref, grad_ref, hidden_ref, cot_ref, places_ref, gain_ref,
+    mlp_gain_ref, own_ref, got_ref, slab_ref, out_ref, weights, loaded,
 ):
-    loads = section_loads(core_ref, own_ref, other_ref, weights, loaded)
+    loads = section_loads(quarter_ref, own_ref, got_ref, weights, loaded)
     width_two = merged_ref.shape[1]
     total = parts_ref[0].astype(F32)
     for index in range(1, parts_ref.shape[0]):
@@ -718,7 +734,7 @@
     for load in loads:
         load.wait()
     decoded = [
-        hidden_ref[patch].astype(F32) + dot_nt(bottom, weights[1, patch])
+        hidden_ref[patch].astype(F32) + dot_nt(bottom, weights[4 + patch])
         for patch in range(4)
     ]
     by_row = places_ref[: slab_ref.shape[1], BY_ROW_PATCH : BY_ROW_PATCH + 1]
@@ -737,7 +753,7 @@
     center, scale_inv = norm_stats(hidden, 4 * hidden[0].shape[1])
     units = [(value - center) * scale_inv for value in hidden]
     backs = norm_backward(
-        [dot_nt(grad_merged, weights[0, patch]) for patch in range(4)],
+        [dot_nt(grad_merged, weights[patch]) for patch in range(4)],
         [gain_ref[patch : patch + 1, :] for patch in range(4)],
         units,
         scale_inv,
@@ -766,8 +782,11 @@
         both = spread_over(places, got_ref[:, rows, :].reshape(-1, 2 * HDIM), out_ref.shape[2])
         framed[WIN_H + side] = both[:HDIM]
         framed[2 * WIN_H + side] = both[HDIM:]
+    for side in range(WIN_H // 2):
+        rows = slice(side * PADDED_COLUMNS, (side + 1) * PADDED_COLUMNS)
         both = spread_over(places, edge_ref[:, rows, :].reshape(-1, 2 * HDIM), out_ref.shape[2])
-        framed[side] = both[HDIM:]
+        framed[side] = both[:HDIM]
+        framed[WIN_H // 2 + side] = both[HDIM:]
     first = WIN_H - shift_ref[0]
     for row in range(out_ref.shape[0]):
         out_ref[row] = framed[first + row]
@@ -804,8 +823,13 @@
     padded = -(-merged_count // 16) * 16
     others = range(n_mp)
 
-    section = jnp.where(core == 0, merge_weight, expand_weight.transpose(1, 2, 0))
+    expand_turned = expand_weight.transpose(1, 2, 0)
+    quarter = 2 * lax.rem(lax.div(lat, 4), 2) + core
+    section = merge_weight[:2]
+    for index, part in enumerate((merge_weight[2:], expand_turned[:2], expand_turned[2:])):
+        section = jnp.where(quarter == index + 1, part, section)
     section_own = lax.all_gather(section, "mp", axis=1, tiled=True)
+
     blocks = fields.reshape(rows, n_mp, block, group).transpose(1, 0, 2, 3)
     margin = jnp.roll(blocks[:, :, :WIN_W], -1, axis=0)
     field_blocks = jnp.concatenate([blocks, margin], axis=2)
@@ -868,29 +892,41 @@
     )
     window_shape = (bands, columns, WIN, width)
     around = (2 * bands + 2, WIN, width)
-    halo, cot_got = exchange(
+
+    def quarter_at(extra, half=None):
+        def place(ref, here, target):
+            at = 2 * lax.rem(here["quarter"] + extra, 4)
+            return ref.at[pl.ds(at, 2)] if half is None else ref.at[at + half]
+
+        return place
+
+    halo, cot_got, section_got = exchange(
         2,
-        [attention_framed.reshape(window_shape), cot_slab],
-        [(around, BF16), (cot_slab.shape, BF16)],
-        [
+        [attention_framed.reshape(window_shape), cot_slab, section_own],
+        [(around, BF16), (cot_slab.shape, BF16), ((8, width, width_two), BF16)],
+        [
+            (2, (0,), 2, quarter_at(0, 0), 4, 0),
+            (2, (1,), 2, quarter_at(0, 1), -4, 0),
             (0, (bands - 1, columns - 1), 0, (0,), 1, 1),
             (0, (slice(0, bands), columns - 1), 0, (slice(1, 1 + bands),), 0, 1),
             (0, (bands - 1,), 0, (slice(1 + bands, 1 + bands + columns),), 1, 0),
         ]
-        + [(1, "mp", 1, "mp", 0, step) for step in others],
-    )
-    (section_other,) = exchange(
-        7, [section_own], [(section_own.shape, BF16)], [(0, None, 0, None, "sibling", 0)]
+        + [(1, "mp", 1, "mp", 0, step) for step in others]
+        + [
+            (2, None, 2, quarter_at(0), "sibling", 0),
+            (2, quarter_at(2, 0), 2, quarter_at(2, 0), "sibling", 0, 0),
+            (2, quarter_at(2, 1), 2, quarter_at(2, 1), "sibling", 0, 1),
+        ],
     )
     n_x = n_mp // 2
     section_scratch = [
-        pltpu.VMEM((2,) + section_own.shape, BF16),
-        pltpu.SemaphoreType.DMA((2,)),
+        pltpu.VMEM(section_got.shape, BF16),
+        pltpu.SemaphoreType.DMA((4,)),
     ]
     pair, hidden, merged, grad_bottom, cot_patches = local_kernel(
         merge_forward,
         [
-            core.reshape(1),
+            quarter.reshape(1),
             own_fields,
             attention_framed,
             halo.reshape(-1, width),
@@ -899,7 +935,7 @@
             merge_gain_all,
             mlp_gain_row,
             section_own,
-            section_other,
+            section_got,
         ],
         [
             ((padded, 2 * width_two), BF16),
@@ -957,23 +993,19 @@
         axis=1,
     ).astype(BF16)
     large = (n_lat, width_two // n_lat, span)
-    parts, up_got, down_got = terms_back(
+    parts, up_got = terms_back(
         4,
         terms.reshape(n_x, 2, padded, 2 * width_two),
         jnp.einsum("ae,af->ef", mlp_in, grad_pre, preferred_element_type=F32)
         .astype(BF16)
         .reshape(large),
-        jnp.einsum("ao,af->of", bottom_grad, activated, preferred_element_type=F32)
-        .astype(BF16)
-        .reshape(large),
-    )
-    grad_up = jnp.sum(up_got.astype(F32), axis=0)
-    grad_down = jnp.sum(down_got.astype(F32), axis=0)
+    )
+    down_local = jnp.einsum("ao,af->of", bottom_grad, activated, preferred_element_type=F32)
     row_slab = (n_mp, WIN_H * PADDED_COLUMNS, 2 * group)
     decoded_slab, grad_windows = local_kernel(
         merge_backward,
         [
-            core.reshape(1),
+            quarter.reshape(1),
             parts,
             merged,
             grad_bottom,
@@ -983,25 +1015,32 @@
             merge_gain_all,
             mlp_gain_row,
             section_own,
-            section_other,
+            section_got,
         ],
         [(row_slab, BF16), ((tokens, width), BF16)],
         section_scratch,
         scalars=1,
         outside=2,
     )
-    halo, decoded_got = exchange(
+    halo, decoded_got, down_got = exchange(
         5,
-        [grad_windows.reshape(window_shape), decoded_slab],
-        [(around, BF16), (decoded_slab.shape, BF16)],
+        [
+            grad_windows.reshape(window_shape),
+            decoded_slab,
+            down_local.astype(BF16).reshape(large),
+        ],
+        [(around, BF16), (decoded_slab.shape, BF16), (large, BF16)],
         [
             (0, (0, 0), 0, (0,), -1, -1),
             (0, (slice(0, bands), 0), 0, (slice(1, 1 + bands),), 0, -1),
             (0, (0,), 0, (slice(1 + bands, 1 + bands + columns),), -1, 0),
         ]
         + [(1, "mp", 1, "mp", 0, step) for step in others],
-    )
-    grad_slab, weight_grads = local_kernel(
+        owned=((2, 2),),
+    )
+    grad_up = jnp.sum(up_got.astype(F32), axis=0)
+    grad_down = jnp.sum(down_got.astype(F32), axis=0)
+    grad_slab, grad_edge, weight_grads = local_kernel(
         attention_backward,
         [
             cut,
@@ -1013,7 +1052,11 @@
             halo.reshape(-1, width),
             places,
         ],
-        [(row_slab, BF16), ((4, width, width), BF16)],
+        [
+            (row_slab, BF16),
+            ((n_mp, WIN_H * PADDED_COLUMNS // 2, 2 * group), BF16),
+            ((4, width, width), BF16),
+        ],
         [
             pltpu.VMEM((3, tokens, width), F32),
             pltpu.VMEM((3, tokens, width), F32),
@@ -1021,7 +1064,7 @@
         ],
         scalars=1,
     )
-    weight_total, grad_got, edge_got = gradients_out(6, weight_grads, grad_slab)
+    weight_total, grad_got, edge_got = gradients_out(6, weight_grads, grad_slab, grad_edge)
     grad_qkv = weight_total[:, : 3 * group].reshape(width // n_lat, 3, group)
     grad_proj = weight_total[:, 3 * group :]
     (decoded,) = local_kernel(

time: 311 us -> 307 us (0.987); the launches traced: 310 us -> 303 us
  waiting for transfers between devices: 16.6 us -> 6.76 us
    pallas_call x5 -> x4, Pallas kernels: 118 us -> 130 us  [exchange(): pl.pallas_call(body, out_shape=[jax.ShapeDtypeStruct(shape, dtype) for sh...]
    all_gather x1, waiting for transfers between devices: 16.6 us -> 6.74 us  [shards(): section_own = lax.all_gather(section, 'mp', axis=1, tiled=True)]
    pallas_call x1, Pallas kernels: 35.2 us -> 27.9 us  [terms_back(): pl.pallas_call(body, out_shape=[jax.ShapeDtypeStruct((count, rows, width)...]
    pallas_call x1, Pallas kernels: 41.5 us -> 35.7 us  [gradients_out(): pl.pallas_call(body, out_shape=[jax.ShapeDtypeStruct((share, kinds * grou...]
    unnamed x103 -> x107, local copies, waits for them, and re-layouts: 16.9 us -> 18.5 us
  transfers between devices with their start and end apart: 1 -> 1, of which waited for: 1 -> 1; matrix products, arithmetic and copies ran while one was open for 3% -> 3% of each run, Pallas kernels for 24% -> 15%
where the time goes in v2:
time: 307 us; the launch traced here: 303 us
  Pallas kernels  235 us (77%)
  local copies, waits for them, and re-layouts  23 us (7%)
  between operations  16.1 us (5%)
  matrix products  11.4 us (4%)
  other arithmetic  9.93 us (3%)
  waiting for transfers between devices  6.76 us (2%)
    pallas_call x4, Pallas kernels, exchange(): pl.pallas_call(body, out_shape=[jax.ShapeDtypeStruct(shape, dtype) for sh...  130 us
    pallas_call x6, Pallas kernels, local_kernel(): pl.pallas_call(body, out_shape=[jax.ShapeDtypeStruct(shape, dtype) for sh...  41.4 us
    pallas_call x1, Pallas kernels, gradients_out(): pl.pallas_call(body, out_shape=[jax.ShapeDtypeStruct((share, kinds * grou...  35.7 us
    pallas_call x1, Pallas kernels, terms_back(): pl.pallas_call(body, out_shape=[jax.ShapeDtypeStruct((count, rows, width)...  27.9 us
    unnamed x107, local copies, waits for them, and re-layouts  18.5 us
    all_gather x1, waiting for transfers between devices, shards(): section_own = lax.all_gather(section, 'mp', axis=1, tiled=True)  6.74 us
  transfers between devices with their start and end apart: 1, of which 1 were waited for; matrix products, arithmetic and copies ran while one was open for 3% of the time, Pallas kernels for 15%

profile of v2, /device:TPU:1, one launch (start us, length us, event | category | flops | bytes accessed | tf_op | source)
XLA Modules:
  0.0 302.6 jit_solution(410801589436965485)
XLA Ops:
  7.2 2.0 fusion.23
  17.2 1.1 pad_maximum_fusion.1.refs_0_
  18.4 36.6 %shard_map.289 = (bf16[8,288,128]{2,1,0:T(8,128)(2,1)}, bf16[8,144,128]{2,1,0:T(8,128)(2,1)}, bf16[4,512,512]{2,1,0:T(8,128)(2,1)}, f32[8,8,128]{2,1,0:T(8,128)}) custom-call(bf16[8,288,128]{2,1,0:T(8,128)(2,1)} %pad_maximum_fusion.1.refs_0_, bf16[8,144,128]{2,1,0:T(8,128)(2,1)} %pad_maximum_fusion.3.refs_1_, bf16[4,64,512]{2,1,0:T(8,128)(2,1)} %pad_maximum_fusion.4.refs_2_, ...), custom_call_target="tpu_custom_call" | custom-call | tf_op jit(solution)/shard_map/pallas_call | solution.py:182
  56.6 1.8 copy-done.1
  58.4 1.1 copy-done.6
  59.5 1.0 copy-done.23
  60.5 8.4 %shard_map.290 = (bf16[432,512]{1,0:T(8,128)(2,1)S(1)}, bf16[432,512]{1,0:T(8,128)(2,1)S(1)}, bf16[432,512]{1,0:T(8,128)(2,1)S(1)}, bf16[4,112,512]{2,1,0:T(8,128)(2,1)S(1)}) custom-call(s32[1]{0:T(128)} %bitcast.2.cut_ref, bf16[8,288,128]{2,1,0:T(8,128)(2,1)S(1)} %copy-done.6, bf16[8,144,128]{2,1,0:T(8,128)(2,1)S(1)} %copy-done.23, ...), custom_call_target="tpu_custom_call" | custom-call | tf_op jit(solution)/shard_map/pallas_call | solution.py:381
  71.9 1.0 pad_maximum_fusion.2.refs_1_
  72.9 6.7 %all-gather.2.cloned.1.call-done.refs_2_.own_ref = bf16[2,512,1024]{2,1,0:T(8,128)(2,1)} async-done(((bf16[2,64,1024]{2,1,0:T(8,128)(2,1)}), bf16[2,512,1024]{2,1,0:T(8,128)(2,1)}) %all-gather.2.cloned.1.call-update) | async-done | bytes 2097168 | tf_op jit(solution)/shard_map/all_gather | solution.py:831
  79.7 34.1 %shard_map.291 = (bf16[6,72,512]{2,1,0:T(8,128)(2,1)}, bf16[8,216,128]{2,1,0:T(8,128)(2,1)}, bf16[8,512,1024]{2,1,0:T(8,128)(2,1)}) custom-call(bf16[2,3,72,512]{3,2,1,0:T(8,128)(2,1)} %bitcast.45, bf16[8,216,128]{2,1,0:T(8,128)(2,1)} %pad_maximum_fusion.2.refs_1_, bf16[2,512,1024]{2,1,0:T(8,128)(2,1)} %all-gather.2.cloned.1.call-done.refs_2_.own_ref), custom_call_target="tpu_custom_call" | custom-call | tf_op jit(solution)/shard_map/pallas_call | solution.py:182
  113.9 1.0 copy-done.15
  114.9 1.0 copy-done.21
  115.9 1.0 copy-done.22
  116.9 5.5 %shard_map.292 = (bf16[112,2048]{1,0:T(8,128)(2,1)S(1)}, bf16[4,112,512]{2,1,0:T(8,128)(2,1)S(1)}, bf16[112,1024]{1,0:T(8,128)(2,1)S(1)}, f32[112,1024]{1,0:T(8,128)S(1)}, bf16[4,112,512]{2,1,0:T(8,128)(2,1)S(1)}) custom-call(s32[1]{0:T(128)} %bitcast.quarter_ref, bf16[4,112,512]{2,1,0:T(8,128)(2,1)S(1)} %copy-done.15, bf16[432,512]{1,0:T(8,128)(2,1)S(1)} %copy-done.5, ...), custom_call_target="tpu_custom_call" | custom-call | tf_op jit(solution)/shard_map/pallas_call | solution.py:381
  124.8 28.8 %shard_map.293 = (bf16[4,2,112,2048]{3,2,1,0:T(8,128)(2,1)}, bf16[1024,512]{1,0:T(8,128)(2,1)}, bf16[1024,512]{1,0:T(8,128)(2,1)}) custom-call(bf16[112,2048]{1,0:T(8,128)(2,1)} %copy-done.9, bf16[1024,512]{1,0:T(8,128)(2,1)} %refs_1_.1, bf16[1024,512]{1,0:T(8,128)(2,1)} %refs_2_.1), custom_call_target="tpu_custom_call" | custom-call | tf_op jit(solution)/shard_map/pallas_call | solution.py:182
  153.7 3.0 %fusion.13 = f32[896,512]{1,0:T(8,128)S(1)} fusion(bf16[896,2048]{1,0:T(8,128)(2,1)} %bitcast.74, bf16[1024,512]{1,0:T(8,128)(2,1)S(1)} %copy-done.27, bf16[1024,512]{1,0:T(8,128)(2,1)} %get-tuple-element.49, pred[]{:T(512)S(6)} %eq.27), kind=kOutput, calls=%fused_computation.21 | convolution fusion | flops 940048384 | bytes 5767169 | tf_op jit(solution)/shard_map/dot_general | solution.py:983
  157.1 2.1 fusion.6
  159.2 1.4 convolution_convert_fusion.1
  160.6 2.4 fusion.18
  163.0 1.3 fusion.15
  164.3 1.2 convolution_convert_fusion
  165.5 2.2 pad_maximum_fusion.terms_ref
  167.7 27.9 %shard_map.294 = (bf16[4,112,2048]{2,1,0:T(8,128)(2,1)S(1)}, bf16[16,64,512]{2,1,0:T(8,128)(2,1)S(1)}) custom-call(bf16[4,2,112,2048]{3,2,1,0:T(8,128)(2,1)} %pad_maximum_fusion.terms_ref, bf16[16,64,512]{2,1,0:T(8,128)(2,1)S(1)} %bitcast.46), custom_call_target="tpu_custom_call" | custom-call | tf_op jit(solution)/shard_map/pallas_call | solution.py:252
  195.6 7.3 %shard_map.295 = (bf16[8,288,128]{2,1,0:T(8,128)(2,1)S(1)}, bf16[432,512]{1,0:T(8,128)(2,1)S(1)}) custom-call(s32[1]{0:T(128)} %bitcast.quarter_ref, bf16[4,112,2048]{2,1,0:T(8,128)(2,1)S(1)} %get-tuple-element.51.parts_ref, bf16[112,1024]{1,0:T(8,128)(2,1)S(1)} %get-tuple-element.52.merged_ref, f32[112,1024]{1,0:T(8,128)S(1)} %copy-done.11, ...), custom_call_target="tpu_custom_call" | custom-call | tf_op jit(solution)/shard_map/pallas_call | solution.py:381
  204.5 30.8 %shard_map.296 = (bf16[6,72,512]{2,1,0:T(8,128)(2,1)}, bf16[8,288,128]{2,1,0:T(8,128)(2,1)}, bf16[16,64,512]{2,1,0:T(8,128)(2,1)}) custom-call(bf16[2,3,72,512]{3,2,1,0:T(8,128)(2,1)} %bitcast.44, bf16[8,288,128]{2,1,0:T(8,128)(2,1)} %copy-done.7, bf16[16,64,512]{2,1,0:T(8,128)(2,1)} %bitcast.62), custom_call_target="tpu_custom_call" | custom-call | tf_op jit(solution)/shard_map/pallas_call | solution.py:182
  235.3 1.1 copy-done.8
  236.4 1.5 shard_map.297
  237.9 1.0 copy-done.20
  238.9 16.8 %shard_map.298 = (bf16[8,288,128]{2,1,0:T(8,128)(2,1)S(1)}, bf16[8,144,128]{2,1,0:T(8,128)(2,1)S(1)}, bf16[4,512,512]{2,1,0:T(8,128)(2,1)S(1)}) custom-call(s32[1]{0:T(128)} %bitcast.2.cut_ref, bf16[432,512]{1,0:T(8,128)(2,1)S(1)} %copy-done.19, f32[1,512]{1,0:T(1,128)S(1)} %reshape_squeeze.3.gain_ref, bf16[4,512,512]{2,1,0:T(8,128)(2,1)} %get-tuple-element.41.weights_ref, ...), custom_call_target="tpu_custom_call" | custom-call | tf_op jit(solution)/shard_map/pallas_call | solution.py:381
  255.7 35.7 %shard_map.299 = (f32[32,256]{1,0:T(8,128)S(1)}, bf16[8,288,128]{2,1,0:T(8,128)(2,1)S(1)}, bf16[8,144,128]{2,1,0:T(8,128)(2,1)S(1)}) custom-call(bf16[4,512,512]{2,1,0:T(8,128)(2,1)S(1)} %get-tuple-element.62.weight_ref, bf16[8,288,128]{2,1,0:T(8,128)(2,1)S(1)} %get-tuple-element.63.slab_ref, bf16[8,144,128]{2,1,0:T(8,128)(2,1)S(1)} %get-tuple-element.64.edge_ref), custom_call_target="tpu_custom_call" | custom-call | tf_op jit(solution)/shard_map/pallas_call | solution.py:354
  292.8 1.0 convert_reduce_fusion
  293.8 2.0 shard_map.300
  (132 shorter events, 16.8 us)
Async XLA Ops:
  7.2 2.1 copy-start.29
  7.2 72.5 %all-gather.2.cloned.1.call-start = ((), (), s32[]{:S(2)}) async-start(), calls=%async_computation | async-start | bytes 2359296 | tf_op jit(solution)/shard_map/all_gather | solution.py:831
  10.4 1.7 copy-start.42
  10.4 1.7 copy-start.46
  10.4 1.7 copy-start.43
  10.4 1.7 copy-start.44
  10.4 1.8 copy-start.39
  10.4 1.8 copy-start.40
  10.5 1.8 copy-start.45
  10.5 1.8 copy-start.33
  10.5 1.8 copy-start.34
  10.5 1.8 copy-start.35
  10.5 1.8 copy-start.36
  10.5 1.8 copy-start.37
  10.5 1.8 copy-start.38
  10.6 2.8 copy-start.30
  14.3 2.0 copy-start.25
  56.6 1.8 copy-start.1
  71.9 41.9 %copy-start.24 = (f32[1024]{0:T(1024)S(1)}, f32[1024]{0:T(1024)}, u32[]{:S(2)}) copy-start(f32[1024]{0:T(1024)} %param.32) | copy-start | bytes 12292
  72.9 40.9 %copy-start.5 = (bf16[432,512]{1,0:T(8,128)(2,1)S(1)}, bf16[432,512]{1,0:T(8,128)(2,1)}, u32[]{:S(2)}) copy-start(bf16[432,512]{1,0:T(8,128)(2,1)} %copy-done.4) | copy-start | bytes 1327108
  79.7 34.2 %copy-start = (bf16[2,512,1024]{2,1,0:T(8,128)(2,1)S(1)}, bf16[2,512,1024]{2,1,0:T(8,128)(2,1)}, u32[]{:S(2)}) copy-start(bf16[2,512,1024]{2,1,0:T(8,128)(2,1)} %all-gather.2.cloned.1.call-done.refs_2_.own_ref) | copy-start | bytes 6291460
  124.8 28.9 %copy-start.27 = (bf16[1024,512]{1,0:T(8,128)(2,1)S(1)}, bf16[1024,512]{1,0:T(8,128)(2,1)}, u32[]{:S(2)}) copy-start(bf16[1024,512]{1,0:T(8,128)(2,1)} %refs_1_.1) | copy-start | bytes 3145732
  153.6 3.1 %copy-start.26 = (bf16[1024,512]{1,0:T(8,128)(2,1)S(1)}, bf16[1024,512]{1,0:T(8,128)(2,1)}, u32[]{:S(2)}) copy-start(bf16[1024,512]{1,0:T(8,128)(2,1)} %refs_2_.1) | copy-start | bytes 3145732
  153.6 3.2 %copy-start.48 = (bf16[4,2,112,2048]{3,2,1,0:T(8,128)(2,1)S(1)}, bf16[4,2,112,2048]{3,2,1,0:T(8,128)(2,1)}, u32[]{:S(2)}) copy-start(bf16[4,2,112,2048]{3,2,1,0:T(8,128)(2,1)} %get-tuple-element.48) | copy-start | bytes 11010052
  153.6 3.5 %copy-start.50 = (bf16[1024,512]{1,0:T(8,128)(2,1)S(1)}, bf16[1024,512]{1,0:T(8,128)(2,1)}, u32[]{:S(2)}) copy-start(bf16[1024,512]{1,0:T(8,128)(2,1)} %get-tuple-element.50) | copy-start | bytes 3145732
  163.0 1.3 copy-start.49
  167.7 27.9 %copy-start.11 = (f32[112,1024]{1,0:T(8,128)S(1)}, f32[112,1024]{1,0:T(8,128)}, u32[]{:S(2)}) copy-start(f32[112,1024]{1,0:T(8,128)} %copy-done.10) | copy-start | bytes 1376260
  167.7 27.9 %copy-start.13 = (bf16[4,112,512]{2,1,0:T(8,128)(2,1)S(1)}, bf16[4,112,512]{2,1,0:T(8,128)(2,1)}, u32[]{:S(2)}) copy-start(bf16[4,112,512]{2,1,0:T(8,128)(2,1)} %copy-done.12) | copy-start | bytes 1376260
  204.5 33.3 %copy-start.17 = (bf16[432,512]{1,0:T(8,128)(2,1)S(1)}, bf16[432,512]{1,0:T(8,128)(2,1)}, u32[]{:S(2)}) copy-start(bf16[432,512]{1,0:T(8,128)(2,1)} %copy-done.16) | copy-start | bytes 1327108
  204.5 33.3 %copy-start.19 = (bf16[432,512]{1,0:T(8,128)(2,1)S(1)}, bf16[432,512]{1,0:T(8,128)(2,1)}, u32[]{:S(2)}) copy-start(bf16[432,512]{1,0:T(8,128)(2,1)} %copy-done.18) | copy-start | bytes 1327108
  204.5 33.3 %copy-start.3 = (bf16[432,512]{1,0:T(8,128)(2,1)S(1)}, bf16[432,512]{1,0:T(8,128)(2,1)}, u32[]{:S(2)}) copy-start(bf16[432,512]{1,0:T(8,128)(2,1)} %copy-done.2) | copy-start | bytes 1327108
  255.7 37.1 %copy-start.28 = (bf16[16,64,512]{2,1,0:T(8,128)(2,1)S(1)}, bf16[16,64,512]{2,1,0:T(8,128)(2,1)}, u32[]{:S(2)}) copy-start(bf16[16,64,512]{2,1,0:T(8,128)(2,1)} %get-tuple-element.69) | copy-start | bytes 3145732
  (20 other events, 18.0 us)
Sparse Core Ops, SparseCore 0:
  10.4 69.2 all-gather.1

commit v3 on v2

--- a/solution.py
+++ b/solution.py
@@ -147,8 +147,9 @@
             source, source_part, landing, landing_part, down, right = move[:6]
             target = reached(here, down, right)
             if len(move) > 6:
-                copies[move[6]].wait_recv()
-                arrived.add(move[6])
+                if move[6] not in arrived:
+                    copies[move[6]].wait_recv()
+                    arrived.add(move[6])
                 source_ref = part_of(landings[source], source_part, target, target)
             else:
                 source_ref = part_of(sources[source], source_part, target, target)
@@ -197,19 +198,22 @@
 X_STEPS = ((4, 2), (2, 1), (-2, 3))
 
 
-def terms_back(collective, terms, grads):
+def terms_back(collective, terms, up_grads, down_grads):
     count, _, rows, width = terms.shape
     n_lat = lax.axis_size("lat")
 
     def body(
-        terms_ref, grads_ref, parts_ref, grads_got,
+        terms_ref, up_ref, down_ref, parts_ref, up_got, down_got,
         other, own, total, send, receive, fetch, large_send, large_receive,
     ):
         here = positions()
         core, x = here["core"], here["x"]
         sibling = reached(here, "sibling", 0)
         greet(here, [("sibling", 0)] + [(0, right) for right, _ in X_STEPS], True)
-        start, wait = to_owners(here, grads_ref, grads_got, large_send, large_receive)
+        scatters = [
+            to_owners(here, source, landing, large_send.at[index], large_receive.at[index])
+            for index, (source, landing) in enumerate(((up_ref, up_got), (down_ref, down_got)))
+        ]
         order = [lax.rem(x + step, count) for _, step in X_STEPS] + [x]
         swaps, loads = [], []
         for index, spot in enumerate(order):
@@ -225,7 +229,8 @@
             load.start()
             swaps.append(swap)
             loads.append(load)
-        start()
+        for start, _ in scatters:
+            start()
         sends = []
         for index, spot in enumerate(order):
             loads[index].wait()
@@ -247,16 +252,18 @@
             swap.wait_send()
         for copy in sends:
             copy.wait()
-        wait()
+        for _, wait in scatters:
+            wait()
 
     return pl.pallas_call(
         body,
         out_shape=[
             jax.ShapeDtypeStruct((count, rows, width), BF16),
-            jax.ShapeDtypeStruct(grads.shape, BF16),
-        ],
-        in_specs=[pl.BlockSpec(memory_space=pl.ANY)] * 2,
-        out_specs=[pl.BlockSpec(memory_space=pl.ANY)] * 2,
+            jax.ShapeDtypeStruct(up_grads.shape, BF16),
+            jax.ShapeDtypeStruct(down_grads.shape, BF16),
+        ],
+        in_specs=[pl.BlockSpec(memory_space=pl.ANY)] * 3,
+        out_specs=[pl.BlockSpec(memory_space=pl.ANY)] * 3,
         scratch_shapes=[
             pltpu.VMEM((count, rows, width), BF16),
             pltpu.VMEM((count, rows, width), BF16),
@@ -264,13 +271,13 @@
             pltpu.SemaphoreType.DMA((2 * count,)),
             pltpu.SemaphoreType.DMA((2 * count,)),
             pltpu.SemaphoreType.DMA((count + 1,)),
-            pltpu.SemaphoreType.DMA((n_lat,)),
-            pltpu.SemaphoreType.DMA((n_lat,)),
+            pltpu.SemaphoreType.DMA((2, n_lat)),
+            pltpu.SemaphoreType.DMA((2, n_lat)),
         ],
         compiler_params=pltpu.CompilerParams(
             collective_id=collective, has_side_effects=True, vmem_limit_bytes=48 * 1024 * 1024
         ),
-    )(terms, grads)
+    )(terms, up_grads, down_grads)
 
 
 def gradients_out(collective, weight_grads, slabs, edges):
@@ -669,24 +676,27 @@
     pair_slabs(lower[:half], lower[half:], edge_ref, 0)
 
 
-def section_loads(quarter_ref, own_ref, got_ref, weights, loaded):
-    quarter = quarter_ref[0]
-    loads = []
-    for step in range(4):
-        place = pl.ds(2 * lax.rem(quarter + step, 4), 2)
-        source = own_ref if step == 0 else got_ref.at[place]
-        loads.append(pltpu.make_async_copy(source, weights.at[place], loaded.at[step]))
-    for load in loads:
-        load.start()
-    return loads
+def section_load(place_ref, own_ref, got_ref, weights, loaded):
+    whole = pltpu.make_async_copy(got_ref, weights, loaded.at[0])
+    whole.start()
+
+    def wait():
+        whole.wait()
+        count = own_ref.shape[1]
+        rows = pl.ds(pl.multiple_of(place_ref[0] * count, count), count)
+        own = pltpu.make_async_copy(own_ref, weights.at[:, rows], loaded.at[1])
+        own.start()
+        own.wait()
+
+    return wait
 
 
 def merge_forward(
-    quarter_ref, fields_ref, attention_ref, halo_ref, cot_got_ref, places_ref, gain_ref,
+    place_ref, fields_ref, attention_ref, halo_ref, cot_got_ref, places_ref, gain_ref,
     mlp_gain_ref, own_ref, got_ref,
     pair_ref, hidden_ref, merged_ref, grad_ref, cot_ref, weights, loaded, joined,
 ):
-    loads = section_loads(quarter_ref, own_ref, got_ref, weights, loaded)
+    wait = section_load(place_ref, own_ref, got_ref, weights, loaded)
     width_two = merged_ref.shape[1]
     join_slabs(cot_got_ref, joined, 0, cot_got_ref.shape[1])
     cot = joined[...].astype(BF16)
@@ -705,8 +715,7 @@
     center, scale_inv = norm_stats(hidden, 4 * hidden[0].shape[1])
     merged = jnp.zeros(merged_ref.shape, F32)
     grad = jnp.zeros(merged_ref.shape, F32)
-    for load in loads:
-        load.wait()
+    wait()
     for patch in range(4):
         normed = (hidden[patch] - center) * scale_inv * gain_ref[patch : patch + 1, :]
         merged = merged + dot_nn(normed.astype(BF16), weights[patch])
@@ -721,18 +730,17 @@
 
 
 def merge_backward(
-    quarter_ref, parts_ref, merged_ref, grad_ref, hidden_ref, cot_ref, places_ref, gain_ref,
+    place_ref, parts_ref, merged_ref, grad_ref, hidden_ref, cot_ref, places_ref, gain_ref,
     mlp_gain_ref, own_ref, got_ref, slab_ref, out_ref, weights, loaded,
 ):
-    loads = section_loads(quarter_ref, own_ref, got_ref, weights, loaded)
+    wait = section_load(place_ref, own_ref, got_ref, weights, loaded)
     width_two = merged_ref.shape[1]
     total = parts_ref[0].astype(F32)
     for index in range(1, parts_ref.shape[0]):
         total = total + parts_ref[index].astype(F32)
     merged = merged_ref[...].astype(F32)
     bottom = (merged + total[:, :width_two]).astype(BF16)
-    for load in loads:
-        load.wait()
+    wait()
     decoded = [
         hidden_ref[patch].astype(F32) + dot_nt(bottom, weights[4 + patch])
         for patch in range(4)
@@ -823,12 +831,7 @@
     padded = -(-merged_count // 16) * 16
     others = range(n_mp)
 
-    expand_turned = expand_weight.transpose(1, 2, 0)
-    quarter = 2 * lax.rem(lax.div(lat, 4), 2) + core
-    section = merge_weight[:2]
-    for index, part in enumerate((merge_weight[2:], expand_turned[:2], expand_turned[2:])):
-        section = jnp.where(quarter == index + 1, part, section)
-    section_own = lax.all_gather(section, "mp", axis=1, tiled=True)
+    section = jnp.concatenate([merge_weight, expand_weight.transpose(1, 2, 0)], axis=0)
 
     blocks = fields.reshape(rows, n_mp, block, group).transpose(1, 0, 2, 3)
     margin = jnp.roll(blocks[:, :, :WIN_W], -1, axis=0)
@@ -845,34 +848,62 @@
     def rows_at(here, step):
         return pl.ds(pl.multiple_of(lax.rem(here["mp"] + n_mp - step, n_mp) * group, group), group)
 
-    def core_half(ref, here, target):
-        return ref.at[pl.ds(2 * here["core"], 2)]
-
-    def core_half_rows(step):
-        return lambda ref, here, target: ref.at[pl.ds(2 * here["core"], 2), rows_at(here, step)]
-
     def own_rows(ref, here, target):
         return ref.at[:, rows_at(here, 0)]
 
+    def own_quarter(size):
+        return lambda ref, here, target: ref.at[pl.ds(size * here["quarter"], size)]
+
+    def quarter_rows(size, step, extra, half=None):
+        def part(ref, here, target):
+            first = size * lax.rem(here["quarter"] + extra, 4)
+            if half is None:
+                return ref.at[pl.ds(first, size), rows_at(here, step)]
+            if size > 1:
+                return ref.at[first + half, rows_at(here, step)]
+            count = group // 2
+            at = lax.rem(here["mp"] + n_mp - step, n_mp) * group + half * count
+            return ref.at[first, pl.ds(pl.multiple_of(at, count), count)]
+
+        return part
+
+    nearest_first = (2, 6, 1, 7, 4, 3, 5)
+    gather_moves = [
+        (source, own_quarter(size), source, quarter_rows(size, 0, 0), 0, step)
+        for source, size in ((0, 2), (1, 1))
+        for step in nearest_first
+    ]
+    relays, last_relays = [], []
+    for source, size, first in ((0, 2, 0), (1, 1, n_mp - 1)):
+        for index, step in enumerate(nearest_first):
+            after = first + index
+            for half, down in ((0, 4), (1, -4)):
+                part = quarter_rows(size, step, 0, half)
+                relays.append((source, part, source, part, down, 0, after))
+                part = quarter_rows(size, step, 2, half)
+                last_relays.append((source, part, source, part, "sibling", 0, len(relays) - 1))
+            part = quarter_rows(size, step, 0)
+            relays.append((source, part, source, part, "sibling", 0, after))
     places = place_table(lat_offset, lon_offset, rows, block, padded, n_mp)
-    body_got, edge_got, weights_all, gains_all = exchange(
+    moves = (
+        gather_moves
+        + [(4, None, 4, "mp", 0, step) for step in others]
+        + [(2, "mp", 2, "mp", 0, step) for step in others]
+        + [(3, "mp", 3, "mp", -1, step) for step in others]
+        + [(1, None, 1, own_rows, 0, 0)]
+    )
+    last_relays = [move[:6] + (move[6] + len(moves),) for move in last_relays]
+    section_got, weights_all, body_got, edge_got, gains_all = exchange(
         1,
-        [body_slab, edge_slab, weights, gains],
-        [
+        [section, weights, body_slab, edge_slab, gains],
+        [
+            ((8, width, width_two), BF16),
+            ((4, width, width), BF16),
             (body_slab.shape, BF16),
             (edge_slab.shape, BF16),
-            ((4, width, width), BF16),
             ((n_mp,) + gains.shape, F32),
         ],
-        [(2, core_half, 2, core_half_rows(0), 0, step) for step in range(1, n_mp)]
-        + [(3, None, 3, "mp", 0, step) for step in others]
-        + [(0, "mp", 0, "mp", 0, step) for step in others]
-        + [(1, "mp", 1, "mp", -1, step) for step in others]
-        + [(2, None, 2, own_rows, 0, 0)]
-        + [
-            (2, core_half_rows(step), 2, core_half_rows(step), "sibling", 0, step - 1)
-            for step in range(1, n_mp)
-        ],
+        moves + relays + last_relays,
     )
     has_shard = lax.rem(lax.axis_index("mp"), 2) == core
     first_all = gains_all[:, 0, :group].reshape(1, width)
@@ -893,40 +924,26 @@
     window_shape = (bands, columns, WIN, width)
     around = (2 * bands + 2, WIN, width)
 
-    def quarter_at(extra, half=None):
-        def place(ref, here, target):
-            at = 2 * lax.rem(here["quarter"] + extra, 4)
-            return ref.at[pl.ds(at, 2)] if half is None else ref.at[at + half]
-
-        return place
-
-    halo, cot_got, section_got = exchange(
+    halo, cot_got = exchange(
         2,
-        [attention_framed.reshape(window_shape), cot_slab, section_own],
-        [(around, BF16), (cot_slab.shape, BF16), ((8, width, width_two), BF16)],
-        [
-            (2, (0,), 2, quarter_at(0, 0), 4, 0),
-            (2, (1,), 2, quarter_at(0, 1), -4, 0),
+        [attention_framed.reshape(window_shape), cot_slab],
+        [(around, BF16), (cot_slab.shape, BF16)],
+        [
             (0, (bands - 1, columns - 1), 0, (0,), 1, 1),
             (0, (slice(0, bands), columns - 1), 0, (slice(1, 1 + bands),), 0, 1),
             (0, (bands - 1,), 0, (slice(1 + bands, 1 + bands + columns),), 1, 0),
         ]
-        + [(1, "mp", 1, "mp", 0, step) for step in others]
-        + [
-            (2, None, 2, quarter_at(0), "sibling", 0),
-            (2, quarter_at(2, 0), 2, quarter_at(2, 0), "sibling", 0, 0),
-            (2, quarter_at(2, 1), 2, quarter_at(2, 1), "sibling", 0, 1),
-        ],
+        + [(1, "mp", 1, "mp", 0, step) for step in others],
     )
     n_x = n_mp // 2
     section_scratch = [
         pltpu.VMEM(section_got.shape, BF16),
-        pltpu.SemaphoreType.DMA((4,)),
+        pltpu.SemaphoreType.DMA((2,)),
     ]
     pair, hidden, merged, grad_bottom, cot_patches = local_kernel(
         merge_forward,
         [
-            quarter.reshape(1),
+            lax.axis_index("mp").reshape(1),
             own_fields,
             attention_framed,
             halo.reshape(-1, width),
@@ -934,7 +951,7 @@
             places,
             merge_gain_all,
             mlp_gain_row,
-            section_own,
+            section,
             section_got,
         ],
         [
@@ -993,19 +1010,21 @@
         axis=1,
     ).astype(BF16)
     large = (n_lat, width_two // n_lat, span)
-    parts, up_got = terms_back(
+    parts, up_got, down_got = terms_back(
         4,
         terms.reshape(n_x, 2, padded, 2 * width_two),
         jnp.einsum("ae,af->ef", mlp_in, grad_pre, preferred_element_type=F32)
         .astype(BF16)
         .reshape(large),
-    )
-    down_local = jnp.einsum("ao,af->of", bottom_grad, activated, preferred_element_type=F32)
+        jnp.einsum("ao,af->of", bottom_grad, activated, preferred_element_type=F32)
+        .astype(BF16)
+        .reshape(large),
+    )
     row_slab = (n_mp, WIN_H * PADDED_COLUMNS, 2 * group)
     decoded_slab, grad_windows = local_kernel(
         merge_backward,
         [
-            quarter.reshape(1),
+            lax.axis_index("mp").reshape(1),
             parts,
             merged,
             grad_bottom,
@@ -1014,7 +1033,7 @@
             places,
             merge_gain_all,
             mlp_gain_row,
-            section_own,
+            section,
             section_got,
         ],
         [(row_slab, BF16), ((tokens, width), BF16)],
@@ -1022,21 +1041,16 @@
         scalars=1,
         outside=2,
     )
-    halo, decoded_got, down_got = exchange(
+    halo, decoded_got = exchange(
         5,
-        [
-            grad_windows.reshape(window_shape),
-            decoded_slab,
-            down_local.astype(BF16).reshape(large),
-        ],
-        [(around, BF16), (decoded_slab.shape, BF16), (large, BF16)],
+        [grad_windows.reshape(window_shape), decoded_slab],
+        [(around, BF16), (decoded_slab.shape, BF16)],
         [
             (0, (0, 0), 0, (0,), -1, -1),
             (0, (slice(0, bands), 0), 0, (slice(1, 1 + bands),), 0, -1),
             (0, (0,), 0, (slice(1 + bands, 1 + bands + columns),), -1, 0),
         ]
         + [(1, "mp", 1, "mp", 0, step) for step in others],
-        owned=((2, 2),),
     )
     grad_up = jnp.sum(up_got.astype(F32), axis=0)
     grad_down = jnp.sum(down_got.astype(F32), axis=0)

time: 307 us -> 284 us (0.925)
  between operations: 16.1 us -> 2.4 us
  waiting for transfers between devices: 6.76 us -> 0 us
    pallas_call x4, Pallas kernels: 130 us -> 123 us  [exchange(): pl.pallas_call(body, out_shape=[jax.ShapeDtypeStruct(shape, dtype) for sh...]
    all_gather x1 -> x0, waiting for transfers between devices: 6.74 us -> none  [shards(): section_own = lax.all_gather(section, 'mp', axis=1, tiled=True)]
    unnamed x107 -> x69, local copies, waits for them, and re-layouts: 18.5 us -> 16.5 us
  transfers between devices with their start and end apart: 1 -> 0, of which waited for: 1 -> 0; matrix products, arithmetic and copies ran while one was open for 3% -> 0% of each run, Pallas kernels for 15% -> 0%
where the time goes in v3:
time: 284 us; the launch traced here: 283 us
  Pallas kernels  235 us (83%)
  local copies, waits for them, and re-layouts  22.1 us (8%)
  other arithmetic  12.8 us (5%)
  matrix products  10.3 us (4%)
    pallas_call x4, Pallas kernels, exchange(): pl.pallas_call(body, out_shape=[jax.ShapeDtypeStruct(shape, dtype) for sh...  123 us
    pallas_call x6, Pallas kernels, local_kernel(): pl.pallas_call(body, out_shape=[jax.ShapeDtypeStruct(shape, dtype) for sh...  41.8 us
    pallas_call x1, Pallas kernels, gradients_out(): pl.pallas_call(body, out_shape=[jax.ShapeDtypeStruct((share, kinds * grou...  38.7 us
    pallas_call x1, Pallas kernels, terms_back(): pl.pallas_call(body, out_shape=[jax.ShapeDtypeStruct((count, rows, width)...  30.9 us
    unnamed x69, local copies, waits for them, and re-layouts  16.5 us

profile of v3, /device:TPU:1, one launch (start us, length us, event | category | flops | bytes accessed | tf_op | source)
XLA Modules:
  0.0 282.5 jit_solution(17957639143495407436)
XLA Ops:
  2.7 1.3 select_maximum_fusion.refs_4_
  5.5 1.5 stack.51
  7.1 1.7 pad_maximum_fusion.5.refs_1_
  8.8 1.5 copy.51
  12.2 1.1 pad_maximum_fusion.2.refs_2_
  14.3 1.0 pad_maximum_fusion.3.refs_1_
  15.4 1.1 pad_maximum_fusion.1.refs_0_.own_ref
  16.4 58.1 %shard_map.289 = (bf16[8,512,1024]{2,1,0:T(8,128)(2,1)}, bf16[4,512,512]{2,1,0:T(8,128)(2,1)}, bf16[8,288,128]{2,1,0:T(8,128)(2,1)}, bf16[8,144,128]{2,1,0:T(8,128)(2,1)}, f32[8,8,128]{2,1,0:T(8,128)}) custom-call(bf16[8,64,1024]{2,1,0:T(8,128)(2,1)} %pad_maximum_fusion.1.refs_0_.own_ref, bf16[4,64,512]{2,1,0:T(8,128)(2,1)} %pad_maximum_fusion.5.refs_1_, ...), custom_call_target="tpu_custom_call" | custom-call | tf_op jit(solution)/shard_map/pallas_call | solution.py:183
  76.9 1.6 copy-done.1
  78.5 1.1 copy-done.7
  80.5 8.4 %shard_map.290 = (bf16[432,512]{1,0:T(8,128)(2,1)S(1)}, bf16[432,512]{1,0:T(8,128)(2,1)S(1)}, bf16[432,512]{1,0:T(8,128)(2,1)S(1)}, bf16[4,112,512]{2,1,0:T(8,128)(2,1)S(1)}) custom-call(s32[1]{0:T(128)} %bitcast.2.cut_ref, bf16[8,288,128]{2,1,0:T(8,128)(2,1)S(1)} %copy-done.7, bf16[8,144,128]{2,1,0:T(8,128)(2,1)S(1)} %copy-done.15, ...), custom_call_target="tpu_custom_call" | custom-call | tf_op jit(solution)/shard_map/pallas_call | solution.py:388
  89.7 17.3 %shard_map.291 = (bf16[6,72,512]{2,1,0:T(8,128)(2,1)}, bf16[8,216,128]{2,1,0:T(8,128)(2,1)}) custom-call(bf16[2,3,72,512]{3,2,1,0:T(8,128)(2,1)} %bitcast.44, bf16[8,216,128]{2,1,0:T(8,128)(2,1)} %pad_maximum_fusion.3.refs_1_), custom_call_target="tpu_custom_call" | custom-call | tf_op jit(solution)/shard_map/pallas_call | solution.py:183
  108.0 1.0 copy-done.13
  109.0 1.0 copy-done.14
  111.4 6.0 %shard_map.292 = (bf16[112,2048]{1,0:T(8,128)(2,1)S(1)}, bf16[4,112,512]{2,1,0:T(8,128)(2,1)S(1)}, bf16[112,1024]{1,0:T(8,128)(2,1)S(1)}, f32[112,1024]{1,0:T(8,128)S(1)}, bf16[4,112,512]{2,1,0:T(8,128)(2,1)S(1)}) custom-call(s32[1]{0:T(128)} %bitcast.place_ref, bf16[4,112,512]{2,1,0:T(8,128)(2,1)S(1)} %get-tuple-element.42.fields_ref, ...), custom_call_target="tpu_custom_call" | custom-call | tf_op jit(solution)/shard_map/pallas_call | solution.py:388
  118.9 28.0 %shard_map.293 = (bf16[4,2,112,2048]{3,2,1,0:T(8,128)(2,1)}, bf16[1024,512]{1,0:T(8,128)(2,1)}, bf16[1024,512]{1,0:T(8,128)(2,1)}) custom-call(bf16[112,2048]{1,0:T(8,128)(2,1)} %copy-done.9, bf16[1024,512]{1,0:T(8,128)(2,1)} %refs_1_.1, bf16[1024,512]{1,0:T(8,128)(2,1)} %refs_2_.1), custom_call_target="tpu_custom_call" | custom-call | tf_op jit(solution)/shard_map/pallas_call | solution.py:183
  146.9 3.1 %fusion.13 = f32[896,512]{1,0:T(8,128)S(1)} fusion(bf16[896,2048]{1,0:T(8,128)(2,1)} %bitcast.74, bf16[1024,512]{1,0:T(8,128)(2,1)} %refs_1_.1, bf16[1024,512]{1,0:T(8,128)(2,1)} %get-tuple-element.49, pred[]{:T(512)S(6)} %eq.15), kind=kOutput, calls=%fused_computation.21 | convolution fusion | flops 940048384 | bytes 5767169 | tf_op jit(solution)/shard_map/dot_general | solution.py:1000
  150.4 2.1 fusion.6
  152.4 1.3 convolution_convert_fusion.1
  153.8 1.4 fusion.18
  155.2 1.3 fusion.15
  156.7 1.2 convolution_convert_fusion
  157.9 2.2 pad_maximum_fusion.terms_ref
  160.1 30.9 %shard_map.294 = (bf16[4,112,2048]{2,1,0:T(8,128)(2,1)S(1)}, bf16[16,64,512]{2,1,0:T(8,128)(2,1)S(1)}, bf16[16,64,512]{2,1,0:T(8,128)(2,1)S(1)}) custom-call(bf16[4,2,112,2048]{3,2,1,0:T(8,128)(2,1)} %pad_maximum_fusion.terms_ref, bf16[16,64,512]{2,1,0:T(8,128)(2,1)S(1)} %bitcast.47, bf16[16,64,512]{2,1,0:T(8,128)(2,1)S(1)} %bitcast.46), custom_call_target="tpu_custom_call" | custom-call | tf_op jit(solution)/shard_map/pallas_call | solution.py:258
  191.1 7.3 %shard_map.295 = (bf16[8,288,128]{2,1,0:T(8,128)(2,1)S(1)}, bf16[432,512]{1,0:T(8,128)(2,1)S(1)}) custom-call(s32[1]{0:T(128)} %bitcast.place_ref, bf16[4,112,2048]{2,1,0:T(8,128)(2,1)S(1)} %get-tuple-element.51.parts_ref, bf16[112,1024]{1,0:T(8,128)(2,1)S(1)} %copy-done.17, f32[112,1024]{1,0:T(8,128)S(1)} %get-tuple-element.53.grad_ref, ...), custom_call_target="tpu_custom_call" | custom-call | tf_op jit(solution)/shard_map/pallas_call | solution.py:388
  200.1 20.0 %shard_map.296 = (bf16[6,72,512]{2,1,0:T(8,128)(2,1)}, bf16[8,288,128]{2,1,0:T(8,128)(2,1)}) custom-call(bf16[2,3,72,512]{3,2,1,0:T(8,128)(2,1)} %bitcast.45, bf16[8,288,128]{2,1,0:T(8,128)(2,1)} %copy-done.6), custom_call_target="tpu_custom_call" | custom-call | tf_op jit(solution)/shard_map/pallas_call | solution.py:183
  220.1 1.1 copy-done.8
  221.2 1.5 shard_map.297
  222.7 1.0 copy-done.12
  223.7 16.8 %shard_map.298 = (bf16[8,288,128]{2,1,0:T(8,128)(2,1)S(1)}, bf16[8,144,128]{2,1,0:T(8,128)(2,1)S(1)}, bf16[4,512,512]{2,1,0:T(8,128)(2,1)S(1)}) custom-call(s32[1]{0:T(128)} %bitcast.2.cut_ref, bf16[432,512]{1,0:T(8,128)(2,1)S(1)} %copy-done.11, f32[1,512]{1,0:T(1,128)S(1)} %copy-done.21, bf16[4,512,512]{2,1,0:T(8,128)(2,1)} %get-tuple-element.41.weights_ref, ...), custom_call_target="tpu_custom_call" | custom-call | tf_op jit(solution)/shard_map/pallas_call | solution.py:388
  240.4 38.7 %shard_map.299 = (f32[32,256]{1,0:T(8,128)S(1)}, bf16[8,288,128]{2,1,0:T(8,128)(2,1)S(1)}, bf16[8,144,128]{2,1,0:T(8,128)(2,1)S(1)}) custom-call(bf16[4,512,512]{2,1,0:T(8,128)(2,1)S(1)} %get-tuple-element.62.weight_ref, bf16[8,288,128]{2,1,0:T(8,128)(2,1)S(1)} %get-tuple-element.63.slab_ref, bf16[8,144,128]{2,1,0:T(8,128)(2,1)S(1)} %get-tuple-element.64.edge_ref), custom_call_target="tpu_custom_call" | custom-call | tf_op jit(solution)/shard_map/pallas_call | solution.py:361
  279.9 2.0 shard_map.300
  (91 shorter events, 16.8 us)
Async XLA Ops:
  12.1 1.2 copy-start.26
  14.2 1.2 copy-start.27
  14.2 1.2 copy-start.28
  76.2 30.7 %copy-start.20 = (f32[1,512]{1,0:T(1,128)}, f32[1,512]{1,0:T(1,128)S(1)}, u32[]{:S(2)}) copy-start(f32[1,512]{1,0:T(1,128)S(1)} %reshape_squeeze.3.gain_ref) | copy-start | bytes 6148
  76.9 1.6 copy-start.1
  78.5 1.1 copy-start.7
  79.6 1.0 copy-start.15
  80.5 26.5 %copy-start = (bf16[8,64,1024]{2,1,0:T(8,128)(2,1)S(1)}, bf16[8,64,1024]{2,1,0:T(8,128)(2,1)}, u32[]{:S(2)}) copy-start(bf16[8,64,1024]{2,1,0:T(8,128)(2,1)} %pad_maximum_fusion.1.refs_0_.own_ref) | copy-start | bytes 3145732
  88.9 0.8 copy-start.2
  89.7 17.3 %copy-start.10 = (bf16[432,512]{1,0:T(8,128)(2,1)}, bf16[432,512]{1,0:T(8,128)(2,1)S(1)}, u32[]{:S(2)}) copy-start(bf16[432,512]{1,0:T(8,128)(2,1)S(1)} %get-tuple-element.59.fields_ref) | copy-start | bytes 1327108
  107.0 1.0 copy-start.3
  108.0 1.0 copy-start.13
  109.0 1.0 copy-start.14
  110.0 0.7 copy-start.18
  110.7 0.7 copy-start.22
  117.4 0.8 copy-start.9
  118.2 0.7 copy-start.16
  146.8 3.1 %copy-start.24 = (bf16[1024,512]{1,0:T(8,128)(2,1)S(1)}, bf16[1024,512]{1,0:T(8,128)(2,1)}, u32[]{:S(2)}) copy-start(bf16[1024,512]{1,0:T(8,128)(2,1)} %refs_2_.1) | copy-start | bytes 3145732
  146.9 3.2 %copy-start.29 = (bf16[4,2,112,2048]{3,2,1,0:T(8,128)(2,1)S(1)}, bf16[4,2,112,2048]{3,2,1,0:T(8,128)(2,1)}, u32[]{:S(2)}) copy-start(bf16[4,2,112,2048]{3,2,1,0:T(8,128)(2,1)} %get-tuple-element.48) | copy-start | bytes 11010052
  146.9 3.5 %copy-start.31 = (bf16[1024,512]{1,0:T(8,128)(2,1)S(1)}, bf16[1024,512]{1,0:T(8,128)(2,1)}, u32[]{:S(2)}) copy-start(bf16[1024,512]{1,0:T(8,128)(2,1)} %get-tuple-element.50) | copy-start | bytes 3145732
  155.2 1.3 copy-start.25
  155.2 1.5 copy-start.30
  160.1 31.0 %copy-start.17 = (bf16[112,1024]{1,0:T(8,128)(2,1)S(1)}, bf16[112,1024]{1,0:T(8,128)(2,1)}, u32[]{:S(2)}) copy-start(bf16[112,1024]{1,0:T(8,128)(2,1)} %copy-done.16) | copy-start | bytes 688132
  160.1 31.0 %copy-start.19 = (f32[4,512]{1,0:T(4,128)S(1)}, f32[4,512]{1,0:T(4,128)}, u32[]{:S(2)}) copy-start(f32[4,512]{1,0:T(4,128)} %reshape.78.gain_ref) | copy-start | bytes 24580
  160.1 31.0 %copy-start.23 = (f32[1024]{0:T(1024)S(1)}, f32[1024]{0:T(1024)}, u32[]{:S(2)}) copy-start(f32[1024]{0:T(1024)} %param.32) | copy-start | bytes 12292
  198.3 0.8 copy-start.4
  199.1 1.0 copy-start.6
  199.1 23.5 %copy-start.5 = (bf16[432,512]{1,0:T(8,128)(2,1)S(1)}, bf16[432,512]{1,0:T(8,128)(2,1)}, u32[]{:S(2)}) copy-start(bf16[432,512]{1,0:T(8,128)(2,1)} %copy-done.4) | copy-start | bytes 1327108
  199.1 23.5 %copy-start.11 = (bf16[432,512]{1,0:T(8,128)(2,1)S(1)}, bf16[432,512]{1,0:T(8,128)(2,1)}, u32[]{:S(2)}) copy-start(bf16[432,512]{1,0:T(8,128)(2,1)} %copy-done.10) | copy-start | bytes 1327108
  199.1 23.5 %copy-start.21 = (f32[1,512]{1,0:T(1,128)S(1)}, f32[1,512]{1,0:T(1,128)}, u32[]{:S(2)}) copy-start(f32[1,512]{1,0:T(1,128)} %copy-done.20) | copy-start | bytes 6148
  220.1 1.1 copy-start.8
  222.7 1.0 copy-start.12

commit v4 on v3

--- a/solution.py
+++ b/solution.py
@@ -13,6 +13,10 @@
 MASKED = -1e30
 BF16 = jnp.bfloat16
 F32 = jnp.float32
+
+
+def space_of(shape):
+    return pltpu.VMEM if int(np.prod(shape)) <= 2 * 1024 * 1024 else pl.ANY
 
 
 def positions():
@@ -184,14 +188,16 @@
         body,
         out_shape=[jax.ShapeDtypeStruct(shape, dtype) for shape, dtype in outputs],
         in_specs=[pl.BlockSpec(memory_space=pl.ANY)] * len(inputs),
-        out_specs=[pl.BlockSpec(memory_space=pl.ANY)] * len(outputs),
+        out_specs=[pl.BlockSpec(memory_space=space_of(shape)) for shape, _ in outputs],
         scratch_shapes=[
             pltpu.SemaphoreType.DMA((len(moves),)),
             pltpu.SemaphoreType.DMA((len(moves),)),
             pltpu.SemaphoreType.DMA((max(len(owned), 1), n_lat)),
             pltpu.SemaphoreType.DMA((max(len(owned), 1), n_lat)),
         ],
-        compiler_params=pltpu.CompilerParams(collective_id=collective, has_side_effects=True),
+        compiler_params=pltpu.CompilerParams(
+            collective_id=collective, has_side_effects=True, vmem_limit_bytes=32 * 1024 * 1024
+        ),
     )(*inputs)
 
 
@@ -263,7 +269,11 @@
             jax.ShapeDtypeStruct(down_grads.shape, BF16),
         ],
         in_specs=[pl.BlockSpec(memory_space=pl.ANY)] * 3,
-        out_specs=[pl.BlockSpec(memory_space=pl.ANY)] * 3,
+        out_specs=[
+            pl.BlockSpec(memory_space=pltpu.VMEM),
+            pl.BlockSpec(memory_space=pl.ANY),
+            pl.BlockSpec(memory_space=pl.ANY),
+        ],
         scratch_shapes=[
             pltpu.VMEM((count, rows, width), BF16),
             pltpu.VMEM((count, rows, width), BF16),
@@ -366,7 +376,7 @@
             jax.ShapeDtypeStruct(edges.shape, BF16),
         ],
         in_specs=[vmem, any_space, any_space],
-        out_specs=[vmem, any_space, any_space],
+        out_specs=[vmem, vmem, vmem],
         scratch_shapes=[
             pltpu.VMEM((pair, width, width), BF16),
             pltpu.VMEM((pair, width, width), BF16),
@@ -446,82 +456,71 @@
 def place_table(lat_offset, lon_offset, rows, block, padded, n_mp):
     columns = block // WIN_W
     size = max(rows * block, 4 * padded, n_mp * PADDED_COLUMNS)
-
-    def window_place(row, column):
-        window = (row // WIN_H) * columns + column // WIN_W
-        return window * WIN + (row % WIN_H) * WIN_W + column % WIN_W
-
     token = np.arange(rows * block)
     window, spot = token // WIN, token % WIN
     row = (window // columns) * WIN_H + spot // WIN_W
     column = (window % columns) * WIN_W + spot % WIN_W
     patch, at = np.arange(4 * padded) // padded, np.arange(4 * padded) % padded
     real = at < rows * block // 4
-    prow = np.where(real, 2 * (at // (block // 2)) + patch // 2, 0)
-    pcolumn = np.where(real, 2 * (at % (block // 2)) + patch % 2, 0)
-    side, spot = np.arange(WIN_H * PADDED_COLUMNS) // PADDED_COLUMNS, np.arange(WIN_H * PADDED_COLUMNS) % PADDED_COLUMNS
+    prow = 2 * (at // (block // 2)) + patch // 2
+    pcolumn = 2 * (at % (block // 2)) + patch % 2
+    side = np.arange(WIN_H * PADDED_COLUMNS) // PADDED_COLUMNS
+    spot = np.arange(WIN_H * PADDED_COLUMNS) % PADDED_COLUMNS
     shown = spot < block
-    spot = np.where(shown, spot, 0)
     group = np.arange(n_mp * PADDED_COLUMNS) // PADDED_COLUMNS
     place = np.arange(n_mp * PADDED_COLUMNS) % PADDED_COLUMNS
     inside = place < block
+    unpatch = (2 * (row % 2) + column % 2) * padded + (row // 2) * (block // 2) + column // 2
+    by_row = (spot // WIN_W) * WIN + side * WIN_W + spot % WIN_W
+    by_row_patch = (spot % 2) * padded + side * (block // 2) + spot // 2
     lon = group * block + place
-
-    def halo(down, right, row, column):
-        corner = row % WIN_H * WIN_W + column % WIN_W
-        slot = jnp.where(
-            down,
-            jnp.where(right, 0, 3 + column // WIN_W),
-            1 + row // WIN_H,
-        )
-        return jnp.where(jnp.logical_or(down, right), slot * WIN + corner, -1)
-
     wide = block + WIN_W
-    back_row, back_column = prow - lat_offset, pcolumn - lon_offset
-    above, left = back_row < 0, back_column < 0
-    grad_row, grad_column = row + lat_offset, column + lon_offset
-    below, right = grad_row >= rows, grad_column >= block
-    table = {
-        FRAME: (row + lat_offset) * wide + column + lon_offset,
-        OWN: np.where(real, prow * wide + pcolumn, -1),
-        BACK: jnp.where(
-            jnp.logical_and(real, jnp.logical_not(jnp.logical_or(above, left))),
-            window_place(back_row, back_column),
-            -1,
-        ),
-        BACK_HALO: jnp.where(
-            real,
-            halo(
-                above,
-                left,
-                jnp.where(above, back_row + WIN_H, back_row),
-                jnp.where(left, back_column + WIN_W, back_column),
-            ),
-            -1,
-        ),
-        COT: np.where(real, prow * block + pcolumn, -1),
-        UNPATCH: (2 * (row % 2) + column % 2) * padded + (row // 2) * (block // 2) + column // 2,
-        GRAD: jnp.where(
-            jnp.logical_or(below, right), -1, window_place(grad_row, grad_column)
-        ),
-        GRAD_HALO: halo(
-            below,
-            right,
-            jnp.where(below, grad_row - rows, grad_row),
-            jnp.where(right, grad_column - block, grad_column),
-        ),
-        BY_ROW: np.where(shown, (spot // WIN_W) * WIN + side * WIN_W + spot % WIN_W, -1),
-        BY_ROW_PATCH: np.where(
-            shown, (spot % 2) * padded + side * (block // 2) + spot // 2, -1
-        ),
-        SHIFT: jnp.where(inside, (lon + lon_offset) % (n_mp * block), -1),
-        STAY: np.where(inside, lon, -1),
+    source = {
+        FRAME: (row, column, True, wide),
+        OWN: (prow, pcolumn, real, wide),
+        BACK: (prow, pcolumn, real, 0),
+        BACK_HALO: (prow, pcolumn, real, 0),
+        COT: (prow, pcolumn, real, block),
+        UNPATCH: (0, unpatch, True, 0),
+        GRAD: (row, column, True, 0),
+        GRAD_HALO: (row, column, True, 0),
+        BY_ROW: (0, by_row, shown, 0),
+        BY_ROW_PATCH: (0, by_row_patch, shown, 0),
+        SHIFT: (0, lon, inside, 0),
+        STAY: (0, lon, inside, 0),
     }
-    columns_list = [
-        jnp.pad(jnp.asarray(table[key], jnp.int32), (0, size - table[key].shape[0]))
-        for key in range(len(table))
-    ]
-    return jnp.stack(columns_list, axis=1)
+    shape = (size, len(source))
+    row_at, column_at, pitch = (np.zeros(shape, np.int32) for _ in range(3))
+    valid = np.zeros(shape, bool)
+    for key, (row_part, column_part, part, step) in source.items():
+        count = column_part.shape[0]
+        row_at[:count, key], column_at[:count, key], pitch[:, key] = row_part, column_part, step
+        valid[:count, key] = part
+    kind = np.arange(len(source))[None]
+    back = np.isin(kind, (BACK, BACK_HALO))
+    grad = np.isin(kind, (GRAD, GRAD_HALO))
+    row_sign = np.where(back, -1, np.where(grad | (kind == FRAME), 1, 0)).astype(np.int32)
+    column_sign = np.where(kind == SHIFT, 1, row_sign).astype(np.int32)
+    row_at = row_at + row_sign * lat_offset
+    column_at = column_at + column_sign * lon_offset
+    straight = row_at * pitch + column_at
+    full = n_mp * block
+    straight = jnp.where((kind == SHIFT) & (straight >= full), straight - full, straight)
+    down = jnp.where(back, row_at < 0, row_at >= rows)
+    right = jnp.where(back, column_at < 0, column_at >= block)
+    row_in = jnp.where(down, row_at + np.where(back, WIN_H, -rows).astype(np.int32), row_at)
+    column_in = jnp.where(
+        right, column_at + np.where(back, WIN_W, -block).astype(np.int32), column_at
+    )
+    band, slot = lax.div(row_in, jnp.int32(WIN_H)), lax.div(column_in, jnp.int32(WIN_W))
+    halo_slot = jnp.where(down, jnp.where(right, 0, 3 + slot), 1 + band)
+    outside = jnp.logical_or(down, right)
+    halo = np.isin(kind, (BACK_HALO, GRAD_HALO))
+    tile = jnp.where(halo, halo_slot, band * columns + slot)
+    windowed = tile * WIN + (row_in - band * WIN_H) * WIN_W + column_in - slot * WIN_W
+    result = jnp.where(back | grad, windowed, straight)
+    hidden = (back | grad) & jnp.where(halo, jnp.logical_not(outside), outside)
+    return jnp.where(valid & jnp.logical_not(hidden), result, -1).astype(jnp.int32)
 
 
 def norm_stats(values, count):

time: 284 us -> 268 us (0.944)
  local copies, waits for them, and re-layouts: 22.1 us -> 11.3 us
    unnamed x69 -> x39, local copies, waits for them, and re-layouts: 16.5 us -> 9.36 us
where the time goes in v4:
time: 268 us; the launch traced here: 267 us
  Pallas kernels  233 us (87%)
  other arithmetic  12.1 us (5%)
  local copies, waits for them, and re-layouts  11.3 us (4%)
  matrix products  8.38 us (3%)
    pallas_call x4, Pallas kernels, exchange(): pl.pallas_call(body, out_shape=[jax.ShapeDtypeStruct(shape, dtype) for sh...  121 us
    pallas_call x6, Pallas kernels, local_kernel(): pl.pallas_call(body, out_shape=[jax.ShapeDtypeStruct(shape, dtype) for sh...  41.6 us
    pallas_call x1, Pallas kernels, gradients_out(): pl.pallas_call(body, out_shape=[jax.ShapeDtypeStruct((share, kinds * grou...  38.5 us
    pallas_call x1, Pallas kernels, terms_back(): pl.pallas_call(body, out_shape=[jax.ShapeDtypeStruct((count, rows, width)...  31.5 us
    unnamed x39, local copies, waits for them, and re-layouts  9.36 us

profile of v4, /device:TPU:1, one launch (start us, length us, event | category | flops | bytes accessed | tf_op | source)
XLA Modules:
  0.0 267.1 jit_solution(6049067169759729817)
XLA Ops:
  2.7 0.7 select_maximum_fusion.refs_4_
  3.4 1.7 fusion.24.places_ref
  5.1 1.7 pad_maximum_fusion.5.refs_1_
  8.2 0.9 pad_maximum_fusion.4.refs_3_
  9.1 1.1 pad_maximum_fusion.2.refs_2_
  11.3 1.0 pad_maximum_fusion.3.refs_1_
  12.9 57.2 %shard_map.289 = (bf16[8,512,1024]{2,1,0:T(8,128)(2,1)S(1)}, bf16[4,512,512]{2,1,0:T(8,128)(2,1)S(1)}, bf16[8,288,128]{2,1,0:T(8,128)(2,1)S(1)}, bf16[8,144,128]{2,1,0:T(8,128)(2,1)S(1)}, f32[8,8,128]{2,1,0:T(8,128)S(1)}) custom-call(bf16[8,64,1024]{2,1,0:T(8,128)(2,1)S(1)} %pad_maximum_fusion.1.refs_0_.own_ref, bf16[4,64,512]{2,1,0:T(8,128)(2,1)S(1)} %copy-done.5, ...), custom_call_target="tpu_custom_call" | custom-call | tf_op jit(solution)/shard_map/pallas_call | solution.py:187
  70.1 3.2 %copy-done = bf16[8,512,1024]{2,1,0:T(8,128)(2,1)} copy-done((bf16[8,512,1024]{2,1,0:T(8,128)(2,1)}, bf16[8,512,1024]{2,1,0:T(8,128)(2,1)S(1)}, u32[]{:S(2)}) %copy-start) | copy-done | bytes 8388632
  73.3 0.8 copy-done.8
  74.1 0.7 copy-done.10
  75.0 1.5 copy-done.9
  76.6 1.0 copy-done.11
  77.5 8.2 %shard_map.290 = (bf16[432,512]{1,0:T(8,128)(2,1)S(1)}, bf16[432,512]{1,0:T(8,128)(2,1)S(1)}, bf16[432,512]{1,0:T(8,128)(2,1)S(1)}, bf16[4,112,512]{2,1,0:T(8,128)(2,1)S(1)}) custom-call(s32[1]{0:T(128)} %bitcast.2.cut_ref, bf16[8,288,128]{2,1,0:T(8,128)(2,1)S(1)} %copy-done.9, bf16[8,144,128]{2,1,0:T(8,128)(2,1)S(1)} %copy-done.11, ...), custom_call_target="tpu_custom_call" | custom-call | tf_op jit(solution)/shard_map/pallas_call | solution.py:398
  85.7 17.1 %shard_map.291 = (bf16[6,72,512]{2,1,0:T(8,128)(2,1)S(1)}, bf16[8,216,128]{2,1,0:T(8,128)(2,1)S(1)}) custom-call(bf16[2,3,72,512]{3,2,1,0:T(8,128)(2,1)S(1)} %bitcast.39, bf16[8,216,128]{2,1,0:T(8,128)(2,1)S(1)} %copy-done.3), custom_call_target="tpu_custom_call" | custom-call | tf_op jit(solution)/shard_map/pallas_call | solution.py:187
  102.9 6.0 %shard_map.292 = (bf16[112,2048]{1,0:T(8,128)(2,1)S(1)}, bf16[4,112,512]{2,1,0:T(8,128)(2,1)S(1)}, bf16[112,1024]{1,0:T(8,128)(2,1)S(1)}, f32[112,1024]{1,0:T(8,128)S(1)}, bf16[4,112,512]{2,1,0:T(8,128)(2,1)S(1)}) custom-call(s32[1]{0:T(128)} %bitcast.place_ref, bf16[4,112,512]{2,1,0:T(8,128)(2,1)S(1)} %get-tuple-element.42.fields_ref, ...), custom_call_target="tpu_custom_call" | custom-call | tf_op jit(solution)/shard_map/pallas_call | solution.py:398
  108.9 27.4 %shard_map.293 = (bf16[4,2,112,2048]{3,2,1,0:T(8,128)(2,1)S(1)}, bf16[1024,512]{1,0:T(8,128)(2,1)S(1)}, bf16[1024,512]{1,0:T(8,128)(2,1)S(1)}) custom-call(bf16[112,2048]{1,0:T(8,128)(2,1)S(1)} %get-tuple-element.47.refs_0_, bf16[1024,512]{1,0:T(8,128)(2,1)S(1)} %copy-done.7, bf16[1024,512]{1,0:T(8,128)(2,1)S(1)} %copy-done.6), custom_call_target="tpu_custom_call" | custom-call | tf_op jit(solution)/shard_map/pallas_call | solution.py:187
  136.4 1.1 fusion.13
  137.5 2.1 fusion.6
  139.6 1.3 convolution_convert_fusion.1
  140.9 1.4 fusion.18
  142.4 1.3 fusion.15
  143.6 1.2 convolution_convert_fusion
  144.8 2.2 pad_maximum_fusion.terms_ref
  147.0 31.5 %shard_map.294 = (bf16[4,112,2048]{2,1,0:T(8,128)(2,1)S(1)}, bf16[16,64,512]{2,1,0:T(8,128)(2,1)S(1)}, bf16[16,64,512]{2,1,0:T(8,128)(2,1)S(1)}) custom-call(bf16[4,2,112,2048]{3,2,1,0:T(8,128)(2,1)} %pad_maximum_fusion.terms_ref, bf16[16,64,512]{2,1,0:T(8,128)(2,1)S(1)} %bitcast.42, bf16[16,64,512]{2,1,0:T(8,128)(2,1)S(1)} %bitcast.41), custom_call_target="tpu_custom_call" | custom-call | tf_op jit(solution)/shard_map/pallas_call | solution.py:264
  178.5 7.3 %shard_map.295 = (bf16[8,288,128]{2,1,0:T(8,128)(2,1)S(1)}, bf16[432,512]{1,0:T(8,128)(2,1)S(1)}) custom-call(s32[1]{0:T(128)} %bitcast.place_ref, bf16[4,112,2048]{2,1,0:T(8,128)(2,1)S(1)} %get-tuple-element.51.parts_ref, bf16[112,1024]{1,0:T(8,128)(2,1)S(1)} %get-tuple-element.52.merged_ref, f32[112,1024]{1,0:T(8,128)S(1)} %get-tuple-element.53.grad_ref, ...), custom_call_target="tpu_custom_call" | custom-call | tf_op jit(solution)/shard_map/pallas_call | solution.py:398
  185.7 0.8 convert_reduce_fusion.1
  186.5 0.8 convert_reduce_fusion
  187.3 19.7 %shard_map.296 = (bf16[6,72,512]{2,1,0:T(8,128)(2,1)S(1)}, bf16[8,288,128]{2,1,0:T(8,128)(2,1)S(1)}) custom-call(bf16[2,3,72,512]{3,2,1,0:T(8,128)(2,1)S(1)} %bitcast.40, bf16[8,288,128]{2,1,0:T(8,128)(2,1)S(1)} %get-tuple-element.57.refs_1_), custom_call_target="tpu_custom_call" | custom-call | tf_op jit(solution)/shard_map/pallas_call | solution.py:187
  207.0 1.5 shard_map.297
  208.5 16.8 %shard_map.298 = (bf16[8,288,128]{2,1,0:T(8,128)(2,1)S(1)}, bf16[8,144,128]{2,1,0:T(8,128)(2,1)S(1)}, bf16[4,512,512]{2,1,0:T(8,128)(2,1)S(1)}) custom-call(s32[1]{0:T(128)} %bitcast.2.cut_ref, bf16[432,512]{1,0:T(8,128)(2,1)S(1)} %get-tuple-element.59.fields_ref, f32[1,512]{1,0:T(1,128)S(1)} %reshape_squeeze.3.gain_ref, bf16[4,512,512]{2,1,0:T(8,128)(2,1)} %copy-done.1, ...), custom_call_target="tpu_custom_call" | custom-call | tf_op jit(solution)/shard_map/pallas_call | solution.py:398
  225.3 38.5 %shard_map.299 = (f32[32,256]{1,0:T(8,128)S(1)}, bf16[8,288,128]{2,1,0:T(8,128)(2,1)S(1)}, bf16[8,144,128]{2,1,0:T(8,128)(2,1)S(1)}) custom-call(bf16[4,512,512]{2,1,0:T(8,128)(2,1)S(1)} %get-tuple-element.62.weight_ref, bf16[8,288,128]{2,1,0:T(8,128)(2,1)S(1)} %get-tuple-element.63.slab_ref, bf16[8,144,128]{2,1,0:T(8,128)(2,1)S(1)} %get-tuple-element.64.edge_ref), custom_call_target="tpu_custom_call" | custom-call | tf_op jit(solution)/shard_map/pallas_call | solution.py:371
  264.4 2.0 shard_map.300
  (55 shorter events, 5.2 us)
Async XLA Ops:
  0.6 6.2 %copy-start.13 = (bf16[12,288,64]{1,2,0:T(8,128)(2,1)S(1)}, bf16[12,288,64]{1,2,0:T(8,128)(2,1)}, u32[]{:S(2)}) copy-start(bf16[12,288,64]{1,2,0:T(8,128)(2,1)} %param.26) | copy-start | bytes 1327108
  9.1 1.2 copy-start.14
  11.2 1.2 copy-start.15
  11.2 1.2 copy-start.16
  11.3 1.4 copy-start.2
  11.3 1.5 copy-start.4
  11.3 1.6 copy-start.5
  70.1 3.3 %copy-start = (bf16[8,512,1024]{2,1,0:T(8,128)(2,1)}, bf16[8,512,1024]{2,1,0:T(8,128)(2,1)S(1)}, u32[]{:S(2)}) copy-start(bf16[8,512,1024]{2,1,0:T(8,128)(2,1)S(1)} %get-tuple-element.46.got_ref) | copy-start | bytes 25165828
  73.3 0.8 copy-start.8
  74.1 0.7 copy-start.10
  74.8 28.0 %copy-start.1 = (bf16[4,512,512]{2,1,0:T(8,128)(2,1)}, bf16[4,512,512]{2,1,0:T(8,128)(2,1)S(1)}, u32[]{:S(2)}) copy-start(bf16[4,512,512]{2,1,0:T(8,128)(2,1)S(1)} %get-tuple-element.41.weights_ref) | copy-start | bytes 6291460
  75.0 1.5 copy-start.9
  76.6 1.0 copy-start.11
  77.5 8.2 %copy-start.3 = (bf16[8,216,128]{2,1,0:T(8,128)(2,1)S(1)}, bf16[8,216,128]{2,1,0:T(8,128)(2,1)}, u32[]{:S(2)}) copy-start(bf16[8,216,128]{2,1,0:T(8,128)(2,1)} %pad_maximum_fusion.3.refs_1_) | copy-start | bytes 1327108
  77.5 25.4 %copy-start.12 = (f32[1024]{0:T(1024)S(1)}, f32[1024]{0:T(1024)}, u32[]{:S(2)}) copy-start(f32[1024]{0:T(1024)} %param.32) | copy-start | bytes 12292
  102.9 6.0 %copy-start.6 = (bf16[1024,512]{1,0:T(8,128)(2,1)S(1)}, bf16[1024,512]{1,0:T(8,128)(2,1)}, u32[]{:S(2)}) copy-start(bf16[1024,512]{1,0:T(8,128)(2,1)} %refs_2_.1) | copy-start | bytes 3145732
  102.9 6.0 %copy-start.7 = (bf16[1024,512]{1,0:T(8,128)(2,1)S(1)}, bf16[1024,512]{1,0:T(8,128)(2,1)}, u32[]{:S(2)}) copy-start(bf16[1024,512]{1,0:T(8,128)(2,1)} %refs_1_.1) | copy-start | bytes 3145732

commit v5 on v4

--- a/solution.py
+++ b/solution.py
@@ -204,12 +204,13 @@
 X_STEPS = ((4, 2), (2, 1), (-2, 3))
 
 
-def terms_back(collective, terms, up_grads, down_grads):
+def terms_back(collective, terms, backs, up_grads, down_grads):
     count, _, rows, width = terms.shape
     n_lat = lax.axis_size("lat")
+    both = range(2)
 
     def body(
-        terms_ref, up_ref, down_ref, parts_ref, up_got, down_got,
+        terms_ref, backs_ref, up_ref, down_ref, parts_ref, up_got, down_got,
         other, own, total, send, receive, fetch, large_send, large_receive,
     ):
         here = positions()
@@ -223,35 +224,40 @@
         order = [lax.rem(x + step, count) for _, step in X_STEPS] + [x]
         swaps, loads = [], []
         for index, spot in enumerate(order):
-            swap = remote(
-                terms_ref.at[spot, 1 - core],
-                other.at[index],
-                send.at[index],
-                receive.at[index],
-                sibling,
-            )
-            load = pltpu.make_async_copy(terms_ref.at[spot, core], own.at[index], fetch.at[index])
-            swap.start()
-            load.start()
-            swaps.append(swap)
-            loads.append(load)
+            for which, source in enumerate((terms_ref, backs_ref)):
+                swap = remote(
+                    source.at[spot, 1 - core],
+                    other.at[which, index],
+                    send.at[2 * index + which],
+                    receive.at[2 * index + which],
+                    sibling,
+                )
+                load = pltpu.make_async_copy(
+                    source.at[spot, core], own.at[which, index], fetch.at[2 * index + which]
+                )
+                swap.start()
+                load.start()
+                swaps.append(swap)
+                loads.append(load)
         for start, _ in scatters:
             start()
         sends = []
         for index, spot in enumerate(order):
-            loads[index].wait()
-            swaps[index].wait_recv()
-            total[index] = (own[index].astype(F32) + other[index].astype(F32)).astype(BF16)
+            for which in both:
+                loads[2 * index + which].wait()
+                swaps[2 * index + which].wait_recv()
+                summed = own[which, index].astype(F32) + other[which, index].astype(F32)
+                total[index, :, width * which : width * (which + 1)] = summed.astype(BF16)
             if index < len(X_STEPS):
                 copy = remote(
                     total.at[index],
                     parts_ref.at[x],
-                    send.at[count + index],
-                    receive.at[count + index],
+                    send.at[2 * count + index],
+                    receive.at[2 * count + index],
                     reached(here, 0, X_STEPS[index][0]),
                 )
             else:
-                copy = pltpu.make_async_copy(total.at[index], parts_ref.at[x], fetch.at[count])
+                copy = pltpu.make_async_copy(total.at[index], parts_ref.at[x], fetch.at[2 * count])
             copy.start()
             sends.append(copy)
         for swap in swaps:
@@ -264,39 +270,39 @@
     return pl.pallas_call(
         body,
         out_shape=[
-            jax.ShapeDtypeStruct((count, rows, width), BF16),
+            jax.ShapeDtypeStruct((count, rows, 2 * width), BF16),
             jax.ShapeDtypeStruct(up_grads.shape, BF16),
             jax.ShapeDtypeStruct(down_grads.shape, BF16),
         ],
-        in_specs=[pl.BlockSpec(memory_space=pl.ANY)] * 3,
+        in_specs=[pl.BlockSpec(memory_space=pl.ANY)] * 4,
         out_specs=[
             pl.BlockSpec(memory_space=pltpu.VMEM),
             pl.BlockSpec(memory_space=pl.ANY),
             pl.BlockSpec(memory_space=pl.ANY),
         ],
         scratch_shapes=[
-            pltpu.VMEM((count, rows, width), BF16),
-            pltpu.VMEM((count, rows, width), BF16),
-            pltpu.VMEM((count, rows, width), BF16),
-            pltpu.SemaphoreType.DMA((2 * count,)),
-            pltpu.SemaphoreType.DMA((2 * count,)),
-            pltpu.SemaphoreType.DMA((count + 1,)),
+            pltpu.VMEM((2, count, rows, width), BF16),
+            pltpu.VMEM((2, count, rows, width), BF16),
+            pltpu.VMEM((count, rows, 2 * width), BF16),
+            pltpu.SemaphoreType.DMA((3 * count,)),
+            pltpu.SemaphoreType.DMA((3 * count,)),
+            pltpu.SemaphoreType.DMA((2 * count + 1,)),
             pltpu.SemaphoreType.DMA((2, n_lat)),
             pltpu.SemaphoreType.DMA((2, n_lat)),
         ],
         compiler_params=pltpu.CompilerParams(
             collective_id=collective, has_side_effects=True, vmem_limit_bytes=48 * 1024 * 1024
         ),
-    )(terms, up_grads, down_grads)
-
-
-def gradients_out(collective, weight_grads, slabs, edges):
+    )(terms, backs, up_grads, down_grads)
+
+
+def gradients_out(collective, weight_grads, slabs, edges, decoded_slabs):
     n_lat, n_mp = lax.axis_size("lat"), lax.axis_size("mp")
     kinds, width, _ = weight_grads.shape
     pair, group, share = kinds // 2, width // n_mp, width // n_lat
 
     def body(
-        weight_ref, slab_ref, edge_ref, out_ref, got_ref, edge_got,
+        weight_ref, slab_ref, edge_ref, decoded_ref, out_ref, got_ref, edge_got, decoded_got,
         other, total, parts, turned, landed, send, receive,
     ):
         here = positions()
@@ -321,8 +327,13 @@
             return copy
 
         swap = sent(weight_ref.at[pl.ds(pair * (1 - core), pair)], other, sibling)
+        for step in range(1, n_mp):
+            target = reached(here, 0, step)
+            sent(decoded_ref.at[target["mp"]], decoded_got.at[mp], target)
         own_slab = pltpu.make_async_copy(slab_ref.at[mp], got_ref.at[mp], send.at[60])
         own_slab.start()
+        own_decoded = pltpu.make_async_copy(decoded_ref.at[mp], decoded_got.at[mp], send.at[61])
+        own_decoded.start()
 
         swap.wait_recv()
         total[...] = (
@@ -365,6 +376,7 @@
             if not any(copy is other_copy for other_copy in done):
                 copy.wait_recv()
         own_slab.wait()
+        own_decoded.wait()
 
     any_space = pl.BlockSpec(memory_space=pl.ANY)
     vmem = pl.BlockSpec(memory_space=pltpu.VMEM)
@@ -374,9 +386,10 @@
             jax.ShapeDtypeStruct((share, kinds * group), F32),
             jax.ShapeDtypeStruct(slabs.shape, BF16),
             jax.ShapeDtypeStruct(edges.shape, BF16),
-        ],
-        in_specs=[vmem, any_space, any_space],
-        out_specs=[vmem, vmem, vmem],
+            jax.ShapeDtypeStruct(decoded_slabs.shape, BF16),
+        ],
+        in_specs=[vmem, any_space, any_space, any_space],
+        out_specs=[vmem, vmem, vmem, vmem],
         scratch_shapes=[
             pltpu.VMEM((pair, width, width), BF16),
             pltpu.VMEM((pair, width, width), BF16),
@@ -389,10 +402,10 @@
         compiler_params=pltpu.CompilerParams(
             collective_id=collective, has_side_effects=True, vmem_limit_bytes=48 * 1024 * 1024
         ),
-    )(weight_grads, slabs, edges)
-
-
-def local_kernel(body, operands, outputs, scratch=(), scalars=0, outside=0):
+    )(weight_grads, slabs, edges, decoded_slabs)
+
+
+def local_kernel(body, operands, outputs, scratch=(), scalars=0, outside=0, grant=48):
     spaces = [pltpu.SMEM] * scalars + [pltpu.VMEM] * (len(operands) - scalars - outside)
     spaces += [pl.ANY] * outside
     return pl.pallas_call(
@@ -401,7 +414,7 @@
         in_specs=[pl.BlockSpec(memory_space=space) for space in spaces],
         out_specs=[pl.BlockSpec(memory_space=pltpu.VMEM)] * len(outputs),
         scratch_shapes=list(scratch),
-        compiler_params=pltpu.CompilerParams(vmem_limit_bytes=48 * 1024 * 1024),
+        compiler_params=pltpu.CompilerParams(vmem_limit_bytes=grant * 1024 * 1024),
     )(*operands)
 
 
@@ -963,6 +976,7 @@
         section_scratch + [pltpu.VMEM((tokens, width), F32)],
         scalars=1,
         outside=2,
+        grant=56,
     )
 
     def chip_spot(step):
@@ -1001,17 +1015,17 @@
     grad_act = jnp.dot(bottom_grad, down_shard, preferred_element_type=F32)
     gelu_back = jax.vjp(jax.nn.gelu, hidden_up)[1]
     grad_pre = gelu_back(grad_act)[0].astype(BF16)
-    terms = jnp.concatenate(
-        [
-            jnp.einsum("af,ef->ae", activated, down_shard, preferred_element_type=F32),
-            jnp.einsum("af,ef->ae", grad_pre, up_shard, preferred_element_type=F32),
-        ],
-        axis=1,
-    ).astype(BF16)
+    terms, backs = (
+        jnp.einsum("af,ef->ae", part, weight, preferred_element_type=F32)
+        .astype(BF16)
+        .reshape(n_x, 2, padded, width_two)
+        for part, weight in ((activated, down_shard), (grad_pre, up_shard))
+    )
     large = (n_lat, width_two // n_lat, span)
     parts, up_got, down_got = terms_back(
         4,
-        terms.reshape(n_x, 2, padded, 2 * width_two),
+        terms,
+        backs,
         jnp.einsum("ae,af->ef", mlp_in, grad_pre, preferred_element_type=F32)
         .astype(BF16)
         .reshape(large),
@@ -1039,17 +1053,17 @@
         section_scratch,
         scalars=1,
         outside=2,
-    )
-    halo, decoded_got = exchange(
+        grant=56,
+    )
+    (halo,) = exchange(
         5,
-        [grad_windows.reshape(window_shape), decoded_slab],
-        [(around, BF16), (decoded_slab.shape, BF16)],
+        [grad_windows.reshape(window_shape)],
+        [(around, BF16)],
         [
             (0, (0, 0), 0, (0,), -1, -1),
             (0, (slice(0, bands), 0), 0, (slice(1, 1 + bands),), 0, -1),
             (0, (0,), 0, (slice(1 + bands, 1 + bands + columns),), -1, 0),
-        ]
-        + [(1, "mp", 1, "mp", 0, step) for step in others],
+        ],
     )
     grad_up = jnp.sum(up_got.astype(F32), axis=0)
     grad_down = jnp.sum(down_got.astype(F32), axis=0)
@@ -1077,7 +1091,9 @@
         ],
         scalars=1,
     )
-    weight_total, grad_got, edge_got = gradients_out(6, weight_grads, grad_slab, grad_edge)
+    weight_total, grad_got, edge_got, decoded_got = gradients_out(
+        6, weight_grads, grad_slab, grad_edge, decoded_slab
+    )
     grad_qkv = weight_total[:, : 3 * group].reshape(width // n_lat, 3, group)
     grad_proj = weight_total[:, 3 * group :]
     (decoded,) = local_kernel(

time: 268 us -> 275 us (1.026)
  local copies, waits for them, and re-layouts: 11.3 us -> 16.2 us
    pallas_call x6, Pallas kernels: 41.6 us -> 48.4 us  [local_kernel(): pl.pallas_call(body, out_shape=[jax.ShapeDtypeStruct(shape, dtype) for sh...]
    pallas_call x4, Pallas kernels: 121 us -> 116 us  [exchange(): pl.pallas_call(body, out_shape=[jax.ShapeDtypeStruct(shape, dtype) for sh...]
    unnamed x39 -> x59, local copies, waits for them, and re-layouts: 9.36 us -> 13.5 us
where the time goes in v5:
time: 275 us; the launch traced here: 274 us
  Pallas kernels  234 us (85%)
  local copies, waits for them, and re-layouts  16.2 us (6%)
  matrix products  10.9 us (4%)
  other arithmetic  9.99 us (4%)
    pallas_call x4, Pallas kernels, exchange(): pl.pallas_call(body, out_shape=[jax.ShapeDtypeStruct(shape, dtype) for sh...  116 us
    pallas_call x6, Pallas kernels, local_kernel(): pl.pallas_call(body, out_shape=[jax.ShapeDtypeStruct(shape, dtype) for sh...  48.4 us
    pallas_call x1, Pallas kernels, gradients_out(): pl.pallas_call(body, out_shape=[jax.ShapeDtypeStruct((share, kinds * grou...  38.4 us
    pallas_call x1, Pallas kernels, terms_back(): pl.pallas_call(body, out_shape=[jax.ShapeDtypeStruct((count, rows, 2 * wi...  31.8 us
    unnamed x59, local copies, waits for them, and re-layouts  13.5 us

profile of v5, /device:TPU:1, one launch (start us, length us, event | category | flops | bytes accessed | tf_op | source)
XLA Modules:
  0.0 273.9 jit_solution(2029842870340177164)
XLA Ops:
  3.4 1.7 fusion.24.places_ref
  5.1 1.8 pad_maximum_fusion.4.refs_1_
  8.2 0.9 pad_maximum_fusion.3.refs_3_
  9.2 1.1 pad_maximum_fusion.1.refs_2_
  11.4 1.0 pad_maximum_fusion.2.refs_1_
  13.0 57.1 %shard_map.289 = (bf16[8,512,1024]{2,1,0:T(8,128)(2,1)S(1)}, bf16[4,512,512]{2,1,0:T(8,128)(2,1)S(1)}, bf16[8,288,128]{2,1,0:T(8,128)(2,1)S(1)}, bf16[8,144,128]{2,1,0:T(8,128)(2,1)S(1)}, f32[8,8,128]{2,1,0:T(8,128)S(1)}) custom-call(bf16[8,64,1024]{2,1,0:T(8,128)(2,1)S(1)} %pad_maximum_fusion.refs_0_.own_ref, bf16[4,64,512]{2,1,0:T(8,128)(2,1)S(1)} %copy-done.11, ...), custom_call_target="tpu_custom_call" | custom-call | tf_op jit(solution)/shard_map/pallas_call | solution.py:187
  70.1 3.3 %copy-done = bf16[8,512,1024]{2,1,0:T(8,128)(2,1)} copy-done((bf16[8,512,1024]{2,1,0:T(8,128)(2,1)}, bf16[8,512,1024]{2,1,0:T(8,128)(2,1)S(1)}, u32[]{:S(2)}) %copy-start) | copy-done | bytes 8388632
  73.3 0.8 copy-done.15
  75.0 0.9 reshape.79.gain_ref
  75.9 1.1 copy-done.16
  76.9 1.0 copy-done.22
  77.9 8.2 %shard_map.290 = (bf16[432,512]{1,0:T(8,128)(2,1)S(1)}, bf16[432,512]{1,0:T(8,128)(2,1)S(1)}, bf16[432,512]{1,0:T(8,128)(2,1)S(1)}, bf16[4,112,512]{2,1,0:T(8,128)(2,1)S(1)}) custom-call(s32[1]{0:T(128)} %bitcast.1.cut_ref, bf16[8,288,128]{2,1,0:T(8,128)(2,1)S(1)} %copy-done.16, bf16[8,144,128]{2,1,0:T(8,128)(2,1)S(1)} %copy-done.22, ...), custom_call_target="tpu_custom_call" | custom-call | tf_op jit(solution)/shard_map/pallas_call | solution.py:411
  86.9 17.0 %shard_map.291 = (bf16[6,72,512]{2,1,0:T(8,128)(2,1)S(1)}, bf16[8,216,128]{2,1,0:T(8,128)(2,1)S(1)}) custom-call(bf16[2,3,72,512]{3,2,1,0:T(8,128)(2,1)S(1)} %bitcast.40, bf16[8,216,128]{2,1,0:T(8,128)(2,1)S(1)} %copy-done.7), custom_call_target="tpu_custom_call" | custom-call | tf_op jit(solution)/shard_map/pallas_call | solution.py:187
  105.5 8.7 %shard_map.292 = (bf16[112,2048]{1,0:T(8,128)(2,1)}, bf16[4,112,512]{2,1,0:T(8,128)(2,1)}, bf16[112,1024]{1,0:T(8,128)(2,1)}, f32[112,1024]{1,0:T(8,128)}, bf16[4,112,512]{2,1,0:T(8,128)(2,1)}) custom-call(s32[1]{0:T(128)} %bitcast.13.place_ref, bf16[4,112,512]{2,1,0:T(8,128)(2,1)} %copy-done.18, bf16[432,512]{1,0:T(8,128)(2,1)} %copy-done.9, ...), custom_call_target="tpu_custom_call" | custom-call | tf_op jit(solution)/shard_map/pallas_call | solution.py:411
  114.2 1.0 copy-done.17
  115.2 27.3 %shard_map.293 = (bf16[4,2,112,2048]{3,2,1,0:T(8,128)(2,1)S(1)}, bf16[1024,512]{1,0:T(8,128)(2,1)S(1)}, bf16[1024,512]{1,0:T(8,128)(2,1)S(1)}) custom-call(bf16[112,2048]{1,0:T(8,128)(2,1)S(1)} %copy-done.17, bf16[1024,512]{1,0:T(8,128)(2,1)S(1)} %copy-done.13, bf16[1024,512]{1,0:T(8,128)(2,1)S(1)} %copy-done.12), custom_call_target="tpu_custom_call" | custom-call | tf_op jit(solution)/shard_map/pallas_call | solution.py:187
  142.6 1.1 fusion.13
  143.7 2.1 fusion.6
  145.8 2.6 convolution_convert_fusion.1
  148.3 1.4 fusion.18
  149.7 1.3 fusion.15
  151.0 2.4 convolution_convert_fusion
  153.5 31.8 %shard_map.294 = (bf16[4,112,2048]{2,1,0:T(8,128)(2,1)S(1)}, bf16[16,64,512]{2,1,0:T(8,128)(2,1)S(1)}, bf16[16,64,512]{2,1,0:T(8,128)(2,1)S(1)}) custom-call(bf16[4,2,112,1024]{3,2,1,0:T(8,128)(2,1)} %bitcast.57, bf16[4,2,112,1024]{3,2,1,0:T(8,128)(2,1)} %bitcast.58, bf16[16,64,512]{2,1,0:T(8,128)(2,1)S(1)} %bitcast.43, bf16[16,64,512]{2,1,0:T(8,128)(2,1)S(1)} %bitcast.42), custom_call_target="tpu_custom_call" | custom-call | tf_op jit(solution)/shard_map/pallas_call | solution.py:270
  185.3 1.2 copy-done.6
  186.5 11.2 %shard_map.295 = (bf16[8,288,128]{2,1,0:T(8,128)(2,1)}, bf16[432,512]{1,0:T(8,128)(2,1)}) custom-call(s32[1]{0:T(128)} %bitcast.13.place_ref, bf16[4,112,2048]{2,1,0:T(8,128)(2,1)} %copy-done.6, bf16[112,1024]{1,0:T(8,128)(2,1)} %get-tuple-element.53.merged_ref, f32[112,1024]{1,0:T(8,128)} %get-tuple-element.54.grad_ref, ...), custom_call_target="tpu_custom_call" | custom-call | tf_op jit(solution)/shard_map/pallas_call | solution.py:411
  197.8 0.8 convert_reduce_fusion.1
  198.6 0.8 convert_reduce_fusion
  199.4 14.5 %shard_map.296 = bf16[6,72,512]{2,1,0:T(8,128)(2,1)S(1)} custom-call(bf16[2,3,72,512]{3,2,1,0:T(8,128)(2,1)S(1)} %bitcast.39), custom_call_target="tpu_custom_call" | custom-call | tf_op jit(solution)/shard_map/pallas_call | solution.py:187
  213.9 16.8 %shard_map.297 = (bf16[8,288,128]{2,1,0:T(8,128)(2,1)S(1)}, bf16[8,144,128]{2,1,0:T(8,128)(2,1)S(1)}, bf16[4,512,512]{2,1,0:T(8,128)(2,1)S(1)}) custom-call(s32[1]{0:T(128)} %bitcast.1.cut_ref, bf16[432,512]{1,0:T(8,128)(2,1)S(1)} %get-tuple-element.41.fields_ref, f32[1,512]{1,0:T(1,128)S(1)} %reshape_squeeze.3.gain_ref, bf16[4,512,512]{2,1,0:T(8,128)(2,1)} %copy-done.4, ...), custom_call_target="tpu_custom_call" | custom-call | tf_op jit(solution)/shard_map/pallas_call | solution.py:411
  230.7 38.4 %shard_map.298 = (f32[32,256]{1,0:T(8,128)S(1)}, bf16[8,288,128]{2,1,0:T(8,128)(2,1)S(1)}, bf16[8,144,128]{2,1,0:T(8,128)(2,1)S(1)}, bf16[8,288,128]{2,1,0:T(8,128)(2,1)S(1)}) custom-call(bf16[4,512,512]{2,1,0:T(8,128)(2,1)S(1)} %get-tuple-element.58.weight_ref, bf16[8,288,128]{2,1,0:T(8,128)(2,1)S(1)} %get-tuple-element.59.slab_ref, ...), custom_call_target="tpu_custom_call" | custom-call | tf_op jit(solution)/shard_map/pallas_call | solution.py:383
  269.1 1.5 shard_map.299
  271.3 2.0 shard_map.300
  (74 shorter events, 8.8 us)
Async XLA Ops:
  0.6 6.3 %copy-start.23 = (bf16[12,288,64]{1,2,0:T(8,128)(2,1)S(1)}, bf16[12,288,64]{1,2,0:T(8,128)(2,1)}, u32[]{:S(2)}) copy-start(bf16[12,288,64]{1,2,0:T(8,128)(2,1)} %param.26) | copy-start | bytes 1327108
  5.1 70.8 %copy-start.2 = (s32[448,12]{1,0:T(8,128)}, s32[448,12]{1,0:T(8,128)S(1)}, u32[]{:S(2)}) copy-start(s32[448,12]{1,0:T(8,128)S(1)} %fusion.24.places_ref) | copy-start | bytes 64516
  9.1 1.2 copy-start.24
  11.2 1.2 copy-start.25
  11.2 1.2 copy-start.26
  11.4 1.4 copy-start.5
  11.4 1.5 copy-start.10
  11.4 1.6 copy-start.11
  13.0 73.1 %copy-start.1 = (bf16[8,64,1024]{2,1,0:T(8,128)(2,1)}, bf16[8,64,1024]{2,1,0:T(8,128)(2,1)S(1)}, u32[]{:S(2)}) copy-start(bf16[8,64,1024]{2,1,0:T(8,128)(2,1)S(1)} %pad_maximum_fusion.refs_0_.own_ref) | copy-start | bytes 3145732
  70.1 3.3 %copy-start = (bf16[8,512,1024]{2,1,0:T(8,128)(2,1)}, bf16[8,512,1024]{2,1,0:T(8,128)(2,1)S(1)}, u32[]{:S(2)}) copy-start(bf16[8,512,1024]{2,1,0:T(8,128)(2,1)S(1)} %get-tuple-element.47.got_ref) | copy-start | bytes 25165828
  73.3 0.8 copy-start.15
  74.1 0.7 copy-start.21
  74.9 29.0 %copy-start.4 = (bf16[4,512,512]{2,1,0:T(8,128)(2,1)}, bf16[4,512,512]{2,1,0:T(8,128)(2,1)S(1)}, u32[]{:S(2)}) copy-start(bf16[4,512,512]{2,1,0:T(8,128)(2,1)S(1)} %get-tuple-element.40.weights_ref) | copy-start | bytes 6291460
  75.9 1.1 copy-start.16
  76.9 1.0 copy-start.22
  77.9 9.0 %copy-start.7 = (bf16[8,216,128]{2,1,0:T(8,128)(2,1)S(1)}, bf16[8,216,128]{2,1,0:T(8,128)(2,1)}, u32[]{:S(2)}) copy-start(bf16[8,216,128]{2,1,0:T(8,128)(2,1)} %pad_maximum_fusion.2.refs_1_) | copy-start | bytes 1327108
  86.1 0.8 copy-start.18
  86.9 18.6 %copy-start.9 = (bf16[432,512]{1,0:T(8,128)(2,1)}, bf16[432,512]{1,0:T(8,128)(2,1)S(1)}, u32[]{:S(2)}) copy-start(bf16[432,512]{1,0:T(8,128)(2,1)S(1)} %get-tuple-element.44.attention_ref) | copy-start | bytes 1327108
  103.9 0.8 copy-start.19
  104.7 0.8 copy-start.20
  105.5 8.7 %copy-start.12 = (bf16[1024,512]{1,0:T(8,128)(2,1)S(1)}, bf16[1024,512]{1,0:T(8,128)(2,1)}, u32[]{:S(2)}) copy-start(bf16[1024,512]{1,0:T(8,128)(2,1)} %refs_2_.1) | copy-start | bytes 3145732
  105.5 8.7 %copy-start.13 = (bf16[1024,512]{1,0:T(8,128)(2,1)S(1)}, bf16[1024,512]{1,0:T(8,128)(2,1)}, u32[]{:S(2)}) copy-start(bf16[1024,512]{1,0:T(8,128)(2,1)} %refs_1_.1) | copy-start | bytes 3145732
  114.2 1.0 copy-start.17
  185.3 1.2 copy-start.6
  197.7 1.6 copy-start.8
  197.8 16.1 %copy-start.3 = (s32[448,12]{1,0:T(8,128)S(1)}, s32[448,12]{1,0:T(8,128)}, u32[]{:S(2)}) copy-start(s32[448,12]{1,0:T(8,128)} %copy-done.2) | copy-start | bytes 64516
  213.9 16.9 %copy-start.14 = (bf16[8,288,128]{2,1,0:T(8,128)(2,1)S(1)}, bf16[8,288,128]{2,1,0:T(8,128)(2,1)}, u32[]{:S(2)}) copy-start(bf16[8,288,128]{2,1,0:T(8,128)(2,1)} %get-tuple-element.61.decoded_ref) | copy-start | bytes 1769476

commit v6 on v4

--- a/solution.py
+++ b/solution.py
@@ -116,7 +116,7 @@
     )
 
 
-def exchange(collective, inputs, outputs, moves, owned=()):
+def exchange(collective, inputs, outputs, moves, owned=(), outside=()):
     n_lat = lax.axis_size("lat")
     steps = []
     for move in moves:
@@ -188,7 +188,10 @@
         body,
         out_shape=[jax.ShapeDtypeStruct(shape, dtype) for shape, dtype in outputs],
         in_specs=[pl.BlockSpec(memory_space=pl.ANY)] * len(inputs),
-        out_specs=[pl.BlockSpec(memory_space=space_of(shape)) for shape, _ in outputs],
+        out_specs=[
+            pl.BlockSpec(memory_space=pl.ANY if index in outside else space_of(shape))
+            for index, (shape, _) in enumerate(outputs)
+        ],
         scratch_shapes=[
             pltpu.SemaphoreType.DMA((len(moves),)),
             pltpu.SemaphoreType.DMA((len(moves),)),
@@ -290,13 +293,13 @@
     )(terms, up_grads, down_grads)
 
 
-def gradients_out(collective, weight_grads, slabs, edges):
+def gradients_out(collective, weight_grads, slabs, edges, decoded_slabs):
     n_lat, n_mp = lax.axis_size("lat"), lax.axis_size("mp")
     kinds, width, _ = weight_grads.shape
     pair, group, share = kinds // 2, width // n_mp, width // n_lat
 
     def body(
-        weight_ref, slab_ref, edge_ref, out_ref, got_ref, edge_got,
+        weight_ref, slab_ref, edge_ref, decoded_ref, out_ref, got_ref, edge_got, decoded_got,
         other, total, parts, turned, landed, send, receive,
     ):
         here = positions()
@@ -321,8 +324,13 @@
             return copy
 
         swap = sent(weight_ref.at[pl.ds(pair * (1 - core), pair)], other, sibling)
+        for step in range(1, n_mp):
+            target = reached(here, 0, step)
+            sent(decoded_ref.at[target["mp"]], decoded_got.at[mp], target)
         own_slab = pltpu.make_async_copy(slab_ref.at[mp], got_ref.at[mp], send.at[60])
         own_slab.start()
+        own_decoded = pltpu.make_async_copy(decoded_ref.at[mp], decoded_got.at[mp], send.at[61])
+        own_decoded.start()
 
         swap.wait_recv()
         total[...] = (
@@ -365,6 +373,7 @@
             if not any(copy is other_copy for other_copy in done):
                 copy.wait_recv()
         own_slab.wait()
+        own_decoded.wait()
 
     any_space = pl.BlockSpec(memory_space=pl.ANY)
     vmem = pl.BlockSpec(memory_space=pltpu.VMEM)
@@ -374,9 +383,10 @@
             jax.ShapeDtypeStruct((share, kinds * group), F32),
             jax.ShapeDtypeStruct(slabs.shape, BF16),
             jax.ShapeDtypeStruct(edges.shape, BF16),
-        ],
-        in_specs=[vmem, any_space, any_space],
-        out_specs=[vmem, vmem, vmem],
+            jax.ShapeDtypeStruct(decoded_slabs.shape, BF16),
+        ],
+        in_specs=[vmem, any_space, any_space, any_space],
+        out_specs=[vmem, vmem, vmem, vmem],
         scratch_shapes=[
             pltpu.VMEM((pair, width, width), BF16),
             pltpu.VMEM((pair, width, width), BF16),
@@ -389,7 +399,7 @@
         compiler_params=pltpu.CompilerParams(
             collective_id=collective, has_side_effects=True, vmem_limit_bytes=48 * 1024 * 1024
         ),
-    )(weight_grads, slabs, edges)
+    )(weight_grads, slabs, edges, decoded_slabs)
 
 
 def local_kernel(body, operands, outputs, scratch=(), scalars=0, outside=0):
@@ -903,6 +913,7 @@
             ((n_mp,) + gains.shape, F32),
         ],
         moves + relays + last_relays,
+        outside=(2, 3),
     )
     has_shard = lax.rem(lax.axis_index("mp"), 2) == core
     first_all = gains_all[:, 0, :group].reshape(1, width)
@@ -1040,16 +1051,15 @@
         scalars=1,
         outside=2,
     )
-    halo, decoded_got = exchange(
+    (halo,) = exchange(
         5,
-        [grad_windows.reshape(window_shape), decoded_slab],
-        [(around, BF16), (decoded_slab.shape, BF16)],
+        [grad_windows.reshape(window_shape)],
+        [(around, BF16)],
         [
             (0, (0, 0), 0, (0,), -1, -1),
             (0, (slice(0, bands), 0), 0, (slice(1, 1 + bands),), 0, -1),
             (0, (0,), 0, (slice(1 + bands, 1 + bands + columns),), -1, 0),
-        ]
-        + [(1, "mp", 1, "mp", 0, step) for step in others],
+        ],
     )
     grad_up = jnp.sum(up_got.astype(F32), axis=0)
     grad_down = jnp.sum(down_got.astype(F32), axis=0)
@@ -1077,7 +1087,9 @@
         ],
         scalars=1,
     )
-    weight_total, grad_got, edge_got = gradients_out(6, weight_grads, grad_slab, grad_edge)
+    weight_total, grad_got, edge_got, decoded_got = gradients_out(
+        6, weight_grads, grad_slab, grad_edge, decoded_slab
+    )
     grad_qkv = weight_total[:, : 3 * group].reshape(width // n_lat, 3, group)
     grad_proj = weight_total[:, 3 * group :]
     (decoded,) = local_kernel(

time: 268 us -> 263 us (0.981)
  Pallas kernels: 233 us -> 228 us
    pallas_call x4, Pallas kernels: 121 us -> 116 us  [exchange(): pl.pallas_call(body, out_shape=[jax.ShapeDtypeStruct(shape, dtype) for sh...]
where the time goes in v6:
time: 263 us; the launch traced here: 262 us
  Pallas kernels  228 us (87%)
  other arithmetic  12.1 us (5%)
  local copies, waits for them, and re-layouts  11.3 us (4%)
  matrix products  8.4 us (3%)
    pallas_call x4, Pallas kernels, exchange(): pl.pallas_call(body, out_shape=[jax.ShapeDtypeStruct(shape, dtype) for sh...  116 us
    pallas_call x6, Pallas kernels, local_kernel(): pl.pallas_call(body, out_shape=[jax.ShapeDtypeStruct(shape, dtype) for sh...  41.7 us
    pallas_call x1, Pallas kernels, gradients_out(): pl.pallas_call(body, out_shape=[jax.ShapeDtypeStruct((share, kinds * grou...  38.6 us
    pallas_call x1, Pallas kernels, terms_back(): pl.pallas_call(body, out_shape=[jax.ShapeDtypeStruct((count, rows, width)...  31.5 us
    unnamed x39, local copies, waits for them, and re-layouts  9.36 us

profile of v6, /device:TPU:1, one launch (start us, length us, event | category | flops | bytes accessed | tf_op | source)
XLA Modules:
  0.0 262.1 jit_solution(13029547370223462294)
XLA Ops:
  2.7 0.7 select_maximum_fusion.refs_4_
  3.4 1.7 fusion.24.places_ref
  5.1 1.7 pad_maximum_fusion.5.refs_1_
  8.2 0.9 pad_maximum_fusion.4.refs_3_
  9.1 1.1 pad_maximum_fusion.2.refs_2_
  11.3 1.0 pad_maximum_fusion.3.refs_1_
  12.9 57.2 %shard_map.289 = (bf16[8,512,1024]{2,1,0:T(8,128)(2,1)S(1)}, bf16[4,512,512]{2,1,0:T(8,128)(2,1)S(1)}, bf16[8,288,128]{2,1,0:T(8,128)(2,1)S(1)}, bf16[8,144,128]{2,1,0:T(8,128)(2,1)S(1)}, f32[8,8,128]{2,1,0:T(8,128)S(1)}) custom-call(bf16[8,64,1024]{2,1,0:T(8,128)(2,1)S(1)} %pad_maximum_fusion.1.refs_0_.own_ref, bf16[4,64,512]{2,1,0:T(8,128)(2,1)S(1)} %copy-done.5, ...), custom_call_target="tpu_custom_call" | custom-call | tf_op jit(solution)/shard_map/pallas_call | solution.py:187
  70.1 3.2 %copy-done = bf16[8,512,1024]{2,1,0:T(8,128)(2,1)} copy-done((bf16[8,512,1024]{2,1,0:T(8,128)(2,1)}, bf16[8,512,1024]{2,1,0:T(8,128)(2,1)S(1)}, u32[]{:S(2)}) %copy-start) | copy-done | bytes 8388632
  73.3 0.8 copy-done.8
  74.1 0.7 copy-done.10
  75.0 1.5 copy-done.9
  76.5 1.0 copy-done.11
  77.5 8.2 %shard_map.290 = (bf16[432,512]{1,0:T(8,128)(2,1)S(1)}, bf16[432,512]{1,0:T(8,128)(2,1)S(1)}, bf16[432,512]{1,0:T(8,128)(2,1)S(1)}, bf16[4,112,512]{2,1,0:T(8,128)(2,1)S(1)}) custom-call(s32[1]{0:T(128)} %bitcast.1.cut_ref, bf16[8,288,128]{2,1,0:T(8,128)(2,1)S(1)} %copy-done.9, bf16[8,144,128]{2,1,0:T(8,128)(2,1)S(1)} %copy-done.11, ...), custom_call_target="tpu_custom_call" | custom-call | tf_op jit(solution)/shard_map/pallas_call | solution.py:408
  85.7 17.1 %shard_map.291 = (bf16[6,72,512]{2,1,0:T(8,128)(2,1)S(1)}, bf16[8,216,128]{2,1,0:T(8,128)(2,1)S(1)}) custom-call(bf16[2,3,72,512]{3,2,1,0:T(8,128)(2,1)S(1)} %bitcast.40, bf16[8,216,128]{2,1,0:T(8,128)(2,1)S(1)} %copy-done.3), custom_call_target="tpu_custom_call" | custom-call | tf_op jit(solution)/shard_map/pallas_call | solution.py:187
  102.9 6.0 %shard_map.292 = (bf16[112,2048]{1,0:T(8,128)(2,1)S(1)}, bf16[4,112,512]{2,1,0:T(8,128)(2,1)S(1)}, bf16[112,1024]{1,0:T(8,128)(2,1)S(1)}, f32[112,1024]{1,0:T(8,128)S(1)}, bf16[4,112,512]{2,1,0:T(8,128)(2,1)S(1)}) custom-call(s32[1]{0:T(128)} %bitcast.13.place_ref, bf16[4,112,512]{2,1,0:T(8,128)(2,1)S(1)} %get-tuple-element.43.fields_ref, ...), custom_call_target="tpu_custom_call" | custom-call | tf_op jit(solution)/shard_map/pallas_call | solution.py:408
  108.9 27.4 %shard_map.293 = (bf16[4,2,112,2048]{3,2,1,0:T(8,128)(2,1)S(1)}, bf16[1024,512]{1,0:T(8,128)(2,1)S(1)}, bf16[1024,512]{1,0:T(8,128)(2,1)S(1)}) custom-call(bf16[112,2048]{1,0:T(8,128)(2,1)S(1)} %get-tuple-element.48.refs_0_, bf16[1024,512]{1,0:T(8,128)(2,1)S(1)} %copy-done.7, bf16[1024,512]{1,0:T(8,128)(2,1)S(1)} %copy-done.6), custom_call_target="tpu_custom_call" | custom-call | tf_op jit(solution)/shard_map/pallas_call | solution.py:187
  136.4 1.1 fusion.13
  137.5 2.1 fusion.6
  139.6 1.3 convolution_convert_fusion.1
  140.9 1.4 fusion.18
  142.3 1.3 fusion.15
  143.6 1.2 convolution_convert_fusion
  144.8 2.2 pad_maximum_fusion.terms_ref
  147.0 31.5 %shard_map.294 = (bf16[4,112,2048]{2,1,0:T(8,128)(2,1)S(1)}, bf16[16,64,512]{2,1,0:T(8,128)(2,1)S(1)}, bf16[16,64,512]{2,1,0:T(8,128)(2,1)S(1)}) custom-call(bf16[4,2,112,2048]{3,2,1,0:T(8,128)(2,1)} %pad_maximum_fusion.terms_ref, bf16[16,64,512]{2,1,0:T(8,128)(2,1)S(1)} %bitcast.43, bf16[16,64,512]{2,1,0:T(8,128)(2,1)S(1)} %bitcast.42), custom_call_target="tpu_custom_call" | custom-call | tf_op jit(solution)/shard_map/pallas_call | solution.py:267
  178.5 7.3 %shard_map.295 = (bf16[8,288,128]{2,1,0:T(8,128)(2,1)S(1)}, bf16[432,512]{1,0:T(8,128)(2,1)S(1)}) custom-call(s32[1]{0:T(128)} %bitcast.13.place_ref, bf16[4,112,2048]{2,1,0:T(8,128)(2,1)S(1)} %get-tuple-element.52.parts_ref, bf16[112,1024]{1,0:T(8,128)(2,1)S(1)} %get-tuple-element.53.merged_ref, f32[112,1024]{1,0:T(8,128)S(1)} %get-tuple-element.54.grad_ref, ...), custom_call_target="tpu_custom_call" | custom-call | tf_op jit(solution)/shard_map/pallas_call | solution.py:408
  185.8 0.8 convert_reduce_fusion.1
  186.6 0.8 convert_reduce_fusion
  187.4 14.5 %shard_map.296 = bf16[6,72,512]{2,1,0:T(8,128)(2,1)S(1)} custom-call(bf16[2,3,72,512]{3,2,1,0:T(8,128)(2,1)S(1)} %bitcast.39), custom_call_target="tpu_custom_call" | custom-call | tf_op jit(solution)/shard_map/pallas_call | solution.py:187
  201.9 16.8 %shard_map.297 = (bf16[8,288,128]{2,1,0:T(8,128)(2,1)S(1)}, bf16[8,144,128]{2,1,0:T(8,128)(2,1)S(1)}, bf16[4,512,512]{2,1,0:T(8,128)(2,1)S(1)}) custom-call(s32[1]{0:T(128)} %bitcast.1.cut_ref, bf16[432,512]{1,0:T(8,128)(2,1)S(1)} %get-tuple-element.41.fields_ref, f32[1,512]{1,0:T(1,128)S(1)} %reshape_squeeze.3.gain_ref, bf16[4,512,512]{2,1,0:T(8,128)(2,1)} %copy-done.1, ...), custom_call_target="tpu_custom_call" | custom-call | tf_op jit(solution)/shard_map/pallas_call | solution.py:408
  218.7 38.6 %shard_map.298 = (f32[32,256]{1,0:T(8,128)S(1)}, bf16[8,288,128]{2,1,0:T(8,128)(2,1)S(1)}, bf16[8,144,128]{2,1,0:T(8,128)(2,1)S(1)}, bf16[8,288,128]{2,1,0:T(8,128)(2,1)S(1)}) custom-call(bf16[4,512,512]{2,1,0:T(8,128)(2,1)S(1)} %get-tuple-element.58.weight_ref, bf16[8,288,128]{2,1,0:T(8,128)(2,1)S(1)} %get-tuple-element.59.slab_ref, ...), custom_call_target="tpu_custom_call" | custom-call | tf_op jit(solution)/shard_map/pallas_call | solution.py:380
  257.3 1.5 shard_map.299
  259.4 2.0 shard_map.300
  (55 shorter events, 5.2 us)
Async XLA Ops:
  0.6 6.2 %copy-start.13 = (bf16[12,288,64]{1,2,0:T(8,128)(2,1)S(1)}, bf16[12,288,64]{1,2,0:T(8,128)(2,1)}, u32[]{:S(2)}) copy-start(bf16[12,288,64]{1,2,0:T(8,128)(2,1)} %param.26) | copy-start | bytes 1327108
  9.0 1.2 copy-start.14
  11.1 1.2 copy-start.15
  11.1 1.2 copy-start.16
  11.3 1.4 copy-start.2
  11.3 1.5 copy-start.4
  11.3 1.6 copy-start.5
  70.0 3.2 %copy-start = (bf16[8,512,1024]{2,1,0:T(8,128)(2,1)}, bf16[8,512,1024]{2,1,0:T(8,128)(2,1)S(1)}, u32[]{:S(2)}) copy-start(bf16[8,512,1024]{2,1,0:T(8,128)(2,1)S(1)} %get-tuple-element.47.got_ref) | copy-start | bytes 25165828
  73.3 0.8 copy-start.8
  74.1 0.7 copy-start.10
  74.8 28.0 %copy-start.1 = (bf16[4,512,512]{2,1,0:T(8,128)(2,1)}, bf16[4,512,512]{2,1,0:T(8,128)(2,1)S(1)}, u32[]{:S(2)}) copy-start(bf16[4,512,512]{2,1,0:T(8,128)(2,1)S(1)} %get-tuple-element.40.weights_ref) | copy-start | bytes 6291460
  75.0 1.5 copy-start.9
  76.5 1.0 copy-start.11
  77.5 8.2 %copy-start.3 = (bf16[8,216,128]{2,1,0:T(8,128)(2,1)S(1)}, bf16[8,216,128]{2,1,0:T(8,128)(2,1)}, u32[]{:S(2)}) copy-start(bf16[8,216,128]{2,1,0:T(8,128)(2,1)} %pad_maximum_fusion.3.refs_1_) | copy-start | bytes 1327108
  77.5 25.4 %copy-start.12 = (f32[1024]{0:T(1024)S(1)}, f32[1024]{0:T(1024)}, u32[]{:S(2)}) copy-start(f32[1024]{0:T(1024)} %param.32) | copy-start | bytes 12292
  102.9 6.0 %copy-start.6 = (bf16[1024,512]{1,0:T(8,128)(2,1)S(1)}, bf16[1024,512]{1,0:T(8,128)(2,1)}, u32[]{:S(2)}) copy-start(bf16[1024,512]{1,0:T(8,128)(2,1)} %refs_2_.1) | copy-start | bytes 3145732
  102.9 6.0 %copy-start.7 = (bf16[1024,512]{1,0:T(8,128)(2,1)S(1)}, bf16[1024,512]{1,0:T(8,128)(2,1)}, u32[]{:S(2)}) copy-start(bf16[1024,512]{1,0:T(8,128)(2,1)} %refs_1_.1) | copy-start | bytes 3145732
